TPU v7x, 128 devices: a whole 4x4x4 slice. The times are simulated.
128 devices in a mesh: dp: 16 (over z, y), vocab: 8 (over x, core).
Axes of the slice: x: 4, y: 4, z: 4, core: 2. Of those that a mesh axis runs over, the one named last changes fastest.
Arguments:
- token_ids: int32 [16384], P(('dp', 'vocab')), may hold values from 0 to 50303, as said below
- targets: int32 [16384], P(('dp', 'vocab')), may hold values from 0 to 50303, as said below
- lengths: int32 [16, 8, 3], P('dp'), may hold values from 1 to 80, 128 in all within a row
- embed_table: float32 [50304, 768], P(('dp', 'vocab')), may hold values from -0.3125 to 0.3125
- embed_moment: float32 [50304, 768], P(('dp', 'vocab')), may hold values from -9.536743e-06 to 9.536743e-06
- embed_average: float32 [50304, 768], P(('dp', 'vocab')), may hold values from -0.3125 to 0.3125
- blocks: float32 [2, 768, 9216], P(None, None, ('dp', 'vocab')), may hold values from -0.21875 to 0.21875
- block_moment: float32 [2, 768, 9216], P(None, None, ('dp', 'vocab')), may hold values from -9.536743e-06 to 9.536743e-06
- block_average: float32 [2, 768, 9216], P(None, None, ('dp', 'vocab')), may hold values from -0.21875 to 0.21875
- pos_table: float32 [80, 768], P(None, ('dp', 'vocab')), may hold values from -0.3125 to 0.3125
- pos_moment: float32 [80, 768], P(None, ('dp', 'vocab')), may hold values from -9.536743e-06 to 9.536743e-06
- pos_average: float32 [80, 768], P(None, ('dp', 'vocab')), may hold values from -0.3125 to 0.3125
- vectors: float32 [19968], P(('dp', 'vocab'))
- vector_moment: float32 [19968], P(('dp', 'vocab')), may hold values from -9.536743e-06 to 9.536743e-06
- vector_average: float32 [19968], P(('dp', 'vocab'))
Outputs:
- loss_sum: float32 [], replicated
- grad_norm: float32 [], replicated
- embed_moment_next: float32 [50304, 768], P(('dp', 'vocab'))
- embed_next: float32 [50304, 768], P(('dp', 'vocab'))
- embed_average_next: float32 [50304, 768], P(('dp', 'vocab'))
- embed_copy: bfloat16 [50304, 768], P(('dp', 'vocab'))
- block_moment_next: float32 [2, 768, 9216], P(None, None, ('dp', 'vocab'))
- blocks_next: float32 [2, 768, 9216], P(None, None, ('dp', 'vocab'))
- block_average_next: float32 [2, 768, 9216], P(None, None, ('dp', 'vocab'))
- block_copy: bfloat16 [2, 768, 9216], P(None, None, ('dp', 'vocab'))
- pos_moment_next: float32 [80, 768], P(None, ('dp', 'vocab'))
- pos_next: float32 [80, 768], P(None, ('dp', 'vocab'))
- pos_average_next: float32 [80, 768], P(None, ('dp', 'vocab'))
- pos_copy: bfloat16 [80, 768], P(None, ('dp', 'vocab'))
- vector_moment_next: float32 [19968], P(('dp', 'vocab'))
- vectors_next: float32 [19968], P(('dp', 'vocab'))
- vector_average_next: float32 [19968], P(('dp', 'vocab'))
- vector_copy: bfloat16 [19968], P(('dp', 'vocab'))
Inputs may be any that keep to these rules, and one draw needn't show every extreme that they name: `token_ids`: among one device's 128 ids, at most 2 lie in any one block of 393 consecutive rows. Likewise for one device's targets. Each device's 3 lengths sum to 128.
All inputs are finite; a program needn't handle non-finite values.
Results may differ from a plain program's by a relative error of at most 0.018.
Values may be sent and summed in bfloat16 or wider, within the bound.
A program may use at most 320 MiB of HBM per device.

v0:
```python
from functools import partial

import jax
import jax.numpy as jnp
from jax import lax
from jax.sharding import PartitionSpec as P

H = 12


norm_eps = 1e-05
clip_bound = 0.01
learn_rate = 10000.0
momentum_coef = 0.5
ema_decay = 0.5


def layer_norm(inputs, gain, shift):
    centered = inputs - jnp.mean(inputs, -1, keepdims=True)
    spread = jnp.mean(centered * centered, -1, keepdims=True)
    return centered * lax.rsqrt(spread + norm_eps) * gain + shift


def gelu_tanh(inputs):
    return jax.nn.gelu(inputs, approximate=True)


def doc_info(doc_lens, tok_count, total_docs):
    doc_ends = jnp.cumsum(doc_lens)
    places = jnp.arange(tok_count, dtype=jnp.int32)
    seg_ids = jnp.sum((places[:, None] >= doc_ends[None, :]).astype(jnp.int32), 1)
    one_hot = seg_ids[:, None] == jnp.arange(doc_lens.shape[0], dtype=jnp.int32)[None, :]
    starts = doc_ends - doc_lens
    pos_ids = places - jnp.sum(jnp.where(one_hot, starts[None, :], 0), 1)
    doc_len = jnp.sum(jnp.where(one_hot, doc_lens[None, :], 0), 1)
    weights = 1.0 / (doc_len.astype(jnp.float32) * total_docs)
    return (seg_ids, pos_ids, weights)


def device_rise(first, count, devices):
    places = first + jnp.arange(count, dtype=jnp.int32)
    return 1.0 + 2.0 * places.astype(jnp.float32) / (devices - 1)


def contract(left, right, left_dim, right_dim):
    return lax.dot_general(
        left, right, (((left_dim,), (right_dim,)), ((), ())), preferred_element_type=jnp.float32
    )


def split_vecs(vecs, width):
    pieces = [vecs[index * width : (index + 1) * width] for index in range(7)]
    ff_width = vecs.shape[0] - 8 * width
    pieces.append(vecs[7 * width : 7 * width + ff_width])
    pieces.append(vecs[7 * width + ff_width :])
    return pieces


def layer_forward(hidden, mats, vecs, attn_mask):
    tok, width = hidden.shape
    head_dim = width // H
    ff_width = (mats.shape[1] - 4 * width) // 2
    gain_one, shift_one, bias_q, bias_v, bias_proj, gain_two, shift_two, bias_fc, bias_out = (
        split_vecs(vecs, width)
    )
    normed_low = layer_norm(hidden, gain_one, shift_one).astype(jnp.bfloat16)
    bias_qkv = jnp.concatenate([bias_q, jnp.zeros_like(bias_q), bias_v])
    qkv_f = jnp.dot(normed_low, mats[:, : 3 * width], preferred_element_type=jnp.float32) + bias_qkv
    qkv_low = qkv_f.astype(jnp.bfloat16).reshape(tok, 3, H, head_dim)
    scores = jnp.einsum(
        "thd,uhd->htu", qkv_low[:, 0], qkv_low[:, 1], preferred_element_type=jnp.float32
    ) * head_dim ** (-0.5)
    scores = jnp.where(attn_mask[None], scores, -1000000000.0)
    shifted = jnp.exp(scores - jnp.max(scores, -1, keepdims=True))
    attn_probs = shifted / jnp.sum(shifted, -1, keepdims=True)
    probs_low = attn_probs.astype(jnp.bfloat16)
    attended = jnp.einsum(
        "htu,uhd->thd", probs_low, qkv_low[:, 2], preferred_element_type=jnp.float32
    )
    attended = attended.reshape(tok, width).astype(jnp.bfloat16)
    middle = (
        hidden
        + jnp.dot(attended, mats[:, 3 * width : 4 * width], preferred_element_type=jnp.float32)
        + bias_proj
    )
    two_low = layer_norm(middle, gain_two, shift_two).astype(jnp.bfloat16)
    up_act = (
        jnp.dot(
            two_low, mats[:, 4 * width : 4 * width + ff_width], preferred_element_type=jnp.float32
        )
        + bias_fc
    )
    activ_low = gelu_tanh(up_act).astype(jnp.bfloat16)
    output = middle + contract(activ_low, mats[:, 4 * width + ff_width :], 1, 1) + bias_out
    saved = (
        normed_low,
        qkv_low,
        attn_probs,
        probs_low,
        attended,
        middle,
        two_low,
        up_act,
        activ_low,
    )
    return (output, saved)


def layer_backward(hidden, mats, vecs, attn_mask, grad_out):
    tok, width = hidden.shape
    head_dim = width // H
    ff_width = (mats.shape[1] - 4 * width) // 2
    unused, saved = layer_forward(hidden, mats, vecs, attn_mask)
    normed_low, qkv_low, attn_probs, probs_low, attended, middle, two_low, up_act, activ_low = saved
    gain_one, shift_one, bias_q, bias_v, bias_proj, gain_two, shift_two, bias_fc, bias_out = (
        split_vecs(vecs, width)
    )
    out_low = grad_out.astype(jnp.bfloat16)
    grad_wout = contract(out_low, activ_low, 0, 0)
    grad_bout = jnp.sum(grad_out, 0)
    grad_act = jnp.dot(out_low, mats[:, 4 * width + ff_width :], preferred_element_type=jnp.float32)
    unused_up, gelu_pull = jax.vjp(gelu_tanh, up_act)
    grad_up = gelu_pull(grad_act)[0]
    up_low = grad_up.astype(jnp.bfloat16)
    grad_wfc = contract(two_low, up_low, 0, 0)
    grad_bfc = jnp.sum(grad_up, 0)
    grad_two = contract(up_low, mats[:, 4 * width : 4 * width + ff_width], 1, 1)
    unused_two, norm_pull = jax.vjp(layer_norm, middle, gain_two, shift_two)
    grad_mid_norm, grad_g2, grad_s2 = norm_pull(grad_two)
    grad_mid = grad_out + grad_mid_norm
    mid_low = grad_mid.astype(jnp.bfloat16)
    grad_wproj = contract(attended, mid_low, 0, 0)
    grad_bproj = jnp.sum(grad_mid, 0)
    grad_att = (
        contract(mid_low, mats[:, 3 * width : 4 * width], 1, 1)
        .astype(jnp.bfloat16)
        .reshape(tok, H, head_dim)
    )
    grad_probs = jnp.einsum(
        "thd,uhd->htu", grad_att, qkv_low[:, 2], preferred_element_type=jnp.float32
    )
    grad_vals = jnp.einsum("htu,thd->uhd", probs_low, grad_att, preferred_element_type=jnp.float32)
    grad_scores = attn_probs * (grad_probs - jnp.sum(attn_probs * grad_probs, -1, keepdims=True))
    score_low = (grad_scores * head_dim ** (-0.5)).astype(jnp.bfloat16)
    grad_q = jnp.einsum(
        "htu,uhd->thd", score_low, qkv_low[:, 1], preferred_element_type=jnp.float32
    )
    grad_k = jnp.einsum(
        "htu,thd->uhd", score_low, qkv_low[:, 0], preferred_element_type=jnp.float32
    )
    grad_qkv = jnp.stack([grad_q, grad_k, grad_vals], 1).reshape(tok, 3 * width)
    qkv_grad_low = grad_qkv.astype(jnp.bfloat16)
    grad_wqkv = contract(normed_low, qkv_grad_low, 0, 0)
    grad_normed = contract(qkv_grad_low, mats[:, : 3 * width], 1, 1)
    unused_one, first_pull = jax.vjp(layer_norm, hidden, gain_one, shift_one)
    grad_in_norm, grad_g1, grad_s1 = first_pull(grad_normed)
    grad_in = grad_mid + grad_in_norm
    grad_mats = jnp.concatenate([grad_wqkv, grad_wproj, grad_wfc, grad_wout], 1)
    grad_vecs = jnp.concatenate(
        [
            grad_g1,
            grad_s1,
            jnp.sum(grad_q, 0).reshape(width),
            jnp.sum(grad_vals, 0).reshape(width),
            grad_bproj,
            grad_g2,
            grad_s2,
            grad_bfc,
            grad_bout,
        ]
    )
    return (grad_in, grad_mats, grad_vecs)


def renew(weight, moment, average, grad, factor):
    clipped = factor * grad
    moment_next = momentum_coef * moment + clipped
    weight_next = weight - learn_rate * (clipped + momentum_coef * moment_next)
    average_next = ema_decay * average + (1.0 - ema_decay) * weight_next
    return (moment_next, weight_next, average_next, weight_next.astype(jnp.bfloat16))


def per_device(
    token_ids,
    targets,
    lengths,
    embed_table,
    embed_moment,
    embed_average,
    blocks,
    block_moment,
    block_average,
    pos_table,
    pos_moment,
    pos_average,
    vectors,
    vector_moment,
    vector_average,
):
    devices = lax.axis_size(("dp", "vocab"))
    vocab_count = lax.axis_size("vocab")
    vocab_at = lax.axis_index("vocab")
    data_at = lax.axis_index("dp")
    tok = token_ids.shape[0]
    own_rows, width = embed_table.shape
    layers = blocks.shape[0]
    capacity = max(2, 2 * tok // devices)
    mats_all, pos_low, vec_low = (
        lax.all_gather(blocks.astype(jnp.bfloat16), ("dp", "vocab"), axis=2, tiled=True),
        lax.all_gather(pos_table.astype(jnp.bfloat16), ("dp", "vocab"), axis=1, tiled=True),
        lax.all_gather(vectors.astype(jnp.bfloat16), ("dp", "vocab"), axis=0, tiled=True),
    )
    vecs_all = vec_low.astype(jnp.float32)
    vec_width = (vecs_all.shape[0] - 2 * width) // layers
    lens_group = lengths[0]
    seg_group, pos_group, weight_group = jax.vmap(
        partial(doc_info, tok_count=tok, total_docs=devices * lens_group.shape[1])
    )(lens_group)
    weight_group = weight_group * device_rise(data_at * vocab_count, vocab_count, devices)[:, None]
    seg_ids = lax.dynamic_index_in_dim(seg_group, vocab_at, 0, keepdims=False)
    pos_ids = lax.dynamic_index_in_dim(pos_group, vocab_at, 0, keepdims=False)
    own_weight = lax.dynamic_index_in_dim(weight_group, vocab_at, 0, keepdims=False)
    places = jnp.arange(tok, dtype=jnp.int32)
    attn_mask = (seg_ids[:, None] == seg_ids[None, :]) & (places[None, :] <= places[:, None])
    both_ids = jnp.stack([token_ids, targets])
    owners = both_ids // own_rows
    hits = (owners[:, :, None] == jnp.arange(devices, dtype=jnp.int32)[None, None, :]).astype(
        jnp.int32
    )
    ranks = jnp.sum((jnp.cumsum(hits, 1) - 1) * hits, 2)
    which = jnp.broadcast_to(jnp.arange(2, dtype=jnp.int32)[:, None], (2, tok))
    send_rows = (
        jnp.zeros((2, devices, capacity), jnp.int32)
        .at[which, owners, ranks]
        .set(both_ids % own_rows)
    )
    table_low = embed_table.astype(jnp.bfloat16)
    local_rows = lax.all_to_all(send_rows, ("dp", "vocab"), split_axis=1, concat_axis=1, tiled=True)
    fetched = table_low[local_rows]
    returned_rows = lax.all_to_all(
        fetched, ("dp", "vocab"), split_axis=1, concat_axis=1, tiled=True
    )
    gotten = returned_rows[which, owners, ranks]
    pos_hot = (pos_ids[:, None] == jnp.arange(pos_low.shape[0], dtype=jnp.int32)[None, :]).astype(
        jnp.bfloat16
    )
    hidden = gotten[0].astype(jnp.float32) + jnp.dot(
        pos_hot, pos_low, preferred_element_type=jnp.float32
    )
    layer_inputs = []
    for layer in range(layers):
        layer_inputs.append(hidden)
        hidden, unused = layer_forward(
            hidden,
            mats_all[layer],
            vecs_all[layer * vec_width : (layer + 1) * vec_width],
            attn_mask,
        )
    tail = vecs_all[layers * vec_width :]
    final_low = layer_norm(hidden, tail[:width], tail[width:]).astype(jnp.bfloat16)
    group_rows = lax.all_gather(final_low, "vocab", axis=0, tiled=True)
    vocab_rows = lax.all_gather(table_low, "dp", axis=0, tiled=True)
    table_blocks = vocab_rows.reshape(vocab_rows.shape[0] // own_rows, own_rows, width)
    group_weight = weight_group.reshape(-1)
    group_count = group_rows.shape[0]

    def forward_block(carry, piece):
        top, total = carry
        logits = contract(group_rows, piece, 1, 1)
        new_top = jnp.maximum(top, jnp.max(logits, 1))
        total = total * jnp.exp(top - new_top) + jnp.sum(jnp.exp(logits - new_top[:, None]), 1)
        return ((new_top, total), None)

    start_top = jnp.full((group_count,), -1e30, jnp.float32)
    (row_top, row_total), unused = lax.scan(
        forward_block, (start_top, jnp.zeros((group_count,), jnp.float32)), table_blocks
    )
    peak = lax.pmax(row_top, "vocab")
    row_total = lax.psum(row_total * jnp.exp(row_top - peak), "vocab")
    row_top = peak
    group_lse = row_top + jnp.log(row_total)
    own_lse = lax.dynamic_slice_in_dim(group_lse, vocab_at * tok, tok)
    target_rows = gotten[1].astype(jnp.float32)
    final_f = final_low.astype(jnp.float32)
    loss_part = jnp.sum(own_weight * (own_lse - jnp.sum(final_f * target_rows, 1)))

    def backward_block(acc, piece):
        logits = contract(group_rows, piece, 1, 1)
        grad_low = (group_weight[:, None] * jnp.exp(logits - group_lse[:, None])).astype(
            jnp.bfloat16
        )
        return (acc + jnp.dot(grad_low, piece, preferred_element_type=jnp.float32), grad_low)

    group_grad, grad_stack = lax.scan(
        backward_block, jnp.zeros((group_count, width), jnp.float32), table_blocks
    )
    own_grad = lax.psum_scatter(
        group_grad.astype(jnp.bfloat16), "vocab", scatter_dimension=0, tiled=True
    ).astype(jnp.float32)
    term = jnp.einsum("ktr,td->krd", grad_stack, group_rows, preferred_element_type=jnp.float32)
    table_grad = lax.psum_scatter(
        term.reshape(own_rows * lax.axis_size("dp"), width).astype(jnp.bfloat16),
        "dp",
        scatter_dimension=0,
        tiled=True,
    ).astype(jnp.float32)
    grad_final = own_grad - own_weight[:, None] * target_rows
    target_grad = -own_weight[:, None] * final_f
    unused_final, final_pull = jax.vjp(layer_norm, hidden, tail[:width], tail[width:])
    grad_hidden, grad_gf, grad_sf = final_pull(grad_final)
    mats_parts = [None] * layers
    vec_parts = [None] * layers
    for layer in reversed(range(layers)):
        grad_hidden, grad_mats, grad_vecs = layer_backward(
            layer_inputs[layer],
            mats_all[layer],
            vecs_all[layer * vec_width : (layer + 1) * vec_width],
            attn_mask,
            grad_hidden,
        )
        mats_parts[layer] = grad_mats
        vec_parts[layer] = grad_vecs
    grad_vec_all = jnp.concatenate(vec_parts + [grad_gf, grad_sf])
    grad_pos = lax.dot_general(
        pos_hot.astype(jnp.float32),
        grad_hidden,
        (((0,), (0,)), ((), ())),
        precision=lax.Precision.HIGHEST,
    )
    mats_shard, pos_shard, vec_shard = (
        lax.psum_scatter(jnp.stack(mats_parts), ("dp", "vocab"), scatter_dimension=2, tiled=True),
        lax.psum_scatter(grad_pos, ("dp", "vocab"), scatter_dimension=1, tiled=True),
        lax.psum_scatter(grad_vec_all, ("dp", "vocab"), scatter_dimension=0, tiled=True),
    )
    send_grads = (
        jnp.zeros((2, devices, capacity, width), jnp.float32)
        .at[which, owners, ranks]
        .set(jnp.stack([grad_hidden, target_grad]))
    )
    back_grads = lax.all_to_all(
        send_grads.astype(jnp.bfloat16), ("dp", "vocab"), split_axis=1, concat_axis=1, tiled=True
    ).astype(send_grads.dtype)
    table_grad = table_grad + jnp.zeros((own_rows, width), jnp.float32).at[
        local_rows.reshape(-1)
    ].add(back_grads.reshape(-1, width))
    local_squares = (
        jnp.sum(table_grad * table_grad)
        + jnp.sum(mats_shard * mats_shard)
        + jnp.sum(pos_shard * pos_shard)
        + jnp.sum(vec_shard * vec_shard)
    )
    loss_sum, squares = lax.psum((loss_part, local_squares), ("dp", "vocab"))
    grad_norm = jnp.sqrt(squares)
    factor = clip_bound / jnp.maximum(grad_norm, clip_bound)
    embed_out = renew(embed_table, embed_moment, embed_average, table_grad, factor)
    block_out = renew(blocks, block_moment, block_average, mats_shard, factor)
    pos_out = renew(pos_table, pos_moment, pos_average, pos_shard, factor)
    vector_out = renew(vectors, vector_moment, vector_average, vec_shard, factor)
    return (
        loss_sum,
        grad_norm,
        embed_out[0],
        embed_out[1],
        embed_out[2],
        embed_out[3],
        block_out[0],
        block_out[1],
        block_out[2],
        block_out[3],
        pos_out[0],
        pos_out[1],
        pos_out[2],
        pos_out[3],
        vector_out[0],
        vector_out[1],
        vector_out[2],
        vector_out[3],
    )


def solution(mesh):
    return jax.shard_map(
        per_device,
        mesh=mesh,
        in_specs=(
            P(("dp", "vocab")),
            P(("dp", "vocab")),
            P("dp", None, None),
            P(("dp", "vocab"), None),
            P(("dp", "vocab"), None),
            P(("dp", "vocab"), None),
            P(None, None, ("dp", "vocab")),
            P(None, None, ("dp", "vocab")),
            P(None, None, ("dp", "vocab")),
            P(None, ("dp", "vocab")),
            P(None, ("dp", "vocab")),
            P(None, ("dp", "vocab")),
            P(("dp", "vocab")),
            P(("dp", "vocab")),
            P(("dp", "vocab")),
        ),
        out_specs=(
            P(),
            P(),
            P(("dp", "vocab"), None),
            P(("dp", "vocab"), None),
            P(("dp", "vocab"), None),
            P(("dp", "vocab"), None),
            P(None, None, ("dp", "vocab")),
            P(None, None, ("dp", "vocab")),
            P(None, None, ("dp", "vocab")),
            P(None, None, ("dp", "vocab")),
            P(None, ("dp", "vocab")),
            P(None, ("dp", "vocab")),
            P(None, ("dp", "vocab")),
            P(None, ("dp", "vocab")),
            P(("dp", "vocab")),
            P(("dp", "vocab")),
            P(("dp", "vocab")),
            P(("dp", "vocab")),
        ),
        check_vma=False,
    )
```

profile of v0, /device:TPU:0, one launch (start us, length us, event | category | flops | bytes accessed | tf_op | source)
XLA Modules:
  0.0 1266.0 jit_solution(8103137043855358326)
XLA Ops:
  11.9 15.1 %scatter_fusion = s32[2,128,2]{1,2,0:T(2,128)S(1)} fusion(s32[2,128,2]{1,2,0:T(2,128)S(1)} %broadcast.418, s32[256]{0:T(256)S(1)} %bitcast.233, s32[256]{0:T(256)S(1)} %get-tuple-element.339), kind=kCustom, calls=%fused_computation.2 | custom fusion | bytes 6144 | tf_op jit(solution)/shard_map/scatter | solution.py:235
  27.7 11.1 all-to-all-start
  39.2 36.2 %all-gather.1 = bf16[128,6,80]{2,1,0:T(8,128)(2,1)S(1)} all-gather(bf16[1,6,80]{2,1,0:T(8,128)(2,1)S(1)} %convert_bitcast_fusion.4), channel_id=1, replica_groups=mesh['dp'=16,'vocab'=8] {'dp','vocab'}, dimensions={0}, use_global_device_ids=true | all-gather | bytes 123840 | tf_op jit(solution)/shard_map/all_gather | solution.py:210
  76.3 66.7 %all-reduce = bf16[19968]{0:T(1024)(128)(2,1)S(1)} all-reduce(bf16[19968]{0:T(1024)(128)(2,1)S(1)} %dynamic-update-slice), channel_id=1, replica_groups=mesh['dp'=16,'vocab'=8] {'dp','vocab'}, use_global_device_ids=true, to_apply=%add | all-reduce | flops 19968 | bytes 79872
  147.8 5.2 all-to-all-start.1
  153.3 16.1 %all-to-all-done.1 = bf16[2,128,2,768]{3,2,0,1:T(2,128)(2,1)S(1)} async-done(((bf16[2,128,2,768]{3,2,0,1:T(2,128)(2,1)}), bf16[2,128,2,768]{3,2,0,1:T(2,128)(2,1)S(1)}, u32[]{:S(2)}, u32[]{:S(2)}) %all-to-all-start.1) | async-done | bytes 786464 | tf_op jit(solution)/shard_map/all_to_all | solution.py:240
  172.8 16.5 %slice_bitcast_fusion = (bf16[768,9216]{0,1:T(8,128)(2,1)}, bf16[768,9216]{0,1:T(8,128)(2,1)S(1)}) fusion(bf16[2,768,9216]{1,2,0:T(8,128)(2,1)} %all-gather.6.cloned.1.call-done), kind=kLoop, calls=%fused_computation.29 | loop fusion | bytes 56623104 | tf_op jit(solution)/shard_map/squeeze | solution.py:255
  225.9 21.7 %all-gather.8.cloned.1.call-done = bf16[1024,768]{1,0:T(8,128)(2,1)} async-done(((bf16[128,768]{1,0:T(8,128)(2,1)}), bf16[1024,768]{1,0:T(8,128)(2,1)}) %all-gather.8.cloned.1.call-update) | async-done | bytes 1572880 | tf_op jit(solution)/shard_map/all_gather | solution.py:261
  247.7 60.0 %while.26 = (s32[]{:T(128)}, f32[1024]{0:T(1024)S(1)}, f32[1024]{0:T(1024)}, bf16[16,393,768]{2,1,0:T(8,128)(2,1)}, bf16[1024,768]{1,0:T(8,128)(2,1)}, /*index=5*/s32[]{:T(128)}, s32[]{:T(128)}) while((s32[]{:T(128)}, f32[1024]{0:T(1024)S(1)}, f32[1024]{0:T(1024)}, bf16[16,393,768]{2,1,0:T(8,128)(2,1)}, ...), condition=%wide.region_24.25_spmd.clone, body=%wide.region_21.24_spmd.clone.sunk | while | flops 619347968 | bytes 5492892 | solution.py:275
  307.6 13.9 %pmax.7 = f32[1024]{0:T(1024)} all-reduce(f32[1024]{0:T(1024)S(1)} %get-tuple-element.84), channel_id=1, replica_groups=mesh['dp'=16,'vocab'=8] {'vocab'}, use_global_device_ids=true, to_apply=%region_25.26 | all-reduce | flops 1024 | bytes 8192 | tf_op jit(solution)/shard_map/pmax | solution.py:278
  322.8 12.5 psum.21
  336.6 101.0 %while.27 = (s32[]{:T(128)}, f32[1024,768]{1,0:T(8,128)S(1)}, bf16[16,1024,393]{1,2,0:T(8,128)(2,1)}, f32[8,128]{1,0:T(8,128)}, bf16[16,393,768]{2,1,0:T(8,128)(...) while((s32[]{:T(128)}, f32[1024,768]{1,0:T(8,128)S(1)}, ...), condition=%wide.region_31.32_spmd.clone, body=%wide.region_30.31_spmd.clone.sunk | while | flops 1239051264 | bytes 11531379 | solution.py:294
  439.5 31.2 %reduce-scatter.4.cloned.1.call-done = bf16[128,768]{1,0:T(8,128)(2,1)} async-done(((bf16[1024,768]{1,0:T(8,128)(2,1)}), bf16[128,768]{1,0:T(8,128)(2,1)}) %reduce-scatter.4.cloned.1.call-update) | async-done | bytes 196624 | tf_op jit(solution)/shard_map/reduce_scatter | solution.py:297
  586.6 19.4 %maximum_bitcast_fusion = f32[1,768,9216]{2,1,0:T(8,128)} fusion(f32[768,3072]{1,0:T(8,128)} %fusion.129, f32[768,3072]{1,0:T(8,128)} %fusion.108, f32[768,768]{1,0:T(8,128)} %fusion.126, f32[768,2304]{1,0:T(8,128)} %fusion.170), kind=kLoop, calls=%fused_computation.27 | loop fusion | flops 21233664 | bytes 56623104 | tf_op jit(solution)/shard_map/stack | solution.py:331
  606.0 18.8 %maximum_bitcast_fusion.1 = f32[1,768,9216]{2,1,0:T(8,128)} fusion(f32[768,3072]{1,0:T(8,128)} %fusion.169, f32[768,3072]{1,0:T(8,128)} %fusion.111, f32[768,768]{1,0:T(8,128)S(1)} %fusion.132, f32[768,2304]{1,0:T(8,128)} %fusion.171), kind=kLoop, calls=%fused_computation.28 | loop fusion | flops 21233664 | bytes 56623104 | tf_op jit(solution)/shard_map/stack | solution.py:331
  624.8 37.7 %pad_maximum_fusion = f32[2,768,9216]{2,1,0:T(8,128)} fusion(f32[1,768,9216]{2,1,0:T(8,128)} %maximum_bitcast_fusion.1, f32[1,768,9216]{2,1,0:T(8,128)} %maximum_bitcast_fusion), kind=kLoop, calls=%fused_computation.26 | loop fusion | flops 14155776 | bytes 113246208 | tf_op jit(solution)/shard_map/stack | solution.py:331
  662.5 81.8 %copy.214 = f32[2,768,9216]{1,0,2:T(2,128)} copy(f32[2,768,9216]{2,1,0:T(8,128)} %pad_maximum_fusion) | data formatting | bytes 113246208 | tf_op jit(solution)/shard_map/stack | solution.py:331
  746.4 17.3 %convolution_convert_fusion = bf16[16,393,768]{2,1,0:T(8,128)(2,1)} fusion(bf16[16,1024,393]{1,2,0:T(8,128)(2,1)} %get-tuple-element.86, bf16[1024,768]{1,0:T(8,128)(2,1)S(1)} %copy-done.133), kind=kOutput, calls=%fused_computation.31 | convolution fusion | flops 9894998016 | bytes 24109056 | tf_op jit(solution)/shard_map/ktr,td->krd/dot_general | solution.py:300
  763.7 12.4 convert_element_type.218
  777.0 16.3 %scatter_fusion.1 = f32[2,128,2,768]{3,2,1,0:T(2,128)S(1)} fusion(f32[2,128,2,768]{3,2,1,0:T(2,128)S(1)} %broadcast_in_dim.93, s32[256]{0:T(256)S(1)} %bitcast.234, f32[256,768]{1,0:T(8,128)S(1)} %bitcast.236), kind=kCustom, calls=%fused_computation.3 | custom fusion | bytes 2362368 | tf_op jit(solution)/shard_map/scatter | solution.py:338
  795.2 8.0 all-to-all-start.2
  803.2 133.5 %fusion = bf16[400,768]{1,0:T(8,128)(2,1)S(1)} fusion(bf16[6288,768]{1,0:T(8,128)(2,1)} %convert_element_type.218), kind=kCustom, calls=%all-reduce-scatter | all-reduce-scatter fusion | flops 4915201 | bytes 10273280
  957.7 218.3 %all-reduce.11.cloned.1.call-done = f32[2,768,9216]{1,0,2:T(2,128)} async-done(((f32[2,768,9216]{1,0,2:T(2,128)}), f32[2,768,9216]{1,0,2:T(2,128)}) %all-reduce.11.cloned.1.call-update) | async-done | bytes 56623120
  1180.7 66.2 %all-reduce.6 = (f32[]{:T(128)}, f32[]{:T(128)}) all-reduce(f32[]{:T(128)} %multiply_reduce_fusion.21, f32[]{:T(128)S(6)} %add.489), channel_id=1, replica_groups=mesh['dp'=16,'vocab'=8] {'dp','vocab'}, use_global_device_ids=true, to_apply=%region_29.30 | all-reduce | flops 2 | bytes 16 | tf_op jit(solution)/shard_map/psum | solution.py:352
  (652 shorter events, 367.2 us)
Async XLA Ops:
  7.2 165.6 %all-gather.6.cloned.1.call-start = ((), (), s32[]{:S(2)}) async-start(), calls=%async_computation.4 | async-start | bytes 28532736 | tf_op jit(solution)/shard_map/all_gather | solution.py:209
  9.0 216.9 %all-gather.10.cloned.1.call-start = ((), (), s32[]{:S(2)}) async-start(), calls=%async_computation.7 | async-start | bytes 10444800 | tf_op jit(solution)/shard_map/all_gather | solution.py:262
  11.8 131.3 %copy-start.3 = (f32[393,768]{1,0:T(8,128)S(1)}, f32[393,768]{1,0:T(8,128)}, u32[]{:S(2)}) copy-start(f32[393,768]{1,0:T(8,128)} %param.22) | copy-start | bytes 3621892
  11.8 64.4 %copy-start = (s32[2,128,1]{1,2,0:T(1,128)}, s32[2,128,1]{1,2,0:T(1,128)S(1)}, u32[]{:S(2)}) copy-start(s32[2,128,1]{1,2,0:T(1,128)S(1)} %get-tuple-element.300) | copy-start | bytes 3076
  27.7 115.5 %all-to-all-start = ((s32[2,128,2]{2,0,1:T(2,128)}), s32[2,128,2]{2,0,1:T(2,128)S(1)}, u32[]{:S(2)}, u32[]{:S(2)}) async-start(s32[2,128,2]{2,0,1:T(2,128)} %copy.189), calls=%async_computation | async-start | bytes 262144 | tf_op jit(solution)/shard_map/all_to_all | solution.py:238
  75.7 96.5 %copy-start.115 = (s32[128]{0:T(128)}, s32[128]{0:T(128)S(1)}, u32[]{:S(2)}) copy-start(s32[128]{0:T(128)S(1)} %fusion.147) | copy-start | bytes 1540
  147.8 21.5 %all-to-all-start.1 = ((bf16[2,128,2,768]{3,2,0,1:T(2,128)(2,1)}), bf16[2,128,2,768]{3,2,0,1:T(2,128)(2,1)S(1)}, u32[]{:S(2)}, u32[]{:S(2)}) async-start(bf16[2,128,2,768]{3,2,0,1:T(2,128)(2,1)} %copy.194), calls=%async_computation.1 | async-start | bytes 1572864 | tf_op jit(solution)/shard_map/all_to_all | solution.py:240
  153.0 94.7 %all-gather.8.cloned.1.call-start = ((), (), s32[]{:S(2)}) async-start(), calls=%async_computation.5 | async-start | bytes 1769472 | tf_op jit(solution)/shard_map/all_gather | solution.py:261
  153.1 47.1 %copy-start.62 = (f32[768]{0:T(1024)}, f32[768]{0:T(1024)S(1)}, u32[]{:S(2)}) copy-start(f32[768]{0:T(1024)S(1)} %get-tuple-element.328) | copy-start | bytes 9220
  153.1 55.5 %copy-start.56 = (f32[768]{0:T(1024)}, f32[768]{0:T(1024)S(1)}, u32[]{:S(2)}) copy-start(f32[768]{0:T(1024)S(1)} %get-tuple-element.323) | copy-start | bytes 9220
  153.1 55.5 %copy-start.64 = (f32[768]{0:T(1024)}, f32[768]{0:T(1024)S(1)}, u32[]{:S(2)}) copy-start(f32[768]{0:T(1024)S(1)} %get-tuple-element.324) | copy-start | bytes 9220
  153.1 63.3 %copy-start.60 = (f32[768]{0:T(1024)}, f32[768]{0:T(1024)S(1)}, u32[]{:S(2)}) copy-start(f32[768]{0:T(1024)S(1)} %get-tuple-element.320) | copy-start | bytes 9220
  153.1 71.7 %copy-start.68 = (f32[768]{0:T(1024)}, f32[768]{0:T(1024)S(1)}, u32[]{:S(2)}) copy-start(f32[768]{0:T(1024)S(1)} %get-tuple-element.317) | copy-start | bytes 9220
  153.2 60.3 %copy-start.71 = (pred[128,128]{0,1:T(8,128)(4,1)}, pred[128,128]{0,1:T(8,128)(4,1)S(1)}, u32[]{:S(2)}) copy-start(pred[128,128]{0,1:T(8,128)(4,1)S(1)} %fusion.136) | copy-start | bytes 49156
  225.8 244.9 %reduce-scatter.4.cloned.1.call-start = ((), (), s32[]{:S(2)}) async-start(), calls=%async_computation.6 | async-start | bytes 1769472 | tf_op jit(solution)/shard_map/reduce_scatter | solution.py:297
  439.0 506.3 %all-reduce.13.cloned.1.call-start = ((), (), s32[]{:S(2)}) async-start(), calls=%async_computation.9 | async-start | bytes 950272
  586.3 589.7 %all-reduce.11.cloned.1.call-start = ((), (), s32[]{:S(2)}) async-start(), calls=%async_computation.8 | async-start | bytes 113246208
  795.2 152.8 %all-to-all-start.2 = ((bf16[2,128,2,768]{3,2,0,1:T(2,128)(2,1)}), bf16[2,128,2,768]{3,2,0,1:T(2,128)(2,1)S(1)}, u32[]{:S(2)}, u32[]{:S(2)}) async-start(bf16[2,128,2,768]{3,2,0,1:T(2,128)(2,1)} %copy.209), calls=%async_computation.3 | async-start | bytes 1572864 | tf_op jit(solution)/shard_map/all_to_all | solution.py:340
  936.8 5.5 collective-permute-start
  956.7 290.9 %copy-start.74 = (f32[80,6]{0,1:T(8,128)S(1)}, f32[80,6]{0,1:T(8,128)}, u32[]{:S(2)}) copy-start(f32[80,6]{0,1:T(8,128)} %param.28) | copy-start | bytes 5764
  956.7 290.9 %copy-start.113 = (f32[80,6]{0,1:T(8,128)S(1)}, f32[80,6]{0,1:T(8,128)}, u32[]{:S(2)}) copy-start(f32[80,6]{0,1:T(8,128)} %param.29) | copy-start | bytes 5764
  956.7 292.2 %copy-start.120 = (f32[156]{0:T(256)S(1)}, f32[156]{0:T(256)}, u32[]{:S(2)}) copy-start(f32[156]{0:T(256)} %param.31) | copy-start | bytes 1876
  956.8 292.2 %copy-start.121 = (f32[156]{0:T(256)S(1)}, f32[156]{0:T(256)}, u32[]{:S(2)}) copy-start(f32[156]{0:T(256)} %param.32) | copy-start | bytes 1876
  956.8 293.6 %copy-start.4 = (f32[393,768]{1,0:T(8,128)S(1)}, f32[393,768]{1,0:T(8,128)}, u32[]{:S(2)}) copy-start(f32[393,768]{1,0:T(8,128)} %param.22) | copy-start | bytes 3621892
  (156 other events, 946.3 us)
Sparse Core Ops, SparseCore 0:
  11.8 101.8 all-gather.5
  116.4 85.2 all-gather.9
  225.9 21.7 all-gather.7
  439.1 31.4 reduce-scatter.3
  586.4 143.1 all-reduce.12
  744.5 431.4 all-reduce.10
where the time goes:
time: 1280 us; the launch traced here: 1270 us
  blocking collectives  329 us (26%)
  waiting for transfers between devices  290 us (23%)
  matrix products  263 us (21%)
  local copies, waits for them, and re-layouts  210 us (16%)
  other arithmetic  123 us (10%)
  starting transfers between devices  28 us (2%)
  between operations  21.7 us (2%)
    unnamed x9, waiting for transfers between devices  221 us
    unnamed x2, blocking collectives  200 us
    dot_general x48, matrix products, contract(): lax.dot_general(left, right, (((left_dim,), (right_dim,)), ((), ())), pre...  151 us
    another operation x1, local copies, waits for them, and re-layouts, per_device(): jnp.stack(mats_parts)  81.8 us
    another operation x3, other arithmetic, per_device(): jnp.stack(mats_parts)  75.9 us
    psum x1, blocking collectives, per_device(): loss_sum, squares = lax.psum((loss_part, local_squares), ('dp', 'vocab'))  66.2 us
    dot_general x16, matrix products, backward_block(): jnp.dot(grad_low, piece, preferred_element_type=jnp.float32)  47.4 us
    all_gather x1, blocking collectives, per_device(): lax.all_gather(pos_table.astype(jnp.bfloat16), ('dp', 'vocab'), axis=1, t...  36.2 us
  transfers between devices with their start and end apart: 10, of which 5 were waited for; matrix products, arithmetic and copies ran while one was open for 34% of the time, Pallas kernels for 0%

commit v1 on v0

v1 whole, which is shorter than its diff:
```python
from functools import partial

import jax
import jax.numpy as jnp
from jax import lax
from jax.experimental import pallas as pl
from jax.experimental.pallas import tpu as pltpu
from jax.sharding import PartitionSpec as P

H = 12
RING = 4
ORDERS = ((2, 1, 0), (1, 0, 2), (0, 2, 1))

norm_eps = 1e-05
clip_bound = 0.01
learn_rate = 10000.0
momentum_coef = 0.5
ema_decay = 0.5


def place():
    dp = lax.axis_index("dp")
    vocab = lax.axis_index("vocab")
    return (lax.div(dp, RING), lax.rem(dp, RING), lax.div(vocab, 2)), lax.rem(vocab, 2)


def device_at(at, core):
    return (at[0] * RING + at[1], at[2] * 2 + core)


def moved(at, axis, by):
    out = list(at)
    out[axis] = lax.rem(at[axis] + by, RING)
    return tuple(out)


class Wires:
    def __init__(self, send, recv):
        self.send, self.recv, self.count, self.live = send, recv, 0, []

    def copy(self, src, dst, device):
        number = self.count
        self.count += 1
        op = pltpu.make_async_remote_copy(
            src_ref=src,
            dst_ref=dst,
            send_sem=self.send.at[number],
            recv_sem=self.recv.at[number],
            device_id=device,
            device_id_type=pl.DeviceIdType.MESH,
        )
        op.start()
        self.live.append(op)
        return op

    def drain(self):
        for op in self.live:
            op.wait_send()


def greet(devices):
    barrier = pltpu.get_barrier_semaphore()
    for device in devices:
        pl.semaphore_signal(
            barrier, inc=1, device_id=device, device_id_type=pl.DeviceIdType.MESH
        )
    pl.semaphore_wait(barrier, len(devices))


def neighbours(at, core):
    near = [device_at(moved(at, axis, by), core) for axis in range(3) for by in (1, RING - 1)]
    return near + [device_at(at, 1 - core)]


def gather_kernel(
    mine_ref, small_ref, first_ref, second_ref, small_out, peer, block, send, recv, local
):
    at, core = place()
    out_refs = (first_ref, second_ref)
    rows, half = mine_ref.shape[1], mine_ref.shape[2] // 2
    part = 2 * rows // 3
    sibling = device_at(at, 1 - core)
    greet(neighbours(at, core))
    wires = Wires(send, recv)
    cols = pl.ds(pl.multiple_of(core * half, half), half)
    other = pl.ds(pl.multiple_of((1 - core) * half, half), half)

    swap = wires.copy(mine_ref.at[:, :, other], peer, sibling)
    small_local = pltpu.make_async_copy(small_ref, small_out.at[at[0], at[1], at[2], core], local.at[0])
    small_local.start()
    swap.wait_recv()
    for layer in range(2):
        own = jnp.where(core == 0, mine_ref[layer, :, :half], mine_ref[layer, :, half:])
        got = peer[layer]
        both = jnp.concatenate(
            [jnp.where(core == 0, own, got), jnp.where(core == 0, got, own)], 0
        )
        block[layer] = both.astype(jnp.bfloat16)
    block_local = []
    for layer in range(2):
        op = pltpu.make_async_copy(
            block.at[layer],
            out_refs[layer].at[at[0], at[1], at[2], :, cols],
            local.at[1 + layer],
        )
        op.start()
        block_local.append(op)

    def bundle(layer, p, phase, c, piece=None):
        order = ORDERS[p]
        index = list(at)
        index[order[phase]] = c
        for axis in order[:phase]:
            index[axis] = pl.ds(0, RING)
        first, count = p * part, part
        if piece is not None:
            if phase == 0:
                first, count = (first, 32) if piece == 0 else (first + 32, part - 32)
            else:
                index[order[0]] = pl.ds(2 * piece, 2)
        return out_refs[layer].at[index[0], index[1], index[2], pl.ds(first, count), cols]

    def small_bundle(phase, c):
        order = ORDERS[0]
        index = list(at)
        index[order[phase]] = c
        for axis in order[:phase]:
            index[axis] = pl.ds(0, RING)
        return small_out.at[index[0], index[1], index[2], core]

    def right(axis):
        return device_at(moved(at, axis, 1), core)

    def left(axis):
        return device_at(moved(at, axis, RING - 1), core)

    chains = [(layer, p) for layer in range(2) for p in range(3)]
    pending = []
    small_local.wait()
    for op in block_local:
        op.wait()
    for phase in range(3):
        steps = {}
        for key in chains:
            layer, p = key
            axis = ORDERS[p][phase]
            src = bundle(layer, p, phase, at[axis])
            if phase == 2:
                pending.append(wires.copy(src, src, sibling))
            steps[key] = (wires.copy(src, src, right(axis)), wires.copy(src, src, left(axis)))
        axis = ORDERS[0][phase]
        src = small_bundle(phase, at[axis])
        small_steps = (wires.copy(src, src, right(axis)), wires.copy(src, src, left(axis)))
        forwards = {}
        for key in chains:
            layer, p = key
            axis = ORDERS[p][phase]
            before, after = lax.rem(at[axis] + 3, RING), lax.rem(at[axis] + 1, RING)
            steps[key][0].wait_recv()
            src = bundle(layer, p, phase, before, 0)
            one = wires.copy(src, src, right(axis))
            steps[key][1].wait_recv()
            src = bundle(layer, p, phase, after, 1)
            two = wires.copy(src, src, left(axis))
            forwards[key] = (one, two)
            if phase == 2:
                for c in (before, after):
                    src = bundle(layer, p, phase, c)
                    pending.append(wires.copy(src, src, sibling))
        axis = ORDERS[0][phase]
        for op in small_steps:
            op.wait_recv()
        src = small_bundle(phase, lax.rem(at[axis] + 3, RING))
        small_forward = wires.copy(src, src, right(axis))
        for key in chains:
            layer, p = key
            axis = ORDERS[p][phase]
            across = lax.rem(at[axis] + 2, RING)
            for piece in range(2):
                forwards[key][piece].wait_recv()
                if phase == 2:
                    src = bundle(layer, p, phase, across, piece)
                    pending.append(wires.copy(src, src, sibling))
        small_forward.wait_recv()
    src = small_out.at[:, :, :, core]
    pending.append(wires.copy(src, src, sibling))
    for op in pending:
        op.wait_recv()
    wires.drain()


GATHER_COPIES = 1 + 3 * (6 * 4 + 3) + 6 * 5 + 1


def gather_weights(mine, small):
    layers, rows, width = mine.shape
    whole = jax.ShapeDtypeStruct((RING, RING, RING, 2 * rows, width), jnp.bfloat16)
    hbm = pl.BlockSpec(memory_space=pltpu.HBM)
    vmem = pl.BlockSpec(memory_space=pltpu.VMEM)
    first, second, small_all = pl.pallas_call(
        gather_kernel,
        out_shape=(
            whole,
            whole,
            jax.ShapeDtypeStruct((RING, RING, RING, 2) + small.shape, jnp.bfloat16),
        ),
        in_specs=[vmem, vmem],
        out_specs=(hbm, hbm, hbm),
        scratch_shapes=[
            pltpu.VMEM((layers, rows, width // 2), jnp.float32),
            pltpu.VMEM((layers, 2 * rows, width // 2), jnp.bfloat16),
            pltpu.SemaphoreType.DMA((GATHER_COPIES,)),
            pltpu.SemaphoreType.DMA((GATHER_COPIES,)),
            pltpu.SemaphoreType.DMA((3,)),
        ],
        compiler_params=pltpu.CompilerParams(
            collective_id=0, has_side_effects=True, vmem_limit_bytes=24 * 2**20
        ),
        name="gather_weights",
    )(mine, small)
    count = RING**3 * 2 * rows
    return (
        (first.reshape(count, width), second.reshape(count, width)),
        small_all.reshape((2 * RING**3,) + small.shape),
    )


def reduce_kernel(
    first_ref,
    second_ref,
    small_ref,
    out_ref,
    small_out,
    acc,
    sib,
    wide_half_0,
    wide_half_1,
    wide_half_2,
    wide_full,
    mid_half,
    mid_full,
    thin_half,
    thin_full,
    small_acc,
    small_sib,
    small_wide,
    small_mid,
    small_thin,
    final,
    final_peer,
    send,
    recv,
    local,
):
    at, core = place()
    grads = (first_ref, second_ref)
    rows, half = acc.shape[4], acc.shape[5]
    own_rows = rows // 2
    part = rows // 3
    sibling = device_at(at, 1 - core)
    cols = pl.ds(pl.multiple_of(core * half, half), half)
    other = pl.ds(pl.multiple_of((1 - core) * half, half), half)
    chains = [(layer, p) for layer in range(2) for p in range(3)]
    loads = {}
    number = 0
    near = (2, 1, 3, 0)

    def span(p, step, c, piece=None):
        order = ORDERS[p]
        index = list(at)
        index[order[2 - step]] = c
        for axis in order[: 2 - step]:
            index[axis] = pl.ds(0, RING)
        first, count = p * part, part
        if piece is not None:
            if step == 2:
                first, count = (first, 32) if piece == 0 else (first + 32, part - 32)
            else:
                index[order[0]] = pl.ds(2 * piece, 2)
        return index, pl.ds(first, count)

    for by in near:
        for key in chains:
            layer, p = key
            c = lax.rem(at[ORDERS[p][2]] + by, RING)
            index, where = span(p, 0, c)
            op = pltpu.make_async_copy(
                grads[layer].at[index[0], index[1], index[2], where, cols],
                acc.at[layer, index[0], index[1], index[2], where],
                local.at[number],
            )
            op.start()
            loads[key, by] = op
            number += 1
    small_load = pltpu.make_async_copy(small_ref.at[:, :, :, core], small_acc, local.at[number])
    small_load.start()

    greet(neighbours(at, core))
    wires = Wires(send, recv)
    swaps = {}
    small_swap = wires.copy(small_ref.at[:, :, :, 1 - core], small_sib, sibling)
    for by in near:
        for key in chains:
            layer, p = key
            c = lax.rem(at[ORDERS[p][2]] + by, RING)
            index, where = span(p, 0, c)
            swaps[key, by] = wires.copy(
                grads[layer].at[index[0], index[1], index[2], where, other],
                sib.at[layer, index[0], index[1], index[2], where],
                sibling,
            )

    def right(axis):
        return device_at(moved(at, axis, 1), core)

    def left(axis):
        return device_at(moved(at, axis, RING - 1), core)

    def add(layer, p, step, c, piece, terms, into=None):
        order = ORDERS[p]
        free = [axis for axis in range(3) if axis in order[: 2 - step]]
        sizes = [2 if piece is not None and axis == order[0] else RING for axis in free]
        index, where = span(p, step, c, piece)
        total = 1
        for size in sizes:
            total *= size

        def body(n, unused):
            spot = list(index)
            inner = []
            if len(free) == 2:
                inner = [lax.div(n, sizes[1]), lax.rem(n, sizes[1])]
            elif len(free) == 1:
                inner = [n]
            for axis, size, i in zip(free, sizes, inner):
                start = 2 * piece if size == 2 else 0
                spot[axis] = start + i
            here = (layer, spot[0], spot[1], spot[2], where)
            value = acc[here].astype(jnp.float32)
            for term in terms:
                value = value + term(inner, spot, where).astype(jnp.float32)
            if into is None:
                acc[here] = value.astype(jnp.bfloat16)
            else:
                into(value)
            return unused

        if total == 1:
            body(0, 0)
        else:
            lax.fori_loop(0, total, body, 0)

    def add_sibling(key, by):
        layer, p = key
        loads[key, by].wait()
        swaps[key, by].wait_recv()
        c = lax.rem(at[ORDERS[p][2]] + by, RING)
        add(
            layer,
            p,
            0,
            c,
            None,
            [lambda inner, spot, where: sib[layer, spot[0], spot[1], spot[2], where]],
        )

    wide_half = (wide_half_0, wide_half_1, wide_half_2)

    def half_slot(layer, p, step, side):
        if step == 0:
            return wide_half[p].at[layer, side]
        if step == 1:
            return mid_half.at[layer, p, side]
        return thin_half.at[layer, p, side, pl.ds(0, 32 if side == 0 else part - 32)]

    def full_slot(layer, p, step, side):
        return (wide_full, mid_full, thin_full)[step].at[layer, p, side]

    def read(slot):
        return lambda inner, spot, where: slot[tuple(inner) + (slice(None), slice(None))]

    def acc_view(layer, p, step, c, piece=None):
        index, where = span(p, step, c, piece)
        return acc.at[layer, index[0], index[1], index[2], where]

    small_order = ORDERS[0]
    small_slots = (small_wide, small_mid, small_thin)

    def small_view(step, c):
        index = list(at)
        index[small_order[2 - step]] = c
        for axis in small_order[: 2 - step]:
            index[axis] = slice(None)
        return tuple(index)

    def small_add(step, c, term):
        where = small_view(step, c)
        small_acc[where] = small_acc[where] + term

    for step in range(3):
        halves = {}
        for key in chains:
            layer, p = key
            axis = ORDERS[p][2 - step]
            if step == 0:
                add_sibling(key, 2)
            across = lax.rem(at[axis] + 2, RING)
            halves[key] = (
                wires.copy(
                    acc_view(layer, p, step, across, 0), half_slot(layer, p, step, 0), right(axis)
                ),
                wires.copy(
                    acc_view(layer, p, step, across, 1), half_slot(layer, p, step, 1), left(axis)
                ),
            )
        if step == 0:
            small_load.wait()
            small_swap.wait_recv()
            small_acc[...] = small_acc[...] + small_sib[...]
        axis = small_order[2 - step]
        across = lax.rem(at[axis] + 2, RING)
        small_half = wires.copy(
            small_acc.at[small_view(step, across)], small_slots[step].at[0], right(axis)
        )
        if step == 0:
            for key in chains:
                add_sibling(key, 1)
                add_sibling(key, 3)
        fulls = {}
        for key in chains:
            layer, p = key
            axis = ORDERS[p][2 - step]
            after, before = lax.rem(at[axis] + 1, RING), lax.rem(at[axis] + 3, RING)
            halves[key][0].wait_recv()
            add(layer, p, step, after, 0, [read(half_slot(layer, p, step, 0))])
            one = wires.copy(
                acc_view(layer, p, step, after), full_slot(layer, p, step, 0), right(axis)
            )
            halves[key][1].wait_recv()
            add(layer, p, step, before, 1, [read(half_slot(layer, p, step, 1))])
            two = wires.copy(
                acc_view(layer, p, step, before), full_slot(layer, p, step, 1), left(axis)
            )
            fulls[key] = (one, two)
        axis = small_order[2 - step]
        after, before = lax.rem(at[axis] + 1, RING), lax.rem(at[axis] + 3, RING)
        small_half.wait_recv()
        small_add(step, after, small_slots[step][0])
        small_full = (
            wires.copy(small_acc.at[small_view(step, after)], small_slots[step].at[1], right(axis)),
            wires.copy(small_acc.at[small_view(step, before)], small_slots[step].at[2], left(axis)),
        )
        for key in chains:
            layer, p = key
            axis = ORDERS[p][2 - step]
            if step == 0:
                add_sibling(key, 0)
            fulls[key][0].wait_recv()
            fulls[key][1].wait_recv()
            terms = [read(full_slot(layer, p, step, side)) for side in range(2)]
            if step < 2:
                add(layer, p, step, at[axis], None, terms)
            else:

                def keep(value, layer=layer, p=p):
                    final[layer, p * part : (p + 1) * part] = value

                add(layer, p, step, at[axis], None, terms, keep)
        axis = small_order[2 - step]
        for op in small_full:
            op.wait_recv()
        small_add(step, at[axis], small_slots[step][1] + small_slots[step][2])

    theirs = pl.ds(pl.multiple_of((1 - core) * own_rows, own_rows), own_rows)
    swap = wires.copy(final.at[:, theirs], final_peer, sibling)
    small_out[...] = small_acc[at]
    swap.wait_recv()
    for layer in range(2):
        own = jnp.where(core == 0, final[layer, :own_rows], final[layer, own_rows:])
        got = final_peer[layer]
        out_ref[layer, :, :half] = jnp.where(core == 0, own, got)
        out_ref[layer, :, half:] = jnp.where(core == 0, got, own)
    wires.drain()


REDUCE_COPIES = 1 + 24 + 3 * (6 * 4 + 3) + 1


def reduce_weights(first, second, small):
    count, width = first.shape
    rows, half = count // RING**3, width // 2
    part = rows // 3
    torus = (RING, RING, RING)
    small_shape = small.shape[1:]
    hbm = pl.BlockSpec(memory_space=pltpu.HBM)
    vmem = pl.BlockSpec(memory_space=pltpu.VMEM)
    low = jnp.bfloat16

    def wide_shape(p):
        order = ORDERS[p]
        free = [axis for axis in range(3) if axis in order[:2]]
        return tuple(2 if axis == order[0] else RING for axis in free)

    return pl.pallas_call(
        reduce_kernel,
        out_shape=(
            jax.ShapeDtypeStruct((2, rows // 2, width), jnp.float32),
            jax.ShapeDtypeStruct(small_shape, jnp.float32),
        ),
        in_specs=[hbm, hbm, hbm],
        out_specs=(vmem, vmem),
        scratch_shapes=[
            pltpu.VMEM((2,) + torus + (rows, half), low),
            pltpu.VMEM((2,) + torus + (rows, half), low),
        ]
        + [pltpu.VMEM((2, 2) + wide_shape(p) + (part, half), low) for p in range(3)]
        + [
            pltpu.VMEM((2, 3, 2, RING, RING, part, half), low),
            pltpu.VMEM((2, 3, 2, 2, part, half), low),
            pltpu.VMEM((2, 3, 2, RING, part, half), low),
            pltpu.VMEM((2, 3, 2, 32, half), low),
            pltpu.VMEM((2, 3, 2, part, half), low),
            pltpu.VMEM(torus + small_shape, jnp.float32),
            pltpu.VMEM(torus + small_shape, jnp.float32),
            pltpu.VMEM((3, RING, RING) + small_shape, jnp.float32),
            pltpu.VMEM((3, RING) + small_shape, jnp.float32),
            pltpu.VMEM((3,) + small_shape, jnp.float32),
            pltpu.VMEM((2, rows, half), jnp.float32),
            pltpu.VMEM((2, rows // 2, half), jnp.float32),
            pltpu.SemaphoreType.DMA((REDUCE_COPIES,)),
            pltpu.SemaphoreType.DMA((REDUCE_COPIES,)),
            pltpu.SemaphoreType.DMA((25,)),
        ],
        compiler_params=pltpu.CompilerParams(
            collective_id=1, has_side_effects=True, vmem_limit_bytes=58 * 2**20
        ),
        name="reduce_weights",
    )(
        first.reshape(torus + (rows, width)),
        second.reshape(torus + (rows, width)),
        small.reshape(torus + (2,) + small_shape),
    )


def sum_kernel(in_ref, out_ref, slots, send, recv):
    at, core = place()
    sibling = device_at(at, 1 - core)
    partners = [sibling] + [
        device_at(moved(at, axis, by), core) for axis in range(3) for by in range(1, RING)
    ]
    greet(partners)
    wires = Wires(send, recv)
    slots[0, core] = in_ref[...]
    swap = wires.copy(in_ref, slots.at[0, core], sibling)
    swap.wait_recv()
    value = slots[0, 0] + slots[0, 1]
    for axis in range(3):
        slots[1 + axis, at[axis]] = value
        ops = []
        for by in range(1, RING):
            ops.append(
                wires.copy(
                    slots.at[1 + axis, at[axis]],
                    slots.at[1 + axis, at[axis]],
                    device_at(moved(at, axis, by), core),
                )
            )
        for op in ops:
            op.wait_recv()
        value = slots[1 + axis, 0]
        for c in range(1, RING):
            value = value + slots[1 + axis, c]
    out_ref[...] = value
    wires.drain()


def sum_all(value):
    vmem = pl.BlockSpec(memory_space=pltpu.VMEM)
    return pl.pallas_call(
        sum_kernel,
        out_shape=jax.ShapeDtypeStruct(value.shape, jnp.float32),
        in_specs=[vmem],
        out_specs=vmem,
        scratch_shapes=[
            pltpu.VMEM((4, RING) + value.shape, jnp.float32),
            pltpu.SemaphoreType.DMA((10,)),
            pltpu.SemaphoreType.DMA((10,)),
        ],
        compiler_params=pltpu.CompilerParams(collective_id=2, has_side_effects=True),
        name="sum_all",
    )(value)


def layer_norm(inputs, gain, shift):
    centered = inputs - jnp.mean(inputs, -1, keepdims=True)
    spread = jnp.mean(centered * centered, -1, keepdims=True)
    return centered * lax.rsqrt(spread + norm_eps) * gain + shift


def gelu_tanh(inputs):
    return jax.nn.gelu(inputs, approximate=True)


def doc_info(doc_lens, tok_count, total_docs):
    doc_ends = jnp.cumsum(doc_lens)
    places = jnp.arange(tok_count, dtype=jnp.int32)
    seg_ids = jnp.sum((places[:, None] >= doc_ends[None, :]).astype(jnp.int32), 1)
    one_hot = seg_ids[:, None] == jnp.arange(doc_lens.shape[0], dtype=jnp.int32)[None, :]
    starts = doc_ends - doc_lens
    pos_ids = places - jnp.sum(jnp.where(one_hot, starts[None, :], 0), 1)
    doc_len = jnp.sum(jnp.where(one_hot, doc_lens[None, :], 0), 1)
    weights = 1.0 / (doc_len.astype(jnp.float32) * total_docs)
    return (seg_ids, pos_ids, weights)


def device_rise(first, count, devices):
    places = first + jnp.arange(count, dtype=jnp.int32)
    return 1.0 + 2.0 * places.astype(jnp.float32) / (devices - 1)


def contract(left, right, left_dim, right_dim):
    return lax.dot_general(
        left, right, (((left_dim,), (right_dim,)), ((), ())), preferred_element_type=jnp.float32
    )


def split_vecs(vecs, width):
    pieces = [vecs[index * width : (index + 1) * width] for index in range(7)]
    ff_width = vecs.shape[0] - 8 * width
    pieces.append(vecs[7 * width : 7 * width + ff_width])
    pieces.append(vecs[7 * width + ff_width :])
    return pieces


def split_mats(mats, width):
    ff_width = (mats.shape[0] - 4 * width) // 2
    cuts = [0, 3 * width, 4 * width, 4 * width + ff_width, 4 * width + 2 * ff_width]
    return [mats[a:b] for a, b in zip(cuts[:-1], cuts[1:])]


def layer_forward(hidden, mats, vecs, attn_mask):
    tok, width = hidden.shape
    head_dim = width // H
    w_qkv, w_proj, w_fc, w_out = split_mats(mats, width)
    gain_one, shift_one, bias_q, bias_v, bias_proj, gain_two, shift_two, bias_fc, bias_out = (
        split_vecs(vecs, width)
    )
    normed_low = layer_norm(hidden, gain_one, shift_one).astype(jnp.bfloat16)
    bias_qkv = jnp.concatenate([bias_q, jnp.zeros_like(bias_q), bias_v])
    qkv_f = contract(normed_low, w_qkv, 1, 1) + bias_qkv
    qkv_low = qkv_f.astype(jnp.bfloat16).reshape(tok, 3, H, head_dim)
    scores = jnp.einsum(
        "thd,uhd->htu", qkv_low[:, 0], qkv_low[:, 1], preferred_element_type=jnp.float32
    ) * head_dim ** (-0.5)
    scores = jnp.where(attn_mask[None], scores, -1000000000.0)
    shifted = jnp.exp(scores - jnp.max(scores, -1, keepdims=True))
    attn_probs = shifted / jnp.sum(shifted, -1, keepdims=True)
    probs_low = attn_probs.astype(jnp.bfloat16)
    attended = jnp.einsum(
        "htu,uhd->thd", probs_low, qkv_low[:, 2], preferred_element_type=jnp.float32
    )
    attended = attended.reshape(tok, width).astype(jnp.bfloat16)
    middle = hidden + contract(attended, w_proj, 1, 1) + bias_proj
    two_low = layer_norm(middle, gain_two, shift_two).astype(jnp.bfloat16)
    up_act = contract(two_low, w_fc, 1, 1) + bias_fc
    activ_low = gelu_tanh(up_act).astype(jnp.bfloat16)
    output = middle + contract(activ_low, w_out, 1, 0) + bias_out
    saved = (
        hidden,
        normed_low,
        qkv_low,
        attn_probs,
        probs_low,
        attended,
        middle,
        two_low,
        up_act,
        activ_low,
    )
    return (output, saved)


def layer_backward(saved, mats, vecs, grad_out):
    hidden, normed_low, qkv_low, attn_probs, probs_low, attended, middle, two_low, up_act, activ_low = saved
    tok, width = hidden.shape
    head_dim = width // H
    w_qkv, w_proj, w_fc, w_out = split_mats(mats, width)
    gain_one, shift_one, bias_q, bias_v, bias_proj, gain_two, shift_two, bias_fc, bias_out = (
        split_vecs(vecs, width)
    )
    low = jnp.bfloat16
    out_low = grad_out.astype(low)
    grad_wout = contract(activ_low, out_low, 0, 0).astype(low)
    grad_bout = jnp.sum(grad_out, 0)
    grad_act = contract(out_low, w_out, 1, 1)
    unused_up, gelu_pull = jax.vjp(gelu_tanh, up_act)
    grad_up = gelu_pull(grad_act)[0]
    up_low = grad_up.astype(low)
    grad_wfc = contract(up_low, two_low, 0, 0).astype(low)
    grad_bfc = jnp.sum(grad_up, 0)
    grad_two = contract(up_low, w_fc, 1, 0)
    unused_two, norm_pull = jax.vjp(layer_norm, middle, gain_two, shift_two)
    grad_mid_norm, grad_g2, grad_s2 = norm_pull(grad_two)
    grad_mid = grad_out + grad_mid_norm
    mid_low = grad_mid.astype(low)
    grad_wproj = contract(mid_low, attended, 0, 0).astype(low)
    grad_bproj = jnp.sum(grad_mid, 0)
    grad_att = contract(mid_low, w_proj, 1, 0).astype(low).reshape(tok, H, head_dim)
    grad_probs = jnp.einsum(
        "thd,uhd->htu", grad_att, qkv_low[:, 2], preferred_element_type=jnp.float32
    )
    grad_vals = jnp.einsum("htu,thd->uhd", probs_low, grad_att, preferred_element_type=jnp.float32)
    grad_scores = attn_probs * (grad_probs - jnp.sum(attn_probs * grad_probs, -1, keepdims=True))
    score_low = (grad_scores * head_dim ** (-0.5)).astype(low)
    grad_q = jnp.einsum(
        "htu,uhd->thd", score_low, qkv_low[:, 1], preferred_element_type=jnp.float32
    )
    grad_k = jnp.einsum(
        "htu,thd->uhd", score_low, qkv_low[:, 0], preferred_element_type=jnp.float32
    )
    grad_qkv = jnp.stack([grad_q, grad_k, grad_vals], 1).reshape(tok, 3 * width)
    qkv_grad_low = grad_qkv.astype(low)
    grad_wqkv = contract(qkv_grad_low, normed_low, 0, 0).astype(low)
    grad_normed = contract(qkv_grad_low, w_qkv, 1, 0)
    unused_one, first_pull = jax.vjp(layer_norm, hidden, gain_one, shift_one)
    grad_in_norm, grad_g1, grad_s1 = first_pull(grad_normed)
    grad_in = grad_mid + grad_in_norm
    grad_mats = jnp.concatenate([grad_wqkv, grad_wproj, grad_wfc, grad_wout], 0)
    grad_vecs = jnp.concatenate(
        [
            grad_g1,
            grad_s1,
            jnp.sum(grad_q, 0).reshape(width),
            jnp.sum(grad_vals, 0).reshape(width),
            grad_bproj,
            grad_g2,
            grad_s2,
            grad_bfc,
            grad_bout,
        ]
    )
    return (grad_in, grad_mats, grad_vecs)


def renew(weight, moment, average, grad, factor):
    clipped = factor * grad
    moment_next = momentum_coef * moment + clipped
    weight_next = weight - learn_rate * (clipped + momentum_coef * moment_next)
    average_next = ema_decay * average + (1.0 - ema_decay) * weight_next
    return (moment_next, weight_next, average_next, weight_next.astype(jnp.bfloat16))


SMALL_ROWS, LANES = 16, 128


def pack_small(values):
    room = SMALL_ROWS * LANES - values.shape[-1]
    pads = [(0, 0)] * (values.ndim - 1) + [(0, room)]
    return jnp.pad(values, pads).reshape(values.shape[:-1] + (SMALL_ROWS, LANES))


def per_device(
    token_ids,
    targets,
    lengths,
    embed_table,
    embed_moment,
    embed_average,
    blocks,
    block_moment,
    block_average,
    pos_table,
    pos_moment,
    pos_average,
    vectors,
    vector_moment,
    vector_average,
):
    devices = lax.axis_size(("dp", "vocab"))
    vocab_count = lax.axis_size("vocab")
    dp_count = lax.axis_size("dp")
    vocab_at = lax.axis_index("vocab")
    data_at = lax.axis_index("dp")
    tok = token_ids.shape[0]
    own_rows, width = embed_table.shape
    layers = blocks.shape[0]
    capacity = max(2, 2 * tok // devices)
    low = jnp.bfloat16
    blocks, block_moment, block_average = (
        jnp.transpose(item, (0, 2, 1)) for item in (blocks, block_moment, block_average)
    )
    pos_rows, pos_cols = pos_table.shape
    vec_own = vectors.shape[0]
    table_low = embed_table.astype(low)
    pad_rows = -own_rows % 16
    table_padded = jnp.pad(table_low, ((0, pad_rows), (0, 0)))
    slot_rows = own_rows + pad_rows

    both_ids = jnp.stack([token_ids, targets])
    owners = both_ids // own_rows
    hits = owners[:, :, None] == jnp.arange(devices, dtype=jnp.int32)[None, None, :]
    tokens = jnp.arange(tok, dtype=jnp.int32)
    earlier = jnp.sum(
        (owners[:, :, None] == owners[:, None, :]) & (tokens[None, None, :] < tokens[None, :, None]), 2
    )
    slot_hot = hits[:, :, :, None] & (
        earlier[:, :, None, None] == jnp.arange(capacity, dtype=jnp.int32)[None, None, None, :]
    )
    send_rows = jnp.sum(
        jnp.where(slot_hot, (both_ids % own_rows)[:, :, None, None], 0), 1
    )
    slot_hot = slot_hot.reshape(2, tok, devices * capacity).astype(low)
    local_rows = lax.all_to_all(send_rows, ("dp", "vocab"), split_axis=1, concat_axis=1, tiled=True)
    asked = (
        local_rows.reshape(-1)[:, None] == jnp.arange(own_rows, dtype=jnp.int32)[None, :]
    ).astype(low)
    fetched = jnp.dot(asked, table_low, preferred_element_type=jnp.float32).astype(low)
    returned_rows = lax.all_to_all(
        fetched.reshape(2, devices, capacity, width),
        ("dp", "vocab"),
        split_axis=1,
        concat_axis=1,
        tiled=True,
    ).reshape(2, devices * capacity, width)

    small = pack_small(
        jnp.concatenate([jnp.transpose(pos_table).reshape(-1), vectors]).astype(low)
    )
    mats_all, small_all = gather_weights(blocks, small)
    small_all = small_all.reshape(devices, -1)
    pos_low_t = small_all[:, : pos_rows * pos_cols].reshape(width, pos_rows)
    vecs_all = (
        small_all[:, pos_rows * pos_cols : pos_rows * pos_cols + vec_own]
        .reshape(-1)
        .astype(jnp.float32)
    )
    vec_width = (vecs_all.shape[0] - 2 * width) // layers

    lens_group = lengths[0]
    seg_group, pos_group, weight_group = jax.vmap(
        partial(doc_info, tok_count=tok, total_docs=devices * lens_group.shape[1])
    )(lens_group)
    weight_group = weight_group * device_rise(data_at * vocab_count, vocab_count, devices)[:, None]
    seg_ids = lax.dynamic_index_in_dim(seg_group, vocab_at, 0, keepdims=False)
    pos_ids = lax.dynamic_index_in_dim(pos_group, vocab_at, 0, keepdims=False)
    own_weight = lax.dynamic_index_in_dim(weight_group, vocab_at, 0, keepdims=False)
    places = jnp.arange(tok, dtype=jnp.int32)
    attn_mask = (seg_ids[:, None] == seg_ids[None, :]) & (places[None, :] <= places[:, None])

    gotten = jnp.einsum(
        "ktr,krd->ktd", slot_hot, returned_rows, preferred_element_type=jnp.float32
    )
    pos_hot = (pos_ids[:, None] == jnp.arange(pos_rows, dtype=jnp.int32)[None, :]).astype(low)
    hidden = gotten[0] + contract(pos_hot, pos_low_t, 1, 1)
    kept = []
    for layer in range(layers):
        hidden, saved = layer_forward(
            hidden,
            mats_all[layer],
            vecs_all[layer * vec_width : (layer + 1) * vec_width],
            attn_mask,
        )
        kept.append(saved)
    tail = vecs_all[layers * vec_width :]
    final_low = layer_norm(hidden, tail[:width], tail[width:]).astype(low)
    group_rows = lax.all_gather(final_low, "vocab", axis=0, tiled=True)
    table_blocks = lax.all_gather(table_padded, "dp", axis=0)
    group_weight = weight_group.reshape(-1)
    group_count = group_rows.shape[0]
    real = jnp.arange(slot_rows, dtype=jnp.int32) < own_rows

    def forward_block(carry, piece):
        top, total = carry
        logits = jnp.where(real[None, :], contract(group_rows, piece, 1, 1), -1e30)
        new_top = jnp.maximum(top, jnp.max(logits, 1))
        total = total * jnp.exp(top - new_top) + jnp.sum(jnp.exp(logits - new_top[:, None]), 1)
        return ((new_top, total), None)

    start_top = jnp.full((group_count,), -1e30, jnp.float32)
    (row_top, row_total), unused = lax.scan(
        forward_block, (start_top, jnp.zeros((group_count,), jnp.float32)), table_blocks
    )
    tops, totals = lax.all_gather(jnp.stack([row_top, row_total]), "vocab", axis=1)
    peak = jnp.max(tops, 0)
    group_lse = peak + jnp.log(jnp.sum(totals * jnp.exp(tops - peak[None]), 0))
    own_lse = lax.dynamic_slice_in_dim(group_lse, vocab_at * tok, tok)
    target_rows = gotten[1]
    final_f = final_low.astype(jnp.float32)
    loss_part = jnp.sum(own_weight * (own_lse - jnp.sum(final_f * target_rows, 1)))

    def backward_block(acc, piece):
        logits = jnp.where(real[None, :], contract(group_rows, piece, 1, 1), -1e30)
        grad_low = (group_weight[:, None] * jnp.exp(logits - group_lse[:, None])).astype(low)
        return (
            acc + jnp.dot(grad_low, piece, preferred_element_type=jnp.float32),
            contract(grad_low, group_rows, 0, 0).astype(low),
        )

    group_grad, term = lax.scan(
        backward_block, jnp.zeros((group_count, width), jnp.float32), table_blocks
    )
    own_grad = lax.psum_scatter(
        group_grad.astype(low), "vocab", scatter_dimension=0, tiled=True
    ).astype(jnp.float32)
    table_grad = lax.psum_scatter(
        term.reshape(slot_rows * dp_count, width), "dp", scatter_dimension=0, tiled=True
    )[:own_rows].astype(jnp.float32)
    grad_final = own_grad - own_weight[:, None] * target_rows
    target_grad = -own_weight[:, None] * final_f
    unused_final, final_pull = jax.vjp(layer_norm, hidden, tail[:width], tail[width:])
    grad_hidden, grad_gf, grad_sf = final_pull(grad_final)
    mats_parts = [None] * layers
    vec_parts = [None] * layers
    for layer in reversed(range(layers)):
        grad_hidden, mats_parts[layer], vec_parts[layer] = layer_backward(
            kept[layer],
            mats_all[layer],
            vecs_all[layer * vec_width : (layer + 1) * vec_width],
            grad_hidden,
        )
    grad_vec_all = jnp.concatenate(vec_parts + [grad_gf, grad_sf])
    grad_pos = lax.dot_general(
        grad_hidden,
        pos_hot.astype(jnp.float32),
        (((0,), (0,)), ((), ())),
        precision=lax.Precision.HIGHEST,
    )
    send_grads = jnp.einsum(
        "ktr,ktd->krd",
        slot_hot,
        jnp.stack([grad_hidden, target_grad]).astype(low),
        preferred_element_type=jnp.float32,
    ).astype(low)
    back_grads = lax.all_to_all(
        send_grads.reshape(2, devices, capacity, width),
        ("dp", "vocab"),
        split_axis=1,
        concat_axis=1,
        tiled=True,
    ).reshape(-1, width)
    small_grads = pack_small(
        jnp.concatenate(
            [grad_pos.reshape(devices, -1), grad_vec_all.reshape(devices, -1)], 1
        )
    )
    mats_shard, small_shard = reduce_weights(mats_parts[0], mats_parts[1], small_grads)
    small_shard = small_shard.reshape(-1)
    pos_shard = small_shard[: pos_rows * pos_cols].reshape(pos_cols, pos_rows)
    vec_shard = small_shard[pos_rows * pos_cols : pos_rows * pos_cols + vec_own]
    table_grad = table_grad + contract(asked, back_grads, 0, 0)
    local_squares = (
        jnp.sum(table_grad * table_grad)
        + jnp.sum(mats_shard * mats_shard)
        + jnp.sum(pos_shard * pos_shard)
        + jnp.sum(vec_shard * vec_shard)
    )
    both_sums = sum_all(
        jnp.broadcast_to(jnp.pad(jnp.stack([loss_part, local_squares]), (0, 6))[:, None], (8, LANES))
    )
    loss_sum, squares = both_sums[0, 0], both_sums[1, 0]
    grad_norm = jnp.sqrt(squares)
    factor = clip_bound / jnp.maximum(grad_norm, clip_bound)
    embed_out = renew(embed_table, embed_moment, embed_average, table_grad, factor)
    block_out = renew(blocks, block_moment, block_average, mats_shard, factor)
    block_out = tuple(jnp.transpose(item, (0, 2, 1)) for item in block_out)
    pos_out = renew(
        jnp.transpose(pos_table),
        jnp.transpose(pos_moment),
        jnp.transpose(pos_average),
        pos_shard,
        factor,
    )
    pos_out = tuple(jnp.transpose(item) for item in pos_out)
    vector_out = renew(vectors, vector_moment, vector_average, vec_shard, factor)
    return (loss_sum, grad_norm) + embed_out + block_out + pos_out + vector_out


def solution(mesh):
    table = P(("dp", "vocab"), None)
    cols = P(None, None, ("dp", "vocab"))
    pos = P(None, ("dp", "vocab"))
    vec = P(("dp", "vocab"))
    return jax.shard_map(
        per_device,
        mesh=mesh,
        in_specs=(vec, vec, P("dp", None, None))
        + (table,) * 3
        + (cols,) * 3
        + (pos,) * 3
        + (vec,) * 3,
        out_specs=(P(), P()) + (table,) * 4 + (cols,) * 4 + (pos,) * 4 + (vec,) * 4,
        check_vma=False,
    )
```

time: 1280 us -> 885 us (0.69)
  blocking collectives: 329 us -> 13.1 us
  Pallas kernels: 0 us -> 167 us
  waiting for transfers between devices: 290 us -> 134 us
  local copies, waits for them, and re-layouts: 210 us -> 60.8 us
  other arithmetic: 123 us -> 156 us
  matrix products: 263 us -> 283 us
    unnamed x9 -> x4, waiting for transfers between devices: 221 us -> 0.07 us
    unnamed x2 -> x0, blocking collectives: 200 us -> none
    pallas_call x0 -> x3, Pallas kernels: none -> 167 us  [the longest x1 79.3 us: reduce_weights(): pl.pallas_call(reduce_kernel, out_shape=(jax.ShapeDtypeStruct((2, rows //...]
    concatenate x1 -> x2, other arithmetic: 0.02 us -> 85.3 us  [layer_backward(): grad_mats = jnp.concatenate([grad_wqkv, grad_wproj, grad_wfc, grad_wout], 0)]
    all_gather x2 -> x1, waiting for transfers between devices: 0.04 us -> 80.5 us  [per_device(): table_blocks = lax.all_gather(table_padded, 'dp', axis=0)]
    psum x2 -> x0, blocking collectives: 78.8 us -> none  [the longest x1 66.2 us: per_device(): loss_sum, squares = lax.psum((loss_part, local_squares), ('dp', 'vocab'))]
    another operation x3 -> x4, local copies, waits for them, and re-layouts: 81.8 us -> 3.54 us  [the longest x3 3.53 us: per_device(): tops, totals = lax.all_gather(jnp.stack([row_top, row_total]), 'vocab', a...]
    another operation x9 -> x6, other arithmetic: 78.3 us -> 3.11 us  [the longest x3 75.9 us: per_device(): jnp.stack(mats_parts)]
  transfers between devices with their start and end apart: 10 -> 7, of which waited for: 5 -> 4; matrix products, arithmetic and copies ran while one was open for 34% -> 21% of each run, Pallas kernels for 0% -> 18%
where the time goes in v1:
time: 885 us; the launch traced here: 870 us
  matrix products  283 us (32%)
  Pallas kernels  167 us (19%)
  other arithmetic  156 us (18%)
  waiting for transfers between devices  134 us (15%)
  local copies, waits for them, and re-layouts  60.8 us (7%)
  starting transfers between devices  34.3 us (4%)
  between operations  21.1 us (2%)
  blocking collectives  13.1 us (1%)
    dot_general x74, matrix products, contract(): lax.dot_general(left, right, (((left_dim,), (right_dim,)), ((), ())), pre...  201 us
    concatenate x2, other arithmetic, layer_backward(): grad_mats = jnp.concatenate([grad_wqkv, grad_wproj, grad_wfc, grad_wout], 0)  85.3 us
    all_gather x1, waiting for transfers between devices, per_device(): table_blocks = lax.all_gather(table_padded, 'dp', axis=0)  80.5 us
    pallas_call x1, Pallas kernels, reduce_weights(): pl.pallas_call(reduce_kernel, out_shape=(jax.ShapeDtypeStruct((2, rows //...  79.3 us
    pallas_call x1, Pallas kernels, gather_weights(): pl.pallas_call(gather_kernel, out_shape=(whole, whole, jax.ShapeDtypeStru...  73.3 us
    dot_general x16, matrix products, backward_block(): jnp.dot(grad_low, piece, preferred_element_type=jnp.float32)  53.6 us
    reduce_sum x16, other arithmetic, forward_block(): jnp.sum(jnp.exp(logits - new_top[:, None]), 1)  28.5 us
    reduce_scatter x1, waiting for transfers between devices, per_device(): lax.psum_scatter(group_grad.astype(low), 'vocab', scatter_dimension=0, ti...  22.9 us
  transfers between devices with their start and end apart: 7, of which 4 were waited for; matrix products, arithmetic and copies ran while one was open for 21% of the time, Pallas kernels for 18%

profile of v1, /device:TPU:0, one launch (start us, length us, event | category | flops | bytes accessed | tf_op | source)
XLA Modules:
  0.0 870.1 jit_solution(17998665960109893602)
XLA Ops:
  8.1 4.4 select_reduce_fusion.1
  13.2 11.7 %all-to-all-start = ((s32[2,128,2]{2,0,1:T(2,128)}), s32[2,128,2]{2,0,1:T(2,128)}, u32[]{:S(2)}, u32[]{:S(2)}) async-start(s32[2,128,2]{2,0,1:T(2,128)} %copy.138), calls=%async_computation | async-start | bytes 262144 | tf_op jit(solution)/shard_map/all_to_all | solution.py:813
  29.0 73.3 %gather_weights.1 = (bf16[4,4,4,144,768]{4,3,2,1,0:T(8,128)(2,1)S(1)}, bf16[4,4,4,144,768]{4,3,2,1,0:T(8,128)(2,1)S(1)}, bf16[4,4,4,2,16,128]{5,4,3,2,1,0:T(8,128)(2,1)S(1)}) custom-call(f32[2,72,768]{2,1,0:T(8,128)S(1)} %bitcast.318, bf16[16,128]{1,0:T(8,128)(2,1)S(1)} %fusion.146.small_ref), custom_call_target="tpu_custom_call" | custom-call | tf_op jit(solution)/shard_map/gather_weights/pallas_call | solution.py:200
  102.3 5.0 copy-done
  107.3 5.1 copy-done.1
  119.6 5.3 slice.201
  135.6 5.9 all-to-all-start.1
  146.7 10.7 %all-to-all-done.1 = bf16[2,128,2,768]{3,2,0,1:T(2,128)(2,1)} async-done(((bf16[2,128,2,768]{3,2,0,1:T(2,128)(2,1)}), bf16[2,128,2,768]{3,2,0,1:T(2,128)(2,1)}, u32[]{:S(2)}, u32[]{:S(2)}) %all-to-all-start.1) | async-done | bytes 786464 | tf_op jit(solution)/shard_map/all_to_all | solution.py:818
  202.8 19.5 %all-gather.5.cloned.1.call-done = bf16[1024,768]{1,0:T(8,128)(2,1)} async-done(((bf16[128,768]{1,0:T(8,128)(2,1)}), bf16[1024,768]{1,0:T(8,128)(2,1)}) %all-gather.5.cloned.1.call-update) | async-done | bytes 1572880 | tf_op jit(solution)/shard_map/all_gather | solution.py:866
  222.3 80.5 %all-gather.7.cloned.1.call-done = bf16[6400,768]{1,0:T(8,128)(2,1)} async-done(((bf16[400,768]{1,0:T(8,128)(2,1)}), bf16[6400,768]{1,0:T(8,128)(2,1)}) %all-gather.7.cloned.1.call-update) | async-done | bytes 9830416 | tf_op jit(solution)/shard_map/all_gather | solution.py:867
  302.8 87.5 %while.26 = (s32[]{:T(128)}, f32[1024]{0:T(1024)S(1)}, f32[1024]{0:T(1024)S(1)}, bf16[16,400,768]{2,1,0:T(8,128)(2,1)}, bf16[1024,768]{1,0:T(8,128)(2,1)}, /*index=5*/s32[]{:T(128)}, s32[]{:T(128)}) while((s32[]{:T(128)}, f32[1024]{0:T(1024)S(1)}, f32[1024]{0:T(1024)S(1)}, bf16[16,400,768]{2,1,0:T(8,128)(2,1)}, ...), condition=%wide.region_23.24_spmd.clone, body=%wide.region_20.23_spmd.clone.sunk | while | flops 631199104 | bytes 5520240 | solution.py:880
  390.4 13.1 %all-gather.1 = f32[2,8192]{1,0:T(2,128)S(1)} all-gather(f32[2,1024]{1,0:T(2,128)S(1)} %pad_maximum_fusion.4), channel_id=3, replica_groups=mesh['dp'=16,'vocab'=8] {'vocab'}, dimensions={1}, use_global_device_ids=true | all-gather | bytes 73728 | tf_op jit(solution)/shard_map/all_gather | solution.py:883
  408.6 133.9 %while.27 = (s32[]{:T(128)}, f32[1024,768]{1,0:T(8,128)S(1)}, bf16[16,400,768]{2,1,0:T(8,128)(2,1)}, f32[8,128]{1,0:T(8,128)}, bf16[16,400,768]{2,1,0:T(8,128)(2...) while((s32[]{:T(128)}, f32[1024,768]{1,0:T(8,128)S(1)}, ...), condition=%wide.region_29.30_spmd.clone, body=%wide.region_28.29_spmd.clone.sunk | while | flops 1890955648 | bytes 23315412 | solution.py:899
  543.8 8.8 %reduce-scatter.3.cloned.1.call-start = ((), (), s32[]{:S(2)}) async-start(), calls=%async_computation.6 | async-start | bytes 10444800 | tf_op jit(solution)/shard_map/reduce_scatter | solution.py:905
  552.7 22.9 %reduce-scatter.5.cloned.1.call-done = bf16[128,768]{1,0:T(8,128)(2,1)} async-done(((bf16[1024,768]{1,0:T(8,128)(2,1)}), bf16[128,768]{1,0:T(8,128)(2,1)}) %reduce-scatter.5.cloned.1.call-update) | async-done | bytes 196624 | tf_op jit(solution)/shard_map/reduce_scatter | solution.py:902
  578.8 5.0 fusion.203
  583.8 4.1 multiply_reduce_fusion.5
  606.3 5.0 fusion.200
  611.3 4.2 multiply_reduce_fusion.7
  635.7 7.6 all-to-all-start.2
  654.5 42.8 %pad_maximum_fusion = bf16[9216,768]{1,0:T(8,128)(2,1)} fusion(bf16[3072,768]{1,0:T(8,128)(2,1)S(1)} %convolution_convert_fusion.4, bf16[3072,768]{1,0:T(8,128)(2,1)S(1)} %convolution_convert_fusion.5, bf16[768,768]{1,0:T(8,128)(2,1)S(1)} %convolution_convert_fusion.8, bf16[2304,768]{1,0:T(8,128)(2,1)S(1)} %convolution_convert_fusion.6), kind=kLoop, calls=%fused_computation.28 | loop fusion | flops 56623104 | bytes 28311552 | tf_op jit(solution)/shard_map/concatenate | solution.py:728
  697.3 42.5 %pad_maximum_fusion.1 = bf16[9216,768]{1,0:T(8,128)(2,1)} fusion(bf16[3072,768]{1,0:T(8,128)(2,1)S(1)} %convolution_convert_fusion.1, bf16[3072,768]{1,0:T(8,128)(2,1)S(1)} %convolution_convert_fusion.2, bf16[768,768]{1,0:T(8,128)(2,1)S(1)} %convolution_convert_fusion.7, bf16[2304,768]{1,0:T(8,128)(2,1)S(1)} %convolution_convert_fusion.3), kind=kLoop, calls=%fused_computation.29 | loop fusion | flops 56623104 | bytes 28311552 | tf_op jit(solution)/shard_map/concatenate | solution.py:728
  741.9 79.3 %reduce_weights.1 = (f32[2,72,768]{2,1,0:T(8,128)}, f32[16,128]{1,0:T(8,128)}) custom-call(bf16[4,4,4,144,768]{4,3,2,1,0:T(8,128)(2,1)} %bitcast.320, bf16[4,4,4,144,768]{4,3,2,1,0:T(8,128)(2,1)} %bitcast.321, f32[4,4,4,2,16,128]{5,4,3,2,1,0:T(8,128)} %bitcast.331), custom_call_target="tpu_custom_call" | custom-call | tf_op jit(solution)/shard_map/reduce_weights/pallas_call | solution.py:504
  835.4 14.4 %sum_all.1 = f32[8,128]{1,0:T(8,128)} custom-call(f32[8,128]{1,0:T(8,128)} %broadcast_in_dim.125.in_ref), custom_call_target="tpu_custom_call" | custom-call | tf_op jit(solution)/shard_map/sum_all/pallas_call | solution.py:579
  (806 shorter events, 376.7 us)
Async XLA Ops:
  13.2 111.7 %all-to-all-start = ((s32[2,128,2]{2,0,1:T(2,128)}), s32[2,128,2]{2,0,1:T(2,128)}, u32[]{:S(2)}, u32[]{:S(2)}) async-start(s32[2,128,2]{2,0,1:T(2,128)} %copy.138), calls=%async_computation | async-start | bytes 262144 | tf_op jit(solution)/shard_map/all_to_all | solution.py:813
  29.0 87.5 %copy-start.34 = (f32[393,768]{1,0:T(8,128)S(1)}, f32[393,768]{1,0:T(8,128)}, u32[]{:S(2)}) copy-start(f32[393,768]{1,0:T(8,128)} %param.22) | copy-start | bytes 3621892
  119.6 47.0 %copy-start.4 = (bf16[1,4,4,144,768]{4,3,2,1,0:T(8,128)(2,1)}, bf16[1,4,4,144,768]{4,3,2,1,0:T(8,128)(2,1)S(1)}, u32[]{:S(2)}) copy-start(bf16[1,4,4,144,768]{4,3,2,1,0:T(8,128)(2,1)S(1)} %slice.184) | copy-start | bytes 10616836
  135.6 21.9 %all-to-all-start.1 = ((bf16[2,128,2,768]{3,2,0,1:T(2,128)(2,1)}), bf16[2,128,2,768]{3,2,0,1:T(2,128)(2,1)}, u32[]{:S(2)}, u32[]{:S(2)}) async-start(bf16[2,128,2,768]{3,2,0,1:T(2,128)(2,1)} %copy.140), calls=%async_computation.1 | async-start | bytes 1572864 | tf_op jit(solution)/shard_map/all_to_all | solution.py:818
  141.5 80.8 %all-gather.5.cloned.1.call-start = ((), (), s32[]{:S(2)}) async-start(), calls=%async_computation.5 | async-start | bytes 1769472 | tf_op jit(solution)/shard_map/all_gather | solution.py:866
  143.3 23.3 %copy-start.72 = (f32[768]{0:T(1024)}, f32[768]{0:T(1024)S(1)}, u32[]{:S(2)}) copy-start(f32[768]{0:T(1024)S(1)} %get-tuple-element.251) | copy-start | bytes 9220
  143.3 48.6 %copy-start.79 = (f32[768]{0:T(1024)}, f32[768]{0:T(1024)S(1)}, u32[]{:S(2)}) copy-start(f32[768]{0:T(1024)S(1)} %get-tuple-element.234) | copy-start | bytes 9220
  143.3 57.0 %copy-start.75 = (f32[768]{0:T(1024)}, f32[768]{0:T(1024)S(1)}, u32[]{:S(2)}) copy-start(f32[768]{0:T(1024)S(1)} %get-tuple-element.236) | copy-start | bytes 9220
  191.1 396.9 %copy-start.22 = (f32[128,768]{1,0:T(8,128)}, f32[128,768]{1,0:T(8,128)S(1)}, u32[]{:S(2)}) copy-start(f32[128,768]{1,0:T(8,128)S(1)} %get-tuple-element.272) | copy-start | bytes 1179652
  201.7 101.1 %all-gather.7.cloned.1.call-start = ((), (), s32[]{:S(2)}) async-start(), calls=%async_computation.8 | async-start | bytes 10444800 | tf_op jit(solution)/shard_map/all_gather | solution.py:867
  202.7 372.9 %reduce-scatter.5.cloned.1.call-start = ((), (), s32[]{:S(2)}) async-start(), calls=%async_computation.7 | async-start | bytes 1769472 | tf_op jit(solution)/shard_map/reduce_scatter | solution.py:902
  543.8 284.1 %reduce-scatter.3.cloned.1.call-start = ((), (), s32[]{:S(2)}) async-start(), calls=%async_computation.6 | async-start | bytes 10444800 | tf_op jit(solution)/shard_map/reduce_scatter | solution.py:905
  552.6 23.0 %copy-start.28 = (f32[128,768]{1,0:T(8,128)S(1)}, f32[128,768]{1,0:T(8,128)}, u32[]{:S(2)}) copy-start(f32[128,768]{1,0:T(8,128)} %copy-done.27) | copy-start | bytes 1179652
  552.6 23.0 %copy-start.37 = (f32[2,128,768]{2,1,0:T(8,128)S(1)}, f32[2,128,768]{2,1,0:T(8,128)}, u32[]{:S(2)}) copy-start(f32[2,128,768]{2,1,0:T(8,128)} %copy-done.36) | copy-start | bytes 2359300
  552.6 24.8 %copy-start.177 = (f32[128]{0:T(128)S(1)}, f32[128]{0:T(128)}, u32[]{:S(2)}) copy-start(f32[128]{0:T(128)} %copy-done.176) | copy-start | bytes 1540
  552.7 26.1 %copy-start.42 = (f32[128,3072]{1,0:T(8,128)S(1)}, f32[128,3072]{1,0:T(8,128)}, u32[]{:S(2)}) copy-start(f32[128,3072]{1,0:T(8,128)} %copy-done.41) | copy-start | bytes 4718596
  635.7 191.2 %all-to-all-start.2 = ((bf16[2,128,2,768]{3,2,0,1:T(2,128)(2,1)}), bf16[2,128,2,768]{3,2,0,1:T(2,128)(2,1)S(1)}, u32[]{:S(2)}, u32[]{:S(2)}) async-start(bf16[2,128,2,768]{3,2,0,1:T(2,128)(2,1)} %copy.155), calls=%async_computation.4 | async-start | bytes 1572864 | tf_op jit(solution)/shard_map/all_to_all | solution.py:934
  697.3 42.5 %copy-start.143 = (s32[128]{0:T(128)S(1)}, s32[128]{0:T(128)}, u32[]{:S(2)}) copy-start(s32[128]{0:T(128)} %get-tuple-element.293) | copy-start | bytes 1540
  741.9 79.3 %copy-start.119 = (f32[128]{0:T(128)S(1)}, f32[128]{0:T(128)}, u32[]{:S(2)}) copy-start(f32[128]{0:T(128)} %get-tuple-element.227) | copy-start | bytes 1540
  741.9 79.3 %copy-start.163 = (f32[128]{0:T(128)S(1)}, f32[128]{0:T(128)}, u32[]{:S(2)}) copy-start(f32[128]{0:T(128)} %get-tuple-element.165) | copy-start | bytes 1540
  827.8 24.7 %copy-start.3 = (f32[2,768,72]{1,2,0:T(8,128)S(1)}, f32[2,768,72]{1,2,0:T(8,128)}, u32[]{:S(2)}) copy-start(f32[2,768,72]{1,2,0:T(8,128)} %param.25) | copy-start | bytes 1327108
  827.8 24.6 %copy-start.54 = (f32[2,72,768]{2,1,0:T(8,128)S(1)}, f32[2,72,768]{2,1,0:T(8,128)}, u32[]{:S(2)}) copy-start(f32[2,72,768]{2,1,0:T(8,128)} %get-tuple-element.106) | copy-start | bytes 1327108
  827.8 24.6 %copy-start.71 = (f32[2,768,72]{1,2,0:T(8,128)S(1)}, f32[2,768,72]{1,2,0:T(8,128)}, u32[]{:S(2)}) copy-start(f32[2,768,72]{1,2,0:T(8,128)} %param.26) | copy-start | bytes 1327108
  831.3 23.5 %copy-start.35 = (f32[393,768]{1,0:T(8,128)S(1)}, f32[393,768]{1,0:T(8,128)}, u32[]{:S(2)}) copy-start(f32[393,768]{1,0:T(8,128)} %param.22) | copy-start | bytes 3621892
  (211 other events, 941.9 us)
Sparse Core Ops, SparseCore 0:
  201.8 20.3 all-gather.4
  225.0 77.7 all-gather.6
  543.9 31.6 reduce-scatter.4
  578.9 90.5 reduce-scatter.2

commit v2 on v1

--- a/solution.py
+++ b/solution.py
@@ -214,7 +214,7 @@
             pltpu.SemaphoreType.DMA((3,)),
         ],
         compiler_params=pltpu.CompilerParams(
-            collective_id=0, has_side_effects=True, vmem_limit_bytes=24 * 2**20
+            collective_id=0, has_side_effects=True, vmem_limit_bytes=58 * 2**20
         ),
         name="gather_weights",
     )(mine, small)
@@ -534,6 +534,7 @@
         compiler_params=pltpu.CompilerParams(
             collective_id=1, has_side_effects=True, vmem_limit_bytes=58 * 2**20
         ),
+        cost_estimate=pl.CostEstimate(flops=0, bytes_accessed=280 * 10**6, transcendentals=0),
         name="reduce_weights",
     )(
         first.reshape(torus + (rows, width)),
@@ -591,6 +592,320 @@
     )(value)
 
 
+TILE = 800
+
+
+def head_kernel(
+    f_ref,
+    code_ref,
+    weight_ref,
+    table_ref,
+    grad_out,
+    dtable_ref,
+    loss_ref,
+    f_all,
+    codes,
+    table,
+    logits,
+    probs,
+    tops,
+    stats,
+    df,
+    df_send,
+    df_sib,
+    ring,
+    ring_half,
+    ring_full,
+    staged,
+    send,
+    recv,
+    load,
+    store,
+):
+    at, core = place()
+    x = at[2]
+    dp, vocab = lax.axis_index("dp"), lax.axis_index("vocab")
+    tok, width = f_ref.shape
+    group = f_all.shape[0]
+    members = group // tok
+    tiles = table.shape[0] // TILE
+    low, f32 = jnp.bfloat16, jnp.float32
+
+    def tile_rows(t):
+        return pl.ds(pl.multiple_of(t * TILE, TILE), TILE)
+
+    loads = []
+    for t in range(tiles):
+        op = pltpu.make_async_copy(
+            table_ref.at[pl.ds(t * TILE, TILE)], table.at[pl.ds(t * TILE, TILE)], load.at[t]
+        )
+        op.start()
+        loads.append(op)
+
+    peers = [(dp, lax.rem(vocab + by, members)) for by in range(1, members)]
+    greet(peers)
+    wires = Wires(send, recv)
+    sibling = device_at(at, 1 - core)
+    right, left = device_at(moved(at, 2, 1), core), device_at(moved(at, 2, 3), core)
+    before, after, across = lax.rem(x + 3, RING), lax.rem(x + 1, RING), lax.rem(x + 2, RING)
+
+    def rows_of(at_x, piece=None):
+        first = (at_x * 2 + core) * tok
+        if piece is None:
+            return f_all.at[pl.ds(pl.multiple_of(first, tok), tok)]
+        half = tok // 2
+        return f_all.at[pl.ds(pl.multiple_of(first + piece * half, half), half)]
+
+    f_all[pl.ds(pl.multiple_of(vocab * tok, tok), tok), :] = f_ref[...]
+    own = rows_of(x)
+    one, two = wires.copy(own, own, right), wires.copy(own, own, left)
+    pending = [wires.copy(own, own, sibling)]
+    codes[vocab] = code_ref[...]
+    for peer in peers:
+        pending.append(wires.copy(codes.at[vocab], codes.at[vocab], peer))
+    one.wait_recv()
+    one_on = wires.copy(rows_of(before, 0), rows_of(before, 0), right)
+    pending.append(wires.copy(rows_of(before), rows_of(before), sibling))
+    two.wait_recv()
+    two_on = wires.copy(rows_of(after, 1), rows_of(after, 1), left)
+    pending.append(wires.copy(rows_of(after), rows_of(after), sibling))
+    one_on.wait_recv()
+    pending.append(wires.copy(rows_of(across, 0), rows_of(across, 0), sibling))
+    two_on.wait_recv()
+    pending.append(wires.copy(rows_of(across, 1), rows_of(across, 1), sibling))
+    for op in pending:
+        op.wait_recv()
+
+    code_row = jnp.concatenate([codes[m, 0:1, :] for m in range(members)], 1) - vocab * table.shape[0]
+    code8 = jnp.broadcast_to(code_row, (8, group))
+    code16 = jnp.broadcast_to(code_row, (16, group))
+    rows8 = lax.broadcasted_iota(jnp.int32, (8, group), 0)
+    rows16 = lax.broadcasted_iota(jnp.int32, (16, group), 0)
+    slot = TILE // 2
+    real = slot - 7
+    steps8, steps16 = 5, 5
+
+    def first_pass(t, carry):
+        top, total, target = carry
+        here = tile_rows(t)
+        logits[...] = lax.dot_general(
+            table[here, :], f_all[...], (((1,), (1,)), ((), ())), preferred_element_type=f32
+        )
+        for part in range(2):
+            last = pl.ds((part + 1) * slot - 8, 8)
+            logits[last, :] = jnp.where(rows8 < 1, logits[last, :], -1e30)
+
+        def look(i, state):
+            high, hit = state
+            for u in range(steps8):
+                first = (i * steps8 + u) * 8
+                value = logits[pl.ds(pl.multiple_of(first, 8), 8), :]
+                high = jnp.maximum(high, value)
+                hit = hit + jnp.where(rows8 + (first + t * TILE) == code8, value, 0.0)
+            return high, hit
+
+        high, hit = lax.fori_loop(
+            0,
+            TILE // (8 * steps8),
+            look,
+            (jnp.full((8, group), -1e30, f32), jnp.zeros((8, group), f32)),
+        )
+        top_next = jnp.maximum(top, jnp.max(high, 0, keepdims=True))
+        target = target + jnp.sum(hit, 0, keepdims=True)
+
+        def lift(i, acc):
+            for u in range(steps16):
+                first = (i * steps16 + u) * 16
+                value = jnp.exp(logits[pl.ds(pl.multiple_of(first, 16), 16), :] - top_next)
+                acc = acc + value
+                probs[pl.ds(pl.multiple_of(t * TILE + first, 16), 16), :] = value.astype(low)
+            return acc
+
+        acc = lax.fori_loop(
+            0, TILE // (16 * steps16), lift, jnp.zeros((16, group), f32)
+        )
+        total = total * jnp.exp(top - top_next) + jnp.sum(acc, 0, keepdims=True)
+        tops[t] = top_next
+        return top_next, total, target
+
+    for op in loads:
+        op.wait()
+    start = (jnp.full((1, group), -1e30, f32), jnp.zeros((1, group), f32), jnp.zeros((1, group), f32))
+    found = lax.fori_loop(0, tiles, first_pass, start)
+    for k in range(3):
+        for m in range(members):
+            stats[vocab, k, m : m + 1, :] = found[k][:, m * tok : (m + 1) * tok]
+    pending = [wires.copy(stats.at[vocab], stats.at[vocab], peer) for peer in peers]
+    for op in pending:
+        op.wait_recv()
+    peak = stats[0, 0]
+    for m in range(1, members):
+        peak = jnp.maximum(peak, stats[m, 0])
+    total, target = jnp.zeros_like(peak), jnp.zeros_like(peak)
+    for m in range(members):
+        total = total + stats[m, 1] * jnp.exp(stats[m, 0] - peak)
+        target = target + stats[m, 2]
+    lse = peak + jnp.log(total)
+    weight = weight_ref[...]
+    mine = lax.broadcasted_iota(jnp.int32, (members, tok), 0) == vocab
+    loss_ref[...] = jnp.where(mine, weight * (lse - target), 0.0)
+    lse_row = jnp.concatenate([lse[m : m + 1, :] for m in range(members)], 1)
+    weight_row = jnp.concatenate([weight[m : m + 1, :] for m in range(members)], 1)
+
+    df[...] = jnp.zeros_like(df)
+
+    def second_pass(t, unused):
+        scale = weight_row * jnp.exp(tops[t] - lse_row)
+
+        def turn(i, unused):
+            for u in range(steps16):
+                first = t * TILE + (i * steps16 + u) * 16
+                here = pl.ds(pl.multiple_of(first, 16), 16)
+                value = probs[here, :].astype(f32) * scale
+                value = value - jnp.where(rows16 + first == code16, weight_row, 0.0)
+                probs[here, :] = value.astype(low)
+            return unused
+
+        lax.fori_loop(0, TILE // (16 * steps16), turn, 0)
+        here = tile_rows(t)
+        df[...] += lax.dot_general(
+            probs[here, :], table[here, :], (((0,), (0,)), ((), ())), preferred_element_type=f32
+        )
+        return unused
+
+    lax.fori_loop(0, tiles, second_pass, 0)
+
+    def third_pass(t):
+        if t >= 2:
+            stores[t - 2].wait()
+        staged[t % 2] = jnp.dot(
+            probs[t * TILE : (t + 1) * TILE, :], f_all[...], preferred_element_type=f32
+        ).astype(low)
+        op = pltpu.make_async_copy(
+            staged.at[t % 2], dtable_ref.at[pl.ds(t * TILE, TILE)], store.at[t]
+        )
+        op.start()
+        stores.append(op)
+
+    stores = []
+    for m in range(members):
+        df_send[m % 2, m // 2] = df[m * tok : (m + 1) * tok, :].astype(low)
+    swap = wires.copy(df_send.at[1 - core], df_sib, sibling)
+    third_pass(0)
+    third_pass(1)
+    swap.wait_recv()
+    for k in range(RING):
+        first = pl.multiple_of((2 * k + core) * tok, tok)
+        ring[k] = (df[pl.ds(first, tok), :] + df_sib[k].astype(f32)).astype(low)
+    half = tok // 2
+    one = wires.copy(ring.at[across, pl.ds(0, half)], ring_half.at[0], right)
+    two = wires.copy(ring.at[across, pl.ds(half, half)], ring_half.at[1], left)
+    third_pass(2)
+    third_pass(3)
+    one.wait_recv()
+    ring[after, :half] = (ring[after, :half].astype(f32) + ring_half[0].astype(f32)).astype(low)
+    one = wires.copy(ring.at[after], ring_full.at[0], right)
+    two.wait_recv()
+    ring[before, half:] = (ring[before, half:].astype(f32) + ring_half[1].astype(f32)).astype(low)
+    two = wires.copy(ring.at[before], ring_full.at[1], left)
+    for t in range(4, tiles):
+        third_pass(t)
+    one.wait_recv()
+    two.wait_recv()
+    grad_out[...] = ring[x].astype(f32) + ring_full[0].astype(f32) + ring_full[1].astype(f32)
+    for op in stores[-2:]:
+        op.wait()
+    wires.drain()
+
+
+HEAD_COPIES = 9 + 7 + 7 + 5
+
+
+def head(final_low, codes, weights, table):
+    tok, width = final_low.shape
+    rows = table.shape[0]
+    members = weights.shape[0]
+    group = members * tok
+    tiles = rows // TILE
+    hbm = pl.BlockSpec(memory_space=pltpu.HBM)
+    vmem = pl.BlockSpec(memory_space=pltpu.VMEM)
+    low, f32 = jnp.bfloat16, jnp.float32
+    return pl.pallas_call(
+        head_kernel,
+        out_shape=(
+            jax.ShapeDtypeStruct((tok, width), f32),
+            jax.ShapeDtypeStruct((rows, width), low),
+            jax.ShapeDtypeStruct((members, tok), f32),
+        ),
+        in_specs=[vmem, vmem, vmem, hbm],
+        out_specs=(vmem, hbm, vmem),
+        scratch_shapes=[
+            pltpu.VMEM((group, width), low),
+            pltpu.VMEM((members, 8, tok), jnp.int32),
+            pltpu.VMEM((rows, width), low),
+            pltpu.VMEM((TILE, group), f32),
+            pltpu.VMEM((rows, group), low),
+            pltpu.VMEM((tiles, 1, group), f32),
+            pltpu.VMEM((members, 3, members, tok), f32),
+            pltpu.VMEM((group, width), f32),
+            pltpu.VMEM((2, RING, tok, width), low),
+            pltpu.VMEM((RING, tok, width), low),
+            pltpu.VMEM((RING, tok, width), low),
+            pltpu.VMEM((2, tok // 2, width), low),
+            pltpu.VMEM((2, tok, width), low),
+            pltpu.VMEM((2, TILE, width), low),
+            pltpu.SemaphoreType.DMA((HEAD_COPIES,)),
+            pltpu.SemaphoreType.DMA((HEAD_COPIES,)),
+            pltpu.SemaphoreType.DMA((tiles,)),
+            pltpu.SemaphoreType.DMA((tiles,)),
+        ],
+        compiler_params=pltpu.CompilerParams(
+            collective_id=3, has_side_effects=True, vmem_limit_bytes=58 * 2**20
+        ),
+        cost_estimate=pl.CostEstimate(
+            flops=6 * group * rows * width, bytes_accessed=4 * rows * width, transcendentals=group * rows
+        ),
+        name="head",
+    )(final_low, codes, weights, table)
+
+
+def grads_kernel(dqkv_ref, dmid_ref, dup_ref, act_ref, a_ref, o_ref, m_ref, dz_ref, out_ref):
+    step = pl.program_id(0)
+
+    def put(left, right):
+        out_ref[...] = lax.dot_general(
+            left[...], right[...], (((0,), (0,)), ((), ())), preferred_element_type=jnp.float32
+        ).astype(out_ref.dtype)
+
+    pl.when(step < 3)(lambda: put(dqkv_ref, a_ref))
+    pl.when(step == 3)(lambda: put(dmid_ref, o_ref))
+    pl.when((step >= 4) & (step < 8))(lambda: put(dup_ref, m_ref))
+    pl.when(step >= 8)(lambda: put(act_ref, dz_ref))
+
+
+def weight_grads(dqkv, dmid, dup, act, a, o, m, dz):
+    tok, width = a.shape
+
+    def piece(first, count):
+        return pl.BlockSpec((tok, width), lambda i: (0, jnp.clip(i - first, 0, count - 1)))
+
+    whole = pl.BlockSpec((tok, width), lambda i: (0, 0))
+    steps = 12
+    return pl.pallas_call(
+        grads_kernel,
+        grid=(steps,),
+        out_shape=jax.ShapeDtypeStruct((steps * width, width), jnp.bfloat16),
+        in_specs=[piece(0, 3), piece(3, 1), piece(4, 4), piece(8, 4)] + [whole] * 4,
+        out_specs=pl.BlockSpec((width, width), lambda i: (i, 0)),
+        cost_estimate=pl.CostEstimate(
+            flops=2 * tok * steps * width * width,
+            bytes_accessed=2 * steps * width * width,
+            transcendentals=0,
+        ),
+        name="weight_grads",
+    )(dqkv, dmid, dup, act, a, o, m, dz)
+
+
 def layer_norm(inputs, gain, shift):
     centered = inputs - jnp.mean(inputs, -1, keepdims=True)
     spread = jnp.mean(centered * centered, -1, keepdims=True)
@@ -690,20 +1005,17 @@
     )
     low = jnp.bfloat16
     out_low = grad_out.astype(low)
-    grad_wout = contract(activ_low, out_low, 0, 0).astype(low)
     grad_bout = jnp.sum(grad_out, 0)
     grad_act = contract(out_low, w_out, 1, 1)
     unused_up, gelu_pull = jax.vjp(gelu_tanh, up_act)
     grad_up = gelu_pull(grad_act)[0]
     up_low = grad_up.astype(low)
-    grad_wfc = contract(up_low, two_low, 0, 0).astype(low)
     grad_bfc = jnp.sum(grad_up, 0)
     grad_two = contract(up_low, w_fc, 1, 0)
     unused_two, norm_pull = jax.vjp(layer_norm, middle, gain_two, shift_two)
     grad_mid_norm, grad_g2, grad_s2 = norm_pull(grad_two)
     grad_mid = grad_out + grad_mid_norm
     mid_low = grad_mid.astype(low)
-    grad_wproj = contract(mid_low, attended, 0, 0).astype(low)
     grad_bproj = jnp.sum(grad_mid, 0)
     grad_att = contract(mid_low, w_proj, 1, 0).astype(low).reshape(tok, H, head_dim)
     grad_probs = jnp.einsum(
@@ -720,12 +1032,13 @@
     )
     grad_qkv = jnp.stack([grad_q, grad_k, grad_vals], 1).reshape(tok, 3 * width)
     qkv_grad_low = grad_qkv.astype(low)
-    grad_wqkv = contract(qkv_grad_low, normed_low, 0, 0).astype(low)
     grad_normed = contract(qkv_grad_low, w_qkv, 1, 0)
     unused_one, first_pull = jax.vjp(layer_norm, hidden, gain_one, shift_one)
     grad_in_norm, grad_g1, grad_s1 = first_pull(grad_normed)
     grad_in = grad_mid + grad_in_norm
-    grad_mats = jnp.concatenate([grad_wqkv, grad_wproj, grad_wfc, grad_wout], 0)
+    grad_mats = weight_grads(
+        qkv_grad_low, mid_low, up_low, activ_low, normed_low, attended, two_low, out_low
+    )
     grad_vecs = jnp.concatenate(
         [
             grad_g1,
@@ -796,32 +1109,32 @@
     table_padded = jnp.pad(table_low, ((0, pad_rows), (0, 0)))
     slot_rows = own_rows + pad_rows
 
-    both_ids = jnp.stack([token_ids, targets])
-    owners = both_ids // own_rows
-    hits = owners[:, :, None] == jnp.arange(devices, dtype=jnp.int32)[None, None, :]
+    owners = token_ids // own_rows
     tokens = jnp.arange(tok, dtype=jnp.int32)
-    earlier = jnp.sum(
-        (owners[:, :, None] == owners[:, None, :]) & (tokens[None, None, :] < tokens[None, :, None]), 2
-    )
-    slot_hot = hits[:, :, :, None] & (
-        earlier[:, :, None, None] == jnp.arange(capacity, dtype=jnp.int32)[None, None, None, :]
-    )
-    send_rows = jnp.sum(
-        jnp.where(slot_hot, (both_ids % own_rows)[:, :, None, None], 0), 1
-    )
-    slot_hot = slot_hot.reshape(2, tok, devices * capacity).astype(low)
-    local_rows = lax.all_to_all(send_rows, ("dp", "vocab"), split_axis=1, concat_axis=1, tiled=True)
-    asked = (
-        local_rows.reshape(-1)[:, None] == jnp.arange(own_rows, dtype=jnp.int32)[None, :]
-    ).astype(low)
+    earlier = jnp.sum((owners[:, None] == owners[None, :]) & (tokens[None, :] < tokens[:, None]), 1)
+    slot_hot = (owners * capacity + earlier)[:, None] == jnp.arange(
+        devices * capacity, dtype=jnp.int32
+    )[None, :]
+    send_rows = jnp.sum(jnp.where(slot_hot, (token_ids % own_rows)[:, None], 0), 0)
+    slot_hot = slot_hot.astype(low)
+    local_rows = lax.all_to_all(send_rows, ("dp", "vocab"), split_axis=0, concat_axis=0, tiled=True)
+    asked = (local_rows[:, None] == jnp.arange(own_rows, dtype=jnp.int32)[None, :]).astype(low)
     fetched = jnp.dot(asked, table_low, preferred_element_type=jnp.float32).astype(low)
+    blocks, fetched = lax.optimization_barrier((blocks, fetched))
     returned_rows = lax.all_to_all(
-        fetched.reshape(2, devices, capacity, width),
+        fetched.reshape(devices, capacity, width),
         ("dp", "vocab"),
-        split_axis=1,
-        concat_axis=1,
+        split_axis=0,
+        concat_axis=0,
         tiled=True,
-    ).reshape(2, devices * capacity, width)
+    ).reshape(devices * capacity, width)
+    table_slice = lax.all_gather(table_padded, "dp", axis=0, tiled=True)
+    target_owners = targets // own_rows
+    codes = (
+        (target_owners % vocab_count) * (dp_count * slot_rows)
+        + (target_owners // vocab_count) * slot_rows
+        + targets % own_rows
+    )
 
     small = pack_small(
         jnp.concatenate([jnp.transpose(pos_table).reshape(-1), vectors]).astype(low)
@@ -843,15 +1156,12 @@
     weight_group = weight_group * device_rise(data_at * vocab_count, vocab_count, devices)[:, None]
     seg_ids = lax.dynamic_index_in_dim(seg_group, vocab_at, 0, keepdims=False)
     pos_ids = lax.dynamic_index_in_dim(pos_group, vocab_at, 0, keepdims=False)
-    own_weight = lax.dynamic_index_in_dim(weight_group, vocab_at, 0, keepdims=False)
     places = jnp.arange(tok, dtype=jnp.int32)
     attn_mask = (seg_ids[:, None] == seg_ids[None, :]) & (places[None, :] <= places[:, None])
 
-    gotten = jnp.einsum(
-        "ktr,krd->ktd", slot_hot, returned_rows, preferred_element_type=jnp.float32
-    )
+    gotten = jnp.dot(slot_hot, returned_rows, preferred_element_type=jnp.float32)
     pos_hot = (pos_ids[:, None] == jnp.arange(pos_rows, dtype=jnp.int32)[None, :]).astype(low)
-    hidden = gotten[0] + contract(pos_hot, pos_low_t, 1, 1)
+    hidden = gotten + contract(pos_hot, pos_low_t, 1, 1)
     kept = []
     for layer in range(layers):
         hidden, saved = layer_forward(
@@ -863,50 +1173,13 @@
         kept.append(saved)
     tail = vecs_all[layers * vec_width :]
     final_low = layer_norm(hidden, tail[:width], tail[width:]).astype(low)
-    group_rows = lax.all_gather(final_low, "vocab", axis=0, tiled=True)
-    table_blocks = lax.all_gather(table_padded, "dp", axis=0)
-    group_weight = weight_group.reshape(-1)
-    group_count = group_rows.shape[0]
-    real = jnp.arange(slot_rows, dtype=jnp.int32) < own_rows
-
-    def forward_block(carry, piece):
-        top, total = carry
-        logits = jnp.where(real[None, :], contract(group_rows, piece, 1, 1), -1e30)
-        new_top = jnp.maximum(top, jnp.max(logits, 1))
-        total = total * jnp.exp(top - new_top) + jnp.sum(jnp.exp(logits - new_top[:, None]), 1)
-        return ((new_top, total), None)
-
-    start_top = jnp.full((group_count,), -1e30, jnp.float32)
-    (row_top, row_total), unused = lax.scan(
-        forward_block, (start_top, jnp.zeros((group_count,), jnp.float32)), table_blocks
-    )
-    tops, totals = lax.all_gather(jnp.stack([row_top, row_total]), "vocab", axis=1)
-    peak = jnp.max(tops, 0)
-    group_lse = peak + jnp.log(jnp.sum(totals * jnp.exp(tops - peak[None]), 0))
-    own_lse = lax.dynamic_slice_in_dim(group_lse, vocab_at * tok, tok)
-    target_rows = gotten[1]
-    final_f = final_low.astype(jnp.float32)
-    loss_part = jnp.sum(own_weight * (own_lse - jnp.sum(final_f * target_rows, 1)))
-
-    def backward_block(acc, piece):
-        logits = jnp.where(real[None, :], contract(group_rows, piece, 1, 1), -1e30)
-        grad_low = (group_weight[:, None] * jnp.exp(logits - group_lse[:, None])).astype(low)
-        return (
-            acc + jnp.dot(grad_low, piece, preferred_element_type=jnp.float32),
-            contract(grad_low, group_rows, 0, 0).astype(low),
-        )
-
-    group_grad, term = lax.scan(
-        backward_block, jnp.zeros((group_count, width), jnp.float32), table_blocks
-    )
-    own_grad = lax.psum_scatter(
-        group_grad.astype(low), "vocab", scatter_dimension=0, tiled=True
-    ).astype(jnp.float32)
-    table_grad = lax.psum_scatter(
-        term.reshape(slot_rows * dp_count, width), "dp", scatter_dimension=0, tiled=True
-    )[:own_rows].astype(jnp.float32)
-    grad_final = own_grad - own_weight[:, None] * target_rows
-    target_grad = -own_weight[:, None] * final_f
+    grad_final, table_part, token_losses = head(
+        final_low, jnp.broadcast_to(codes[None, :], (8, tok)), weight_group, table_slice
+    )
+    loss_part = jnp.sum(token_losses)
+    table_grad = lax.psum_scatter(table_part, "dp", scatter_dimension=0, tiled=True)[
+        :own_rows
+    ].astype(jnp.float32)
     unused_final, final_pull = jax.vjp(layer_norm, hidden, tail[:width], tail[width:])
     grad_hidden, grad_gf, grad_sf = final_pull(grad_final)
     mats_parts = [None] * layers
@@ -925,17 +1198,13 @@
         (((0,), (0,)), ((), ())),
         precision=lax.Precision.HIGHEST,
     )
-    send_grads = jnp.einsum(
-        "ktr,ktd->krd",
-        slot_hot,
-        jnp.stack([grad_hidden, target_grad]).astype(low),
-        preferred_element_type=jnp.float32,
-    ).astype(low)
+    send_grads = contract(slot_hot, grad_hidden.astype(low), 0, 0).astype(low)
+    mats_parts[0], send_grads = lax.optimization_barrier((mats_parts[0], send_grads))
     back_grads = lax.all_to_all(
-        send_grads.reshape(2, devices, capacity, width),
+        send_grads.reshape(devices, capacity, width),
         ("dp", "vocab"),
-        split_axis=1,
-        concat_axis=1,
+        split_axis=0,
+        concat_axis=0,
         tiled=True,
     ).reshape(-1, width)
     small_grads = pack_small(

time: 885 us -> 546 us (0.62)
  matrix products: 283 us -> 97.1 us
  Pallas kernels: 167 us -> 307 us
  waiting for transfers between devices: 134 us -> 7.5 us
  other arithmetic: 156 us -> 35.1 us
  local copies, waits for them, and re-layouts: 60.8 us -> 47.1 us
  blocking collectives: 13.1 us -> 0 us
  starting transfers between devices: 34.3 us -> 25.4 us
    dot_general x74 -> x19, matrix products: 201 us -> 60.1 us  [contract(): lax.dot_general(left, right, (((left_dim,), (right_dim,)), ((), ())), pre...]
    pallas_call x0 -> x3, Pallas kernels: none -> 103 us  [the longest x1 78.1 us: head(): pl.pallas_call(head_kernel, out_shape=(jax.ShapeDtypeStruct((tok, width),...]
    all_gather x2 -> x1, waiting for transfers between devices: 100 us -> 0.01 us  [per_device(): table_slice = lax.all_gather(table_padded, 'dp', axis=0, tiled=True)]
    concatenate x2 -> x0, other arithmetic: 85.3 us -> none  [layer_backward(): grad_mats = jnp.concatenate([grad_wqkv, grad_wproj, grad_wfc, grad_wout], 0)]
    dot_general x18 -> x1, matrix products: 55.5 us -> 1.27 us  [per_device(): jnp.dot(slot_hot, returned_rows, preferred_element_type=jnp.float32)]
    pallas_call x1, Pallas kernels: 73.3 us -> 110 us  [gather_weights(): pl.pallas_call(gather_kernel, out_shape=(whole, whole, jax.ShapeDtypeStru...]
    reduce_sum x20 -> x3, other arithmetic: 35.2 us -> 0.88 us  [the longest x1 0.6 us: per_device(): loss_part = jnp.sum(token_losses)]
    reduce_scatter x2 -> x1, waiting for transfers between devices: 22.9 us -> 0.02 us  [per_device(): lax.psum_scatter(table_part, 'dp', scatter_dimension=0, tiled=True)]
  transfers between devices with their start and end apart: 7 -> 5, of which waited for: 4 -> 2; matrix products, arithmetic and copies ran while one was open for 21% -> 28% of each run, Pallas kernels for 18% -> 40%
where the time goes in v2:
time: 546 us; the launch traced here: 540 us
  Pallas kernels  307 us (56%)
  matrix products  97.1 us (18%)
  local copies, waits for them, and re-layouts  47.1 us (9%)
  other arithmetic  35.1 us (6%)
  starting transfers between devices  25.4 us (5%)
  between operations  20.5 us (4%)
  waiting for transfers between devices  7.5 us (1%)
    pallas_call x1, Pallas kernels, gather_weights(): pl.pallas_call(gather_kernel, out_shape=(whole, whole, jax.ShapeDtypeStru...  110 us
    pallas_call x1, Pallas kernels, reduce_weights(): pl.pallas_call(reduce_kernel, out_shape=(jax.ShapeDtypeStruct((2, rows //...  79 us
    pallas_call x1, Pallas kernels, head(): pl.pallas_call(head_kernel, out_shape=(jax.ShapeDtypeStruct((tok, width),...  78.1 us
    dot_general x19, matrix products, contract(): lax.dot_general(left, right, (((left_dim,), (right_dim,)), ((), ())), pre...  60.1 us
    pallas_call x2, Pallas kernels, weight_grads(): pl.pallas_call(grads_kernel, grid=(steps,), out_shape=jax.ShapeDtypeStruc...  25 us
    pallas_call x1, Pallas kernels, sum_all(): pl.pallas_call(sum_kernel, out_shape=jax.ShapeDtypeStruct(value.shape, jn...  14.4 us
    unnamed x258, local copies, waits for them, and re-layouts  11.7 us
    all_to_all x1, starting transfers between devices, per_device(): lax.all_to_all(send_rows, ('dp', 'vocab'), split_axis=0, concat_axis=0, t...  11.1 us
  transfers between devices with their start and end apart: 5, of which 2 were waited for; matrix products, arithmetic and copies ran while one was open for 28% of the time, Pallas kernels for 40%

profile of v2, /device:TPU:0, one launch (start us, length us, event | category | flops | bytes accessed | tf_op | source)
XLA Modules:
  0.0 539.6 jit_solution(5272097082607996364)
XLA Ops:
  10.7 11.1 %all-to-all-start = ((s32[128,2,1]{1,2,0:T(1,128)}), s32[128,2,1]{1,2,0:T(1,128)S(1)}, u32[]{:S(2)}, u32[]{:S(2)}) async-start(s32[128,2,1]{1,2,0:T(1,128)} %bitcast.1), calls=%async_computation | async-start | bytes 131072 | tf_op jit(solution)/shard_map/all_to_all | solution.py:1120
  25.2 5.8 %all-to-all-done = s32[128,2,1]{1,2,0:T(1,128)S(1)} async-done(((s32[128,2,1]{1,2,0:T(1,128)}), s32[128,2,1]{1,2,0:T(1,128)S(1)}, u32[]{:S(2)}, u32[]{:S(2)}) %all-to-all-start) | async-done | bytes 1056 | tf_op jit(solution)/shard_map/all_to_all | solution.py:1120
  32.9 110.3 %gather_weights.1 = (bf16[4,4,4,144,768]{4,3,2,1,0:T(8,128)(2,1)}, bf16[4,4,4,144,768]{4,3,2,1,0:T(8,128)(2,1)}, bf16[4,4,4,2,16,128]{5,4,3,2,1,0:T(8,128)(2,1)}) custom-call(f32[2,72,768]{2,1,0:T(8,128)} %bitcast.245, bf16[16,128]{1,0:T(8,128)(2,1)} %fusion.118.small_ref), custom_call_target="tpu_custom_call" | custom-call | tf_op jit(solution)/shard_map/gather_weights/pallas_call | solution.py:200
  145.6 5.7 %all-to-all-start.1 = ((bf16[128,2,768]{2,1,0:T(2,128)(2,1)}), bf16[128,2,768]{2,1,0:T(2,128)(2,1)}, u32[]{:S(2)}, u32[]{:S(2)}) async-start(bf16[128,2,768]{2,1,0:T(2,128)(2,1)} %reshape.381), calls=%async_computation.1 | async-start | bytes 786432 | tf_op jit(solution)/shard_map/all_to_all | solution.py:1124
  155.4 4.0 slice.194
  181.6 5.3 multiply_convert_fusion.1
  187.0 3.5 fusion.164
  204.8 5.3 multiply_convert_fusion
  210.1 3.5 fusion.167
  217.0 78.1 %head.1 = (f32[128,768]{1,0:T(8,128)}, bf16[6400,768]{1,0:T(8,128)(2,1)}, f32[8,128]{1,0:T(8,128)}) custom-call(bf16[128,768]{1,0:T(8,128)(2,1)} %add_convert_fusion.f_ref, s32[8,128]{1,0:T(8,128)} %broadcast_in_dim.76.code_ref, f32[8,128]{1,0:T(8,128)} %divide_multiply_fusion.weight_ref, bf16[6400,768]{1,0:T(8,128)(2,1)} %all-gather.2.cloned.1.call-done.table_ref), custom_call_target="tpu_custom_call" | custom-call | flops 30198988800 | bytes 19660800 | tf_op jit(solution)/shard_map/head/pallas_call | solution.py:833
  303.4 5.5 %fusion.156 = (f32[3072]{0:T(1024)}, bf16[128,3072]{1,0:T(8,128)(2,1)S(1)}) fusion(f32[128,3072]{1,0:T(8,128)S(1)} %copy-done.117, bf16[128,768]{1,0:T(8,128)(2,1)S(1)} %get-tuple-element.91.dz_ref, bf16[9216,768]{1,0:T(8,128)(2,1)} %bitcast.257), kind=kOutput, calls=%fused_computation.303 | convolution fusion | flops 612234240 | bytes 7286784 | tf_op jit(solution)/shard_map/dot_general | solution.py:937
  309.0 4.2 multiply_reduce_fusion.5
  324.4 3.6 bitcast_reduce_fusion.3
  328.0 3.1 bitcast_reduce_fusion.2
  335.4 3.8 multiply_reduce_fusion.6
  340.6 5.1 fusion.157
  345.7 4.4 multiply_reduce_fusion.7
  361.3 3.6 bitcast_reduce_fusion.1
  364.9 3.1 bitcast_reduce_fusion
  372.0 12.6 %weight_grads.2 = bf16[9216,768]{1,0:T(8,128)(2,1)} custom-call(bf16[128,2304]{1,0:T(8,128)(2,1)} %copy.112.dqkv_ref, bf16[128,768]{1,0:T(8,128)(2,1)} %copy-done.28, bf16[128,3072]{1,0:T(8,128)(2,1)} %copy-done.32, bf16[128,3072]{1,0:T(8,128)(2,1)} %copy-done.31, bf16[128,768]{1,0:T(8,128)(2,1)} %copy-done.18, bf16[128,768]{1,0:T(8,128)(2,1)} %copy.113.o_ref, ...), custom_call_target="tpu_custom_call" | custom-call | flops 1811939328 | bytes 14155776 | tf_op jit(solution)/shard_map/weight_grads/pallas_call | solution.py:894
  389.2 8.3 %all-to-all-start.2 = ((bf16[128,2,768]{2,1,0:T(2,128)(2,1)}), bf16[128,2,768]{2,1,0:T(2,128)(2,1)S(1)}, u32[]{:S(2)}, u32[]{:S(2)}) async-start(bf16[128,2,768]{2,1,0:T(2,128)(2,1)} %reshape.392), calls=%async_computation.3 | async-start | bytes 786432 | tf_op jit(solution)/shard_map/all_to_all | solution.py:1203
  399.1 12.4 %weight_grads.3 = bf16[9216,768]{1,0:T(8,128)(2,1)} custom-call(bf16[128,2304]{1,0:T(8,128)(2,1)} %copy.114.dqkv_ref, bf16[128,768]{1,0:T(8,128)(2,1)} %copy-done.25, bf16[128,3072]{1,0:T(8,128)(2,1)} %copy-done.30, bf16[128,3072]{1,0:T(8,128)(2,1)} %copy-done.29, bf16[128,768]{1,0:T(8,128)(2,1)} %copy-done.17, bf16[128,768]{1,0:T(8,128)(2,1)} %copy.115.o_ref, ...), custom_call_target="tpu_custom_call" | custom-call | flops 1811939328 | bytes 14155776 | tf_op jit(solution)/shard_map/weight_grads/pallas_call | solution.py:894
  413.5 79.0 %reduce_weights.1 = (f32[2,72,768]{2,1,0:T(8,128)}, f32[16,128]{1,0:T(8,128)}) custom-call(bf16[4,4,4,144,768]{4,3,2,1,0:T(8,128)(2,1)} %bitcast.234, bf16[4,4,4,144,768]{4,3,2,1,0:T(8,128)(2,1)} %bitcast.235, f32[4,4,4,2,16,128]{5,4,3,2,1,0:T(8,128)} %bitcast.244), custom_call_target="tpu_custom_call" | custom-call | bytes 280000000 | tf_op jit(solution)/shard_map/reduce_weights/pallas_call | solution.py:504
  503.5 14.4 %sum_all.1 = f32[8,128]{1,0:T(8,128)} custom-call(f32[8,128]{1,0:T(8,128)} %broadcast_in_dim.88.in_ref), custom_call_target="tpu_custom_call" | custom-call | tf_op jit(solution)/shard_map/sum_all/pallas_call | solution.py:580
  (405 shorter events, 123.3 us)
Async XLA Ops:
  7.2 14.6 %copy-start.102 = (f32[156]{0:T(256)S(1)}, f32[156]{0:T(256)}, u32[]{:S(2)}) copy-start(f32[156]{0:T(256)} %param.27) | copy-start | bytes 1876
  7.2 14.6 %copy-start.53 = (f32[80,6]{0,1:T(8,128)S(1)}, f32[80,6]{0,1:T(8,128)}, u32[]{:S(2)}) copy-start(f32[80,6]{0,1:T(8,128)} %param.24) | copy-start | bytes 5764
  7.2 14.7 %copy-start.72 = (s32[1,8,3]{1,0,2:T(1,128)S(1)}, s32[1,8,3]{1,0,2:T(1,128)}, u32[]{:S(2)}) copy-start(s32[1,8,3]{1,0,2:T(1,128)} %param.17) | copy-start | bytes 292
  7.2 15.6 %copy-start.115 = (s32[128]{0:T(128)S(1)}, s32[128]{0:T(128)}, u32[]{:S(2)}) copy-start(s32[128]{0:T(128)} %param.16) | copy-start | bytes 1540
  7.2 208.5 %all-gather.2.cloned.1.call-start = ((), (), s32[]{:S(2)}) async-start(), calls=%async_computation.4 | async-start | bytes 10444800 | tf_op jit(solution)/shard_map/all_gather | solution.py:1131
  9.8 12.1 %copy-start.82 = (s32[128]{0:T(128)}, s32[128]{0:T(128)S(1)}, u32[]{:S(2)}) copy-start(s32[128]{0:T(128)S(1)} %multiply_add_fusion.8) | copy-start | bytes 1540
  10.7 20.4 %all-to-all-start = ((s32[128,2,1]{1,2,0:T(1,128)}), s32[128,2,1]{1,2,0:T(1,128)S(1)}, u32[]{:S(2)}, u32[]{:S(2)}) async-start(s32[128,2,1]{1,2,0:T(1,128)} %bitcast.1), calls=%async_computation | async-start | bytes 131072 | tf_op jit(solution)/shard_map/all_to_all | solution.py:1120
  32.5 111.9 %copy-start.84 = (s32[256]{0:T(256)}, s32[256]{0:T(256)S(1)}, u32[]{:S(2)}) copy-start(s32[256]{0:T(256)S(1)} %eq.98) | copy-start | bytes 3076
  145.6 17.5 %all-to-all-start.1 = ((bf16[128,2,768]{2,1,0:T(2,128)(2,1)}), bf16[128,2,768]{2,1,0:T(2,128)(2,1)}, u32[]{:S(2)}, u32[]{:S(2)}) async-start(bf16[128,2,768]{2,1,0:T(2,128)(2,1)} %reshape.381), calls=%async_computation.1 | async-start | bytes 786432 | tf_op jit(solution)/shard_map/all_to_all | solution.py:1124
  151.3 345.8 %reduce-scatter.2.cloned.1.call-start = ((), (), s32[]{:S(2)}) async-start(), calls=%async_computation.5 | async-start | bytes 10444800 | tf_op jit(solution)/shard_map/reduce_scatter | solution.py:1180
  387.8 10.2 %copy-start.90 = (f32[768]{0:T(1024)S(1)}, f32[768]{0:T(1024)}, u32[]{:S(2)}) copy-start(f32[768]{0:T(1024)} %get-tuple-element.53) | copy-start | bytes 9220
  387.8 10.2 %copy-start.59 = (f32[3072]{0:T(1024)S(1)}, f32[3072]{0:T(1024)}, u32[]{:S(2)}) copy-start(f32[3072]{0:T(1024)} %get-tuple-element.85) | copy-start | bytes 36868
  387.8 10.3 %copy-start.47 = (f32[768]{0:T(1024)S(1)}, f32[768]{0:T(1024)}, u32[]{:S(2)}) copy-start(f32[768]{0:T(1024)} %get-tuple-element.90) | copy-start | bytes 9220
  387.9 10.3 %copy-start.46 = (f32[768]{0:T(1024)S(1)}, f32[768]{0:T(1024)}, u32[]{:S(2)}) copy-start(f32[768]{0:T(1024)} %get-tuple-element.42) | copy-start | bytes 9220
  387.9 10.3 %copy-start.45 = (f32[768]{0:T(1024)S(1)}, f32[768]{0:T(1024)}, u32[]{:S(2)}) copy-start(f32[768]{0:T(1024)} %get-tuple-element.52) | copy-start | bytes 9220
  387.9 10.4 %copy-start.12 = (f32[128,768]{1,0:T(8,128)S(1)}, f32[128,768]{1,0:T(8,128)}, u32[]{:S(2)}) copy-start(f32[128,768]{1,0:T(8,128)} %copy-done.10) | copy-start | bytes 1179652
  387.9 10.4 %copy-start.96 = (s32[128]{0:T(128)S(1)}, s32[128]{0:T(128)}, u32[]{:S(2)}) copy-start(s32[128]{0:T(128)} %dynamic-slice_bitcast_fusion.1) | copy-start | bytes 1540
  389.2 107.7 %all-to-all-start.2 = ((bf16[128,2,768]{2,1,0:T(2,128)(2,1)}), bf16[128,2,768]{2,1,0:T(2,128)(2,1)S(1)}, u32[]{:S(2)}, u32[]{:S(2)}) async-start(bf16[128,2,768]{2,1,0:T(2,128)(2,1)} %reshape.392), calls=%async_computation.3 | async-start | bytes 786432 | tf_op jit(solution)/shard_map/all_to_all | solution.py:1203
  413.5 83.6 %copy-start.85 = (s32[256]{0:T(256)S(1)}, s32[256]{0:T(256)}, u32[]{:S(2)}) copy-start(s32[256]{0:T(256)} %copy-done.84) | copy-start | bytes 3076
  496.9 23.7 %copy-start.19 = (f32[2,768,72]{1,2,0:T(8,128)S(1)}, f32[2,768,72]{1,2,0:T(8,128)}, u32[]{:S(2)}) copy-start(f32[2,768,72]{1,2,0:T(8,128)} %param.21) | copy-start | bytes 1327108
  496.9 23.7 %copy-start.20 = (f32[2,72,768]{2,1,0:T(8,128)S(1)}, f32[2,72,768]{2,1,0:T(8,128)}, u32[]{:S(2)}) copy-start(f32[2,72,768]{2,1,0:T(8,128)} %get-tuple-element.40) | copy-start | bytes 1327108
  499.4 23.4 %copy-start.103 = (f32[156]{0:T(256)S(1)}, f32[156]{0:T(256)}, u32[]{:S(2)}) copy-start(f32[156]{0:T(256)} %param.27) | copy-start | bytes 1876
  499.4 23.4 %copy-start.104 = (f32[156]{0:T(256)S(1)}, f32[156]{0:T(256)}, u32[]{:S(2)}) copy-start(f32[156]{0:T(256)} %param.28) | copy-start | bytes 1876
  499.4 24.7 %copy-start.14 = (f32[393,768]{1,0:T(8,128)S(1)}, f32[393,768]{1,0:T(8,128)}, u32[]{:S(2)}) copy-start(f32[393,768]{1,0:T(8,128)} %param.18) | copy-start | bytes 3621892
  (99 other events, 394.9 us)
Sparse Core Ops, SparseCore 0:
  10.8 118.1 all-gather.1
  295.2 88.0 reduce-scatter.1

commit v3 on v2

--- a/solution.py
+++ b/solution.py
@@ -73,10 +73,9 @@
 
 
 def gather_kernel(
-    mine_ref, small_ref, first_ref, second_ref, small_out, peer, block, send, recv, local
+    mine_ref, small_ref, out_ref, small_out, peer, block, send, recv, local
 ):
     at, core = place()
-    out_refs = (first_ref, second_ref)
     rows, half = mine_ref.shape[1], mine_ref.shape[2] // 2
     part = 2 * rows // 3
     sibling = device_at(at, 1 - core)
@@ -100,7 +99,7 @@
     for layer in range(2):
         op = pltpu.make_async_copy(
             block.at[layer],
-            out_refs[layer].at[at[0], at[1], at[2], :, cols],
+            out_ref.at[layer, at[0], at[1], at[2], :, cols],
             local.at[1 + layer],
         )
         op.start()
@@ -118,7 +117,7 @@
                 first, count = (first, 32) if piece == 0 else (first + 32, part - 32)
             else:
                 index[order[0]] = pl.ds(2 * piece, 2)
-        return out_refs[layer].at[index[0], index[1], index[2], pl.ds(first, count), cols]
+        return out_ref.at[layer, index[0], index[1], index[2], pl.ds(first, count), cols]
 
     def small_bundle(phase, c):
         order = ORDERS[0]
@@ -194,18 +193,17 @@
 
 def gather_weights(mine, small):
     layers, rows, width = mine.shape
-    whole = jax.ShapeDtypeStruct((RING, RING, RING, 2 * rows, width), jnp.bfloat16)
+    whole = jax.ShapeDtypeStruct((layers, RING, RING, RING, 2 * rows, width), jnp.bfloat16)
     hbm = pl.BlockSpec(memory_space=pltpu.HBM)
     vmem = pl.BlockSpec(memory_space=pltpu.VMEM)
-    first, second, small_all = pl.pallas_call(
+    mats, small_all = pl.pallas_call(
         gather_kernel,
         out_shape=(
-            whole,
             whole,
             jax.ShapeDtypeStruct((RING, RING, RING, 2) + small.shape, jnp.bfloat16),
         ),
         in_specs=[vmem, vmem],
-        out_specs=(hbm, hbm, hbm),
+        out_specs=(hbm, hbm),
         scratch_shapes=[
             pltpu.VMEM((layers, rows, width // 2), jnp.float32),
             pltpu.VMEM((layers, 2 * rows, width // 2), jnp.bfloat16),
@@ -216,31 +214,182 @@
         compiler_params=pltpu.CompilerParams(
             collective_id=0, has_side_effects=True, vmem_limit_bytes=58 * 2**20
         ),
+        cost_estimate=pl.CostEstimate(flops=0, bytes_accessed=250 * 10**6, transcendentals=0),
         name="gather_weights",
     )(mine, small)
-    count = RING**3 * 2 * rows
     return (
-        (first.reshape(count, width), second.reshape(count, width)),
+        mats.reshape(layers * RING**3 * 2 * rows, width),
         small_all.reshape((2 * RING**3,) + small.shape),
     )
 
 
+class Reduction:
+    def __init__(self, at, core, send, recv):
+        self.at, self.core, self.send, self.recv = at, core, send, recv
+        self.number, self.level, self.halves, self.fulls = {}, {}, {}, {}
+        self.final = None
+
+    def copy(self, key, src, dst, device):
+        number = self.number.setdefault(key, len(self.number))
+        return pltpu.make_async_remote_copy(
+            src_ref=src,
+            dst_ref=dst,
+            send_sem=self.send.at[number],
+            recv_sem=self.recv.at[number],
+            device_id=device,
+            device_id_type=pl.DeviceIdType.MESH,
+        )
+
+    def axes(self, p):
+        order = ORDERS[p]
+        free = sorted(order[:2])
+        return free, free.index(order[1])
+
+    def ring(self, p, step):
+        axis = ORDERS[p][2 - step]
+        c = self.at[axis]
+        right = device_at(moved(self.at, axis, 1), self.core)
+        left = device_at(moved(self.at, axis, RING - 1), self.core)
+        return c, lax.rem(c + 1, RING), lax.rem(c + 2, RING), lax.rem(c + 3, RING), right, left
+
+    def index(self, layer, p, step, c, piece=None):
+        part = 48
+        cut, whole = (0, RING) if piece is None else (2 * piece, 2), (0, RING)
+        if step == 0:
+            free, unused = self.axes(p)
+            spot = [c, c, c]
+            spot[free[0]], spot[free[1]] = cut, whole
+            return spot + [pl.ds(p * part, part)]
+        if step == 1:
+            unused, first = self.axes(p)
+            spot = [cut, cut]
+            spot[first] = c
+            return [layer % self.level[1].shape[0], p] + spot
+        if piece is None:
+            return [layer, p, c]
+        return [layer, p, c, pl.ds(0, 32) if piece == 0 else pl.ds(32, part - 32)]
+
+    def view(self, layer, p, step, c, piece=None):
+        index = self.index(layer, p, step, c, piece)
+        held = self.level[0, layer] if step == 0 else self.level[step]
+        return held.at[tuple(pl.ds(*item) if isinstance(item, tuple) else item for item in index)]
+
+    def slot(self, layer, p, step, side, whole):
+        store = (self.fulls if whole else self.halves)[step]
+        if step == 2 and not whole:
+            return store.at[layer, p, side, pl.ds(0, 32 if side == 0 else 16)]
+        return store.at[layer % store.shape[0], p, side]
+
+    def half_copies(self, layer, p, step):
+        unused, after, across, before, right, left = self.ring(p, step)
+        out = []
+        for side, device in ((0, right), (1, left)):
+            out.append(
+                self.copy(
+                    (layer, p, step, side),
+                    self.view(layer, p, step, across, side),
+                    self.slot(layer, p, step, side, False),
+                    device,
+                )
+            )
+        return out
+
+    def full_copies(self, layer, p, step):
+        unused, after, across, before, right, left = self.ring(p, step)
+        out = []
+        for side, c, device in ((0, after, right), (1, before, left)):
+            out.append(
+                self.copy(
+                    (layer, p, step, 2 + side),
+                    self.view(layer, p, step, c),
+                    self.slot(layer, p, step, side, True),
+                    device,
+                )
+            )
+        return out
+
+    def add(self, layer, p, step, c, piece, terms, into):
+        held = self.level[0, layer] if step == 0 else self.level[step]
+        index = self.index(layer, p, step, c, piece)
+        sizes = [item[1] for item in index if isinstance(item, tuple)]
+        total = 1
+        for size in sizes:
+            total *= size
+
+        def body(n, unused):
+            inner = [lax.div(n, sizes[1]), lax.rem(n, sizes[1])] if len(sizes) == 2 else [n] * len(sizes)
+            places = iter(inner)
+            spot = tuple(
+                item[0] + next(places) if isinstance(item, tuple) else item for item in index
+            )
+            value = held[spot].astype(jnp.float32)
+            for term in terms:
+                value = value + term[tuple(inner) + (slice(None), slice(None))].astype(jnp.float32)
+            into(held, spot, inner, value)
+            return unused
+
+        if total == 1:
+            body(0, 0)
+        else:
+            lax.fori_loop(0, total, body, 0)
+
+    def start(self, layer, step):
+        for p in range(3):
+            for op in self.half_copies(layer, p, step):
+                op.start()
+
+    def turn(self, layer, step):
+        def back(held, spot, inner, value):
+            held[spot] = value.astype(held.dtype)
+
+        for p in range(3):
+            unused, after, across, before, right, left = self.ring(p, step)
+            halves, fulls = self.half_copies(layer, p, step), self.full_copies(layer, p, step)
+            for side, c in ((0, after), (1, before)):
+                halves[side].wait_recv()
+                self.add(
+                    layer, p, step, c, side, [self.slot(layer, p, step, side, False)], back
+                )
+                fulls[side].start()
+
+    def finish(self, layer, step):
+        for p in range(3):
+            c = self.ring(p, step)[0]
+            for op in self.full_copies(layer, p, step):
+                op.wait_recv()
+            terms = [self.slot(layer, p, step, side, True) for side in range(2)]
+
+            def up(held, spot, inner, value, p=p):
+                if step == 2:
+                    self.final[layer, p * 48 : (p + 1) * 48] = value
+                else:
+                    target = self.level[step + 1]
+                    spot = (layer % target.shape[0], p) + tuple(inner)
+                    target[spot] = value.astype(target.dtype)
+
+            self.add(layer, p, step, c, None, terms, up)
+
+    def drain(self, layer, step):
+        for p in range(3):
+            for op in self.half_copies(layer, p, step) + self.full_copies(layer, p, step):
+                op.wait_send()
+
+
 def reduce_kernel(
-    first_ref,
-    second_ref,
+    acc_ref,
+    mid_ref,
     small_ref,
     out_ref,
     small_out,
     acc,
-    sib,
-    wide_half_0,
-    wide_half_1,
-    wide_half_2,
-    wide_full,
-    mid_half,
-    mid_full,
-    thin_half,
-    thin_full,
+    mid,
+    thin,
+    half_0,
+    half_1,
+    half_2,
+    full_0,
+    full_1,
+    full_2,
     small_acc,
     small_sib,
     small_wide,
@@ -250,146 +399,42 @@
     final_peer,
     send,
     recv,
+    send_small,
+    recv_small,
     local,
 ):
     at, core = place()
-    grads = (first_ref, second_ref)
-    rows, half = acc.shape[4], acc.shape[5]
-    own_rows = rows // 2
-    part = rows // 3
+    own_rows, half = final_peer.shape[1], final_peer.shape[2]
     sibling = device_at(at, 1 - core)
-    cols = pl.ds(pl.multiple_of(core * half, half), half)
-    other = pl.ds(pl.multiple_of((1 - core) * half, half), half)
-    chains = [(layer, p) for layer in range(2) for p in range(3)]
-    loads = {}
-    number = 0
-    near = (2, 1, 3, 0)
-
-    def span(p, step, c, piece=None):
-        order = ORDERS[p]
+    sums = Reduction(at, core, send, recv)
+    sums.level = {(0, 0): acc, 1: mid, 2: thin}
+    sums.halves = {0: half_0, 1: half_1, 2: half_2}
+    sums.fulls = {0: full_0, 1: full_1, 2: full_2}
+    sums.final = final
+
+    mid_load = pltpu.make_async_copy(mid_ref, mid.at[1], local.at[0])
+    mid_load.start()
+    acc_load = pltpu.make_async_copy(acc_ref, acc, local.at[1])
+    acc_load.start()
+    small_load = pltpu.make_async_copy(small_ref.at[:, :, :, core], small_acc, local.at[2])
+    small_load.start()
+    greet(neighbours(at, core))
+    wires = Wires(send_small, recv_small)
+    small_swap = wires.copy(small_ref.at[:, :, :, 1 - core], small_sib, sibling)
+
+    order = ORDERS[0]
+    slots = (small_wide, small_mid, small_thin)
+
+    def right(axis):
+        return device_at(moved(at, axis, 1), core)
+
+    def left(axis):
+        return device_at(moved(at, axis, RING - 1), core)
+
+    def small_view(step, c):
         index = list(at)
         index[order[2 - step]] = c
         for axis in order[: 2 - step]:
-            index[axis] = pl.ds(0, RING)
-        first, count = p * part, part
-        if piece is not None:
-            if step == 2:
-                first, count = (first, 32) if piece == 0 else (first + 32, part - 32)
-            else:
-                index[order[0]] = pl.ds(2 * piece, 2)
-        return index, pl.ds(first, count)
-
-    for by in near:
-        for key in chains:
-            layer, p = key
-            c = lax.rem(at[ORDERS[p][2]] + by, RING)
-            index, where = span(p, 0, c)
-            op = pltpu.make_async_copy(
-                grads[layer].at[index[0], index[1], index[2], where, cols],
-                acc.at[layer, index[0], index[1], index[2], where],
-                local.at[number],
-            )
-            op.start()
-            loads[key, by] = op
-            number += 1
-    small_load = pltpu.make_async_copy(small_ref.at[:, :, :, core], small_acc, local.at[number])
-    small_load.start()
-
-    greet(neighbours(at, core))
-    wires = Wires(send, recv)
-    swaps = {}
-    small_swap = wires.copy(small_ref.at[:, :, :, 1 - core], small_sib, sibling)
-    for by in near:
-        for key in chains:
-            layer, p = key
-            c = lax.rem(at[ORDERS[p][2]] + by, RING)
-            index, where = span(p, 0, c)
-            swaps[key, by] = wires.copy(
-                grads[layer].at[index[0], index[1], index[2], where, other],
-                sib.at[layer, index[0], index[1], index[2], where],
-                sibling,
-            )
-
-    def right(axis):
-        return device_at(moved(at, axis, 1), core)
-
-    def left(axis):
-        return device_at(moved(at, axis, RING - 1), core)
-
-    def add(layer, p, step, c, piece, terms, into=None):
-        order = ORDERS[p]
-        free = [axis for axis in range(3) if axis in order[: 2 - step]]
-        sizes = [2 if piece is not None and axis == order[0] else RING for axis in free]
-        index, where = span(p, step, c, piece)
-        total = 1
-        for size in sizes:
-            total *= size
-
-        def body(n, unused):
-            spot = list(index)
-            inner = []
-            if len(free) == 2:
-                inner = [lax.div(n, sizes[1]), lax.rem(n, sizes[1])]
-            elif len(free) == 1:
-                inner = [n]
-            for axis, size, i in zip(free, sizes, inner):
-                start = 2 * piece if size == 2 else 0
-                spot[axis] = start + i
-            here = (layer, spot[0], spot[1], spot[2], where)
-            value = acc[here].astype(jnp.float32)
-            for term in terms:
-                value = value + term(inner, spot, where).astype(jnp.float32)
-            if into is None:
-                acc[here] = value.astype(jnp.bfloat16)
-            else:
-                into(value)
-            return unused
-
-        if total == 1:
-            body(0, 0)
-        else:
-            lax.fori_loop(0, total, body, 0)
-
-    def add_sibling(key, by):
-        layer, p = key
-        loads[key, by].wait()
-        swaps[key, by].wait_recv()
-        c = lax.rem(at[ORDERS[p][2]] + by, RING)
-        add(
-            layer,
-            p,
-            0,
-            c,
-            None,
-            [lambda inner, spot, where: sib[layer, spot[0], spot[1], spot[2], where]],
-        )
-
-    wide_half = (wide_half_0, wide_half_1, wide_half_2)
-
-    def half_slot(layer, p, step, side):
-        if step == 0:
-            return wide_half[p].at[layer, side]
-        if step == 1:
-            return mid_half.at[layer, p, side]
-        return thin_half.at[layer, p, side, pl.ds(0, 32 if side == 0 else part - 32)]
-
-    def full_slot(layer, p, step, side):
-        return (wide_full, mid_full, thin_full)[step].at[layer, p, side]
-
-    def read(slot):
-        return lambda inner, spot, where: slot[tuple(inner) + (slice(None), slice(None))]
-
-    def acc_view(layer, p, step, c, piece=None):
-        index, where = span(p, step, c, piece)
-        return acc.at[layer, index[0], index[1], index[2], where]
-
-    small_order = ORDERS[0]
-    small_slots = (small_wide, small_mid, small_thin)
-
-    def small_view(step, c):
-        index = list(at)
-        index[small_order[2 - step]] = c
-        for axis in small_order[: 2 - step]:
             index[axis] = slice(None)
         return tuple(index)
 
@@ -397,79 +442,55 @@
         where = small_view(step, c)
         small_acc[where] = small_acc[where] + term
 
-    for step in range(3):
-        halves = {}
-        for key in chains:
-            layer, p = key
-            axis = ORDERS[p][2 - step]
-            if step == 0:
-                add_sibling(key, 2)
-            across = lax.rem(at[axis] + 2, RING)
-            halves[key] = (
-                wires.copy(
-                    acc_view(layer, p, step, across, 0), half_slot(layer, p, step, 0), right(axis)
-                ),
-                wires.copy(
-                    acc_view(layer, p, step, across, 1), half_slot(layer, p, step, 1), left(axis)
-                ),
-            )
-        if step == 0:
-            small_load.wait()
-            small_swap.wait_recv()
-            small_acc[...] = small_acc[...] + small_sib[...]
-        axis = small_order[2 - step]
+    def small_start(step):
+        axis = order[2 - step]
         across = lax.rem(at[axis] + 2, RING)
-        small_half = wires.copy(
-            small_acc.at[small_view(step, across)], small_slots[step].at[0], right(axis)
+        return wires.copy(small_acc.at[small_view(step, across)], slots[step].at[0], right(axis))
+
+    def small_turn(step, op):
+        axis = order[2 - step]
+        after, before = lax.rem(at[axis] + 1, RING), lax.rem(at[axis] + 3, RING)
+        op.wait_recv()
+        small_add(step, after, slots[step][0])
+        return (
+            wires.copy(small_acc.at[small_view(step, after)], slots[step].at[1], right(axis)),
+            wires.copy(small_acc.at[small_view(step, before)], slots[step].at[2], left(axis)),
         )
-        if step == 0:
-            for key in chains:
-                add_sibling(key, 1)
-                add_sibling(key, 3)
-        fulls = {}
-        for key in chains:
-            layer, p = key
-            axis = ORDERS[p][2 - step]
-            after, before = lax.rem(at[axis] + 1, RING), lax.rem(at[axis] + 3, RING)
-            halves[key][0].wait_recv()
-            add(layer, p, step, after, 0, [read(half_slot(layer, p, step, 0))])
-            one = wires.copy(
-                acc_view(layer, p, step, after), full_slot(layer, p, step, 0), right(axis)
-            )
-            halves[key][1].wait_recv()
-            add(layer, p, step, before, 1, [read(half_slot(layer, p, step, 1))])
-            two = wires.copy(
-                acc_view(layer, p, step, before), full_slot(layer, p, step, 1), left(axis)
-            )
-            fulls[key] = (one, two)
-        axis = small_order[2 - step]
-        after, before = lax.rem(at[axis] + 1, RING), lax.rem(at[axis] + 3, RING)
-        small_half.wait_recv()
-        small_add(step, after, small_slots[step][0])
-        small_full = (
-            wires.copy(small_acc.at[small_view(step, after)], small_slots[step].at[1], right(axis)),
-            wires.copy(small_acc.at[small_view(step, before)], small_slots[step].at[2], left(axis)),
-        )
-        for key in chains:
-            layer, p = key
-            axis = ORDERS[p][2 - step]
-            if step == 0:
-                add_sibling(key, 0)
-            fulls[key][0].wait_recv()
-            fulls[key][1].wait_recv()
-            terms = [read(full_slot(layer, p, step, side)) for side in range(2)]
-            if step < 2:
-                add(layer, p, step, at[axis], None, terms)
-            else:
-
-                def keep(value, layer=layer, p=p):
-                    final[layer, p * part : (p + 1) * part] = value
-
-                add(layer, p, step, at[axis], None, terms, keep)
-        axis = small_order[2 - step]
-        for op in small_full:
+
+    def small_finish(step, ops):
+        for op in ops:
             op.wait_recv()
-        small_add(step, at[axis], small_slots[step][1] + small_slots[step][2])
+        small_add(step, at[order[2 - step]], slots[step][1] + slots[step][2])
+
+    mid_load.wait()
+    sums.start(1, 1)
+    acc_load.wait()
+    sums.start(0, 0)
+    small_load.wait()
+    small_swap.wait_recv()
+    small_acc[...] = small_acc[...] + small_sib[...]
+    op = small_start(0)
+    sums.turn(1, 1)
+    sums.finish(1, 1)
+    sums.start(1, 2)
+    sums.turn(0, 0)
+    ops = small_turn(0, op)
+    sums.turn(1, 2)
+    sums.finish(1, 2)
+    small_finish(0, ops)
+    op = small_start(1)
+    ops = small_turn(1, op)
+    small_finish(1, ops)
+    op = small_start(2)
+    ops = small_turn(2, op)
+    sums.finish(0, 0)
+    sums.start(0, 1)
+    small_finish(2, ops)
+    sums.turn(0, 1)
+    sums.finish(0, 1)
+    sums.start(0, 2)
+    sums.turn(0, 2)
+    sums.finish(0, 2)
 
     theirs = pl.ds(pl.multiple_of((1 - core) * own_rows, own_rows), own_rows)
     swap = wires.copy(final.at[:, theirs], final_peer, sibling)
@@ -480,45 +501,36 @@
         got = final_peer[layer]
         out_ref[layer, :, :half] = jnp.where(core == 0, own, got)
         out_ref[layer, :, half:] = jnp.where(core == 0, got, own)
+    for layer, step in ((1, 1), (1, 2), (0, 0), (0, 1), (0, 2)):
+        sums.drain(layer, step)
     wires.drain()
 
 
-REDUCE_COPIES = 1 + 24 + 3 * (6 * 4 + 3) + 1
-
-
-def reduce_weights(first, second, small):
-    count, width = first.shape
-    rows, half = count // RING**3, width // 2
+def reduce_weights(acc, mid, small):
+    rows, half = acc.shape[3:]
     part = rows // 3
     torus = (RING, RING, RING)
     small_shape = small.shape[1:]
     hbm = pl.BlockSpec(memory_space=pltpu.HBM)
     vmem = pl.BlockSpec(memory_space=pltpu.VMEM)
     low = jnp.bfloat16
-
-    def wide_shape(p):
-        order = ORDERS[p]
-        free = [axis for axis in range(3) if axis in order[:2]]
-        return tuple(2 if axis == order[0] else RING for axis in free)
-
     return pl.pallas_call(
         reduce_kernel,
         out_shape=(
-            jax.ShapeDtypeStruct((2, rows // 2, width), jnp.float32),
+            jax.ShapeDtypeStruct((2, rows // 2, 2 * half), jnp.float32),
             jax.ShapeDtypeStruct(small_shape, jnp.float32),
         ),
         in_specs=[hbm, hbm, hbm],
         out_specs=(vmem, vmem),
         scratch_shapes=[
-            pltpu.VMEM((2,) + torus + (rows, half), low),
-            pltpu.VMEM((2,) + torus + (rows, half), low),
-        ]
-        + [pltpu.VMEM((2, 2) + wide_shape(p) + (part, half), low) for p in range(3)]
-        + [
-            pltpu.VMEM((2, 3, 2, RING, RING, part, half), low),
+            pltpu.VMEM(torus + (rows, half), low),
+            pltpu.VMEM((2, 3, RING, RING, part, half), low),
+            pltpu.VMEM((2, 3, RING, part, half), low),
+            pltpu.VMEM((1, 3, 2, 2, RING, part, half), low),
             pltpu.VMEM((2, 3, 2, 2, part, half), low),
+            pltpu.VMEM((2, 3, 2, 32, half), low),
+            pltpu.VMEM((1, 3, 2, RING, RING, part, half), low),
             pltpu.VMEM((2, 3, 2, RING, part, half), low),
-            pltpu.VMEM((2, 3, 2, 32, half), low),
             pltpu.VMEM((2, 3, 2, part, half), low),
             pltpu.VMEM(torus + small_shape, jnp.float32),
             pltpu.VMEM(torus + small_shape, jnp.float32),
@@ -527,20 +539,18 @@
             pltpu.VMEM((3,) + small_shape, jnp.float32),
             pltpu.VMEM((2, rows, half), jnp.float32),
             pltpu.VMEM((2, rows // 2, half), jnp.float32),
-            pltpu.SemaphoreType.DMA((REDUCE_COPIES,)),
-            pltpu.SemaphoreType.DMA((REDUCE_COPIES,)),
-            pltpu.SemaphoreType.DMA((25,)),
+            pltpu.SemaphoreType.DMA((60,)),
+            pltpu.SemaphoreType.DMA((60,)),
+            pltpu.SemaphoreType.DMA((11,)),
+            pltpu.SemaphoreType.DMA((11,)),
+            pltpu.SemaphoreType.DMA((3,)),
         ],
         compiler_params=pltpu.CompilerParams(
             collective_id=1, has_side_effects=True, vmem_limit_bytes=58 * 2**20
         ),
-        cost_estimate=pl.CostEstimate(flops=0, bytes_accessed=280 * 10**6, transcendentals=0),
+        cost_estimate=pl.CostEstimate(flops=0, bytes_accessed=180 * 10**6, transcendentals=0),
         name="reduce_weights",
-    )(
-        first.reshape(torus + (rows, width)),
-        second.reshape(torus + (rows, width)),
-        small.reshape(torus + (2,) + small_shape),
-    )
+    )(acc, mid, small.reshape(torus + (2,) + small_shape))
 
 
 def sum_kernel(in_ref, out_ref, slots, send, recv):
@@ -869,51 +879,436 @@
     )(final_low, codes, weights, table)
 
 
-def grads_kernel(dqkv_ref, dmid_ref, dup_ref, act_ref, a_ref, o_ref, m_ref, dz_ref, out_ref):
+G1, S1, BQ, BV, BPROJ, G2, S2, BFC, BOUT = 0, 1, 2, 3, 4, 5, 6, 7, 11
+STEPS = 12
+GELU_A, GELU_B = 0.7978845608028654, 0.044715
+
+
+def across_k(left, right):
+    return lax.dot_general(left, right, (((1,), (1,)), ((), ())), preferred_element_type=jnp.float32)
+
+
+def along_k(left, right):
+    return jnp.dot(left, right, preferred_element_type=jnp.float32)
+
+
+def over_rows(left, right):
+    return lax.dot_general(left, right, (((0,), (0,)), ((), ())), preferred_element_type=jnp.float32)
+
+
+def normed(value):
+    centered = value - jnp.mean(value, -1, keepdims=True)
+    scale = lax.rsqrt(jnp.mean(centered * centered, -1, keepdims=True) + norm_eps)
+    return centered * scale, scale
+
+
+def norm_back(grad, value, gain):
+    unit, scale = normed(value)
+    inner = grad * gain
+    mean = jnp.mean(inner, -1, keepdims=True)
+    slope = jnp.mean(inner * unit, -1, keepdims=True)
+    return (
+        scale * (inner - mean - unit * slope),
+        jnp.sum(grad * unit, 0, keepdims=True),
+        jnp.sum(grad, 0, keepdims=True),
+    )
+
+
+def forward_kernel(
+    hot_ref,
+    rows_ref,
+    pos_hot_ref,
+    pos_ref,
+    mask_ref,
+    vec_ref,
+    w_ref,
+    x_out,
+    a_out,
+    qkv_out,
+    probs_out,
+    o_out,
+    mid_out,
+    m_out,
+    u_out,
+    g_out,
+    hidden_out,
+    final_out,
+    cur,
+):
     step = pl.program_id(0)
-
-    def put(left, right):
-        out_ref[...] = lax.dot_general(
-            left[...], right[...], (((0,), (0,)), ((), ())), preferred_element_type=jnp.float32
-        ).astype(out_ref.dtype)
-
-    pl.when(step < 3)(lambda: put(dqkv_ref, a_ref))
-    pl.when(step == 3)(lambda: put(dmid_ref, o_ref))
-    pl.when((step >= 4) & (step < 8))(lambda: put(dup_ref, m_ref))
-    pl.when(step >= 8)(lambda: put(act_ref, dz_ref))
-
-
-def weight_grads(dqkv, dmid, dup, act, a, o, m, dz):
-    tok, width = a.shape
-
-    def piece(first, count):
-        return pl.BlockSpec((tok, width), lambda i: (0, jnp.clip(i - first, 0, count - 1)))
-
-    whole = pl.BlockSpec((tok, width), lambda i: (0, 0))
-    steps = 12
+    layer, s = lax.div(step, STEPS), lax.rem(step, STEPS)
+    low, f32 = jnp.bfloat16, jnp.float32
+    width = cur.shape[1]
+    head_dim = width // H
+
+    def vec(row):
+        return vec_ref[layer * STEPS + row]
+
+    @pl.when(step == 0)
+    def embed():
+        cur[...] = along_k(hot_ref[...], rows_ref[...]) + across_k(pos_hot_ref[...], pos_ref[...])
+
+    @pl.when(s == 0)
+    def first_norm():
+        x_out[layer] = cur[...]
+        a_out[layer] = (normed(cur[...])[0] * vec(G1) + vec(S1)).astype(low)
+
+    @pl.when(s < 3)
+    def project():
+        bias = jnp.where(s == 0, vec(BQ), jnp.where(s == 2, vec(BV), 0.0))
+        qkv_out[layer, s] = (across_k(a_out[layer], w_ref[...]) + bias).astype(low)
+
+    @pl.when(s == 2)
+    def attend():
+        lanes = lax.broadcasted_iota(jnp.int32, (1, 2 * head_dim), 1)
+        for pair in range(H // 2):
+            cols = slice(2 * head_dim * pair, 2 * head_dim * (pair + 1))
+            q, k, v = (qkv_out[layer, part, :, cols] for part in range(3))
+            total = None
+            for side in range(2):
+                own = (lanes < head_dim) if side == 0 else (lanes >= head_dim)
+                scores = across_k(jnp.where(own, q, jnp.zeros_like(q)), k) * head_dim ** (-0.5)
+                scores = jnp.where(mask_ref[...] > 0.0, scores, -1000000000.0)
+                shifted = jnp.exp(scores - jnp.max(scores, -1, keepdims=True))
+                probs = shifted / jnp.sum(shifted, -1, keepdims=True)
+                probs_out[layer, 2 * pair + side] = probs
+                term = along_k(probs.astype(low), jnp.where(own, v, jnp.zeros_like(v)))
+                total = term if total is None else total + term
+            o_out[layer, :, cols] = total.astype(low)
+
+    @pl.when(s == 3)
+    def second_norm():
+        mid = cur[...] + across_k(o_out[layer], w_ref[...]) + vec(BPROJ)
+        mid_out[layer] = mid
+        m_out[layer] = (normed(mid)[0] * vec(G2) + vec(S2)).astype(low)
+        cur[...] = mid + vec(BOUT)
+
+    @pl.when((s >= 4) & (s < 8))
+    def widen():
+        u = across_k(m_out[layer], w_ref[...]) + vec(BFC + s - 4)
+        u_out[layer, s - 4] = u
+        g = 0.5 * u * (1.0 + jnp.tanh(GELU_A * (u + GELU_B * (u * u * u))))
+        g_out[layer, s - 4] = g.astype(low)
+
+    @pl.when(s >= 8)
+    def narrow():
+        cur[...] += along_k(g_out[layer, s - 8], w_ref[...])
+
+    @pl.when(step == 2 * STEPS - 1)
+    def last_norm():
+        hidden_out[...] = cur[...]
+        final_out[...] = (normed(cur[...])[0] * vec_ref[2 * STEPS] + vec_ref[2 * STEPS + 1]).astype(low)
+
+
+def forward_layers(hot, rows, pos_hot, pos, mask, vecs, mats):
+    tok, width = hot.shape[0], rows.shape[1]
+    low, f32 = jnp.bfloat16, jnp.float32
+    shape = jax.ShapeDtypeStruct
+    vmem = pl.BlockSpec(memory_space=pltpu.VMEM)
     return pl.pallas_call(
-        grads_kernel,
-        grid=(steps,),
-        out_shape=jax.ShapeDtypeStruct((steps * width, width), jnp.bfloat16),
-        in_specs=[piece(0, 3), piece(3, 1), piece(4, 4), piece(8, 4)] + [whole] * 4,
-        out_specs=pl.BlockSpec((width, width), lambda i: (i, 0)),
+        forward_kernel,
+        grid=(2 * STEPS,),
+        out_shape=(
+            shape((2, tok, width), f32),
+            shape((2, tok, width), low),
+            shape((2, 3, tok, width), low),
+            shape((2, H, tok, tok), f32),
+            shape((2, tok, width), low),
+            shape((2, tok, width), f32),
+            shape((2, tok, width), low),
+            shape((2, 4, tok, width), f32),
+            shape((2, 4, tok, width), low),
+            shape((tok, width), f32),
+            shape((tok, width), low),
+        ),
+        in_specs=[vmem] * 6 + [pl.BlockSpec((width, width), lambda i: (i, 0))],
+        out_specs=(vmem,) * 11,
+        scratch_shapes=[pltpu.VMEM((tok, width), f32)],
+        compiler_params=pltpu.CompilerParams(vmem_limit_bytes=58 * 2**20),
         cost_estimate=pl.CostEstimate(
-            flops=2 * tok * steps * width * width,
-            bytes_accessed=2 * steps * width * width,
-            transcendentals=0,
+            flops=2 * tok * mats.size, bytes_accessed=2 * mats.size, transcendentals=0
         ),
-        name="weight_grads",
-    )(dqkv, dmid, dup, act, a, o, m, dz)
-
-
-def layer_norm(inputs, gain, shift):
-    centered = inputs - jnp.mean(inputs, -1, keepdims=True)
-    spread = jnp.mean(centered * centered, -1, keepdims=True)
-    return centered * lax.rsqrt(spread + norm_eps) * gain + shift
-
-
-def gelu_tanh(inputs):
-    return jax.nn.gelu(inputs, approximate=True)
+        name="forward_layers",
+    )(hot, rows, pos_hot, pos, mask, vecs, mats)
+
+
+def backward_kernel(
+    grad_ref,
+    hidden_ref,
+    vec_ref,
+    x_ref,
+    a_ref,
+    qkv_ref,
+    probs_ref,
+    o_ref,
+    mid_ref,
+    m_ref,
+    u_ref,
+    g_ref,
+    w_ref,
+    dx_out,
+    vec_out,
+    acc_out,
+    sums_out,
+    cur,
+    wide,
+    du_s,
+    dqkv_s,
+    left_s,
+    right_s,
+    own_s,
+    send_s,
+    recv_s,
+    acc_0,
+    acc_1,
+    level_1,
+    half_0,
+    full_0,
+    send,
+    recv,
+    send_pair,
+    recv_pair,
+    local,
+):
+    step = pl.program_id(0)
+    layer, s = 1 - lax.div(step, STEPS), lax.rem(step, STEPS)
+    low, f32 = jnp.bfloat16, jnp.float32
+    tok, width = cur.shape
+    half = width // 2
+    head_dim = width // H
+    at, core = place()
+    sibling = device_at(at, 1 - core)
+    sums = Reduction(at, core, send, recv)
+    sums.level = {(0, 1): acc_1, 1: level_1}
+    sums.halves, sums.fulls = {0: half_0}, {0: full_0}
+    last = 2 * STEPS
+
+    def vec(row):
+        return vec_ref[layer * STEPS + row]
+
+    def put(row, value):
+        vec_out[layer * STEPS + row] = value
+
+    def pair_copy(slot):
+        return pltpu.make_async_remote_copy(
+            src_ref=send_s.at[slot],
+            dst_ref=recv_s.at[slot],
+            send_sem=send_pair.at[slot],
+            recv_sem=recv_pair.at[slot],
+            device_id=sibling,
+            device_id_type=pl.DeviceIdType.MESH,
+        )
+
+    def set_right(value):
+        right_s[:, :half] = jnp.where(core == 0, value[:, :half], value[:, half:])
+        right_s[:, half:] = jnp.where(core == 0, value[:, half:], value[:, :half])
+
+    @pl.when(step == 0)
+    def enter():
+        greet(neighbours(at, core))
+        dx, dg, ds = norm_back(grad_ref[...], hidden_ref[...], vec_ref[last])
+        cur[...] = dx
+        vec_out[last] = dg
+        vec_out[last + 1] = ds
+
+    def collect(acc, before):
+        slot, b = lax.rem(before, 2), lax.rem(before, STEPS)
+        tile = jnp.where(b < 4, 8 + b, jnp.where(b < 8, b, jnp.where(b == 8, 3, b - 9)))
+        pair_copy(slot).wait_recv()
+        rows, chunk = acc.shape[3], 16
+
+        def body(n, unused):
+            for u in range(4):
+                first = (n * 4 + u) * chunk
+                place_at = tile * width + first
+                block = lax.div(place_at, rows)
+                where = pl.ds(pl.multiple_of(lax.rem(place_at, rows), chunk), chunk)
+                here = pl.ds(pl.multiple_of(first, chunk), chunk)
+                value = own_s[here, :].astype(f32) + recv_s[slot, here, :].astype(f32)
+                acc[
+                    lax.div(block, RING * RING),
+                    lax.rem(lax.div(block, RING), RING),
+                    lax.rem(block, RING),
+                    where,
+                ] = value.astype(low)
+            return unused
+
+        lax.fori_loop(0, width // (4 * chunk), body, 0)
+
+    pl.when((step >= 1) & (step <= STEPS))(lambda: collect(acc_1, step - 1))
+    pl.when(step > STEPS)(lambda: collect(acc_0, step - 1))
+
+    pl.when(step == STEPS)(lambda: sums.start(1, 0))
+    pl.when(step == STEPS + 4)(lambda: sums.turn(1, 0))
+
+    @pl.when((s == 0) & (step < last))
+    def begin():
+        put(BOUT, jnp.sum(cur[...], 0, keepdims=True))
+        set_right(cur[...].astype(low))
+        wide[...] = cur[...].astype(low)
+
+    @pl.when((s < 4) & (step < last))
+    def through_gelu():
+        dg = across_k(wide[...], w_ref[...])
+        u = u_ref[layer, s]
+        square = u * u
+        t = jnp.tanh(GELU_A * (u + GELU_B * (square * u)))
+        slope = 0.5 * (1.0 + t) + (0.5 * GELU_A) * u * (1.0 - t * t) * (1.0 + (3.0 * GELU_B) * square)
+        du = dg * slope
+        put(BFC + s, jnp.sum(du, 0, keepdims=True))
+        du_s[s] = du.astype(low)
+        left_s[...] = g_ref[layer, s]
+
+    @pl.when(s == 4)
+    def begin_fc():
+        set_right(m_ref[layer])
+        dx_out[...] = jnp.zeros_like(dx_out)
+
+    @pl.when((s >= 4) & (s < 8))
+    def through_fc():
+        left = du_s[s - 4]
+        dx_out[...] += along_k(left, w_ref[...])
+        left_s[...] = left
+
+    @pl.when(s == 8)
+    def through_attention():
+        dx, dg, ds = norm_back(dx_out[...], mid_ref[layer], vec(G2))
+        put(G2, dg)
+        put(S2, ds)
+        cur[...] = cur[...] + dx
+        put(BPROJ, jnp.sum(cur[...], 0, keepdims=True))
+        mid_low = cur[...].astype(low)
+        left_s[...] = mid_low
+        set_right(o_ref[layer])
+        wide[...] = along_k(mid_low, w_ref[...]).astype(low)
+        lanes = lax.broadcasted_iota(jnp.int32, (1, 2 * head_dim), 1)
+        scale = head_dim ** (-0.5)
+        for pair in range(H // 2):
+            cols = slice(2 * head_dim * pair, 2 * head_dim * (pair + 1))
+            q, k, v = (qkv_ref[layer, part, :, cols] for part in range(3))
+            do = wide[:, cols]
+            parts = [None] * 3
+            for side in range(2):
+                own = (lanes < head_dim) if side == 0 else (lanes >= head_dim)
+                keep = lambda item, own=own: jnp.where(own, item, jnp.zeros_like(item))
+                probs = probs_ref[layer, 2 * pair + side]
+                do_own = keep(do)
+                dprobs = across_k(do_own, v)
+                dscores = probs * (dprobs - jnp.sum(probs * dprobs, -1, keepdims=True))
+                dlow = (dscores * scale).astype(low)
+                terms = (
+                    along_k(dlow, keep(k)),
+                    over_rows(dlow, keep(q)),
+                    over_rows(probs.astype(low), do_own),
+                )
+                parts = [
+                    term if held is None else held + term for held, term in zip(parts, terms)
+                ]
+            for part in range(3):
+                dqkv_s[part, :, cols] = parts[part].astype(low)
+            vec_out[layer * STEPS + BQ, :, cols] = jnp.sum(parts[0], 0, keepdims=True)
+            vec_out[layer * STEPS + BV, :, cols] = jnp.sum(parts[2], 0, keepdims=True)
+
+    @pl.when(s == 9)
+    def begin_qkv():
+        set_right(a_ref[layer])
+        dx_out[...] = jnp.zeros_like(dx_out)
+
+    @pl.when(s >= 9)
+    def through_qkv():
+        left = dqkv_s[s - 9]
+        dx_out[...] += along_k(left, w_ref[...])
+        left_s[...] = left
+
+    @pl.when(step < last)
+    def gradient():
+        slot = lax.rem(step, 2)
+        grad = over_rows(left_s[...], right_s[...])
+        pl.when(step >= 2)(lambda: pair_copy(slot).wait_send())
+        own_s[...] = grad[:, :half].astype(low)
+        send_s[slot] = grad[:, half:].astype(low)
+        pair_copy(slot).start()
+
+    @pl.when(s == STEPS - 1)
+    def end_layer():
+        dx, dg, ds = norm_back(dx_out[...], x_ref[layer], vec(G1))
+        put(G1, dg)
+        put(S1, ds)
+        cur[...] = cur[...] + dx
+
+    @pl.when(step == last)
+    def leave():
+        copy_acc = pltpu.make_async_copy(acc_0, acc_out, local.at[0])
+        copy_acc.start()
+        dx_out[...] = cur[...]
+        sums.finish(1, 0)
+        copy_sums = pltpu.make_async_copy(level_1.at[0], sums_out, local.at[1])
+        copy_sums.start()
+        for slot in range(2):
+            pair_copy(slot).wait_send()
+        sums.drain(1, 0)
+        copy_acc.wait()
+        copy_sums.wait()
+
+
+def backward_layers(grad, hidden, vecs, saved, mats):
+    tok, width = grad.shape
+    low, f32 = jnp.bfloat16, jnp.float32
+    shape = jax.ShapeDtypeStruct
+    vmem = pl.BlockSpec(memory_space=pltpu.VMEM)
+    hbm = pl.BlockSpec(memory_space=pltpu.HBM)
+    torus, half, rows = (RING, RING, RING), width // 2, 144
+    part = rows // 3
+
+    def tile(i):
+        i = jnp.minimum(i, 2 * STEPS - 1)
+        layer, s = 1 - i // STEPS, i % STEPS
+        return (
+            layer * STEPS
+            + jnp.where(s < 4, 8 + s, jnp.where(s < 8, s, jnp.where(s == 8, 3, s - 9))),
+            0,
+        )
+
+    return pl.pallas_call(
+        backward_kernel,
+        grid=(2 * STEPS + 1,),
+        out_shape=(
+            shape((tok, width), f32),
+            shape((2 * STEPS + 2, 1, width), f32),
+            shape(torus + (rows, half), low),
+            shape((3, RING, RING, part, half), low),
+        ),
+        in_specs=[vmem] * 12 + [pl.BlockSpec((width, width), tile)],
+        out_specs=(vmem, vmem, hbm, hbm),
+        scratch_shapes=[
+            pltpu.VMEM((tok, width), f32),
+            pltpu.VMEM((tok, width), low),
+            pltpu.VMEM((4, tok, width), low),
+            pltpu.VMEM((3, tok, width), low),
+            pltpu.VMEM((tok, width), low),
+            pltpu.VMEM((tok, width), low),
+            pltpu.VMEM((width, half), low),
+            pltpu.VMEM((2, width, half), low),
+            pltpu.VMEM((2, width, half), low),
+            pltpu.VMEM(torus + (rows, half), low),
+            pltpu.VMEM(torus + (rows, half), low),
+            pltpu.VMEM((1, 3, RING, RING, part, half), low),
+            pltpu.VMEM((1, 3, 2, 2, RING, part, half), low),
+            pltpu.VMEM((1, 3, 2, RING, RING, part, half), low),
+            pltpu.SemaphoreType.DMA((12,)),
+            pltpu.SemaphoreType.DMA((12,)),
+            pltpu.SemaphoreType.DMA((2,)),
+            pltpu.SemaphoreType.DMA((2,)),
+            pltpu.SemaphoreType.DMA((2,)),
+        ],
+        compiler_params=pltpu.CompilerParams(
+            collective_id=4, has_side_effects=True, vmem_limit_bytes=60 * 2**20
+        ),
+        cost_estimate=pl.CostEstimate(
+            flops=4 * tok * mats.size, bytes_accessed=2 * mats.size, transcendentals=0
+        ),
+        name="backward_layers",
+    )(grad, hidden, vecs, *saved, mats)
 
 
 def doc_info(doc_lens, tok_count, total_docs):
@@ -937,122 +1332,6 @@
     return lax.dot_general(
         left, right, (((left_dim,), (right_dim,)), ((), ())), preferred_element_type=jnp.float32
     )
-
-
-def split_vecs(vecs, width):
-    pieces = [vecs[index * width : (index + 1) * width] for index in range(7)]
-    ff_width = vecs.shape[0] - 8 * width
-    pieces.append(vecs[7 * width : 7 * width + ff_width])
-    pieces.append(vecs[7 * width + ff_width :])
-    return pieces
-
-
-def split_mats(mats, width):
-    ff_width = (mats.shape[0] - 4 * width) // 2
-    cuts = [0, 3 * width, 4 * width, 4 * width + ff_width, 4 * width + 2 * ff_width]
-    return [mats[a:b] for a, b in zip(cuts[:-1], cuts[1:])]
-
-
-def layer_forward(hidden, mats, vecs, attn_mask):
-    tok, width = hidden.shape
-    head_dim = width // H
-    w_qkv, w_proj, w_fc, w_out = split_mats(mats, width)
-    gain_one, shift_one, bias_q, bias_v, bias_proj, gain_two, shift_two, bias_fc, bias_out = (
-        split_vecs(vecs, width)
-    )
-    normed_low = layer_norm(hidden, gain_one, shift_one).astype(jnp.bfloat16)
-    bias_qkv = jnp.concatenate([bias_q, jnp.zeros_like(bias_q), bias_v])
-    qkv_f = contract(normed_low, w_qkv, 1, 1) + bias_qkv
-    qkv_low = qkv_f.astype(jnp.bfloat16).reshape(tok, 3, H, head_dim)
-    scores = jnp.einsum(
-        "thd,uhd->htu", qkv_low[:, 0], qkv_low[:, 1], preferred_element_type=jnp.float32
-    ) * head_dim ** (-0.5)
-    scores = jnp.where(attn_mask[None], scores, -1000000000.0)
-    shifted = jnp.exp(scores - jnp.max(scores, -1, keepdims=True))
-    attn_probs = shifted / jnp.sum(shifted, -1, keepdims=True)
-    probs_low = attn_probs.astype(jnp.bfloat16)
-    attended = jnp.einsum(
-        "htu,uhd->thd", probs_low, qkv_low[:, 2], preferred_element_type=jnp.float32
-    )
-    attended = attended.reshape(tok, width).astype(jnp.bfloat16)
-    middle = hidden + contract(attended, w_proj, 1, 1) + bias_proj
-    two_low = layer_norm(middle, gain_two, shift_two).astype(jnp.bfloat16)
-    up_act = contract(two_low, w_fc, 1, 1) + bias_fc
-    activ_low = gelu_tanh(up_act).astype(jnp.bfloat16)
-    output = middle + contract(activ_low, w_out, 1, 0) + bias_out
-    saved = (
-        hidden,
-        normed_low,
-        qkv_low,
-        attn_probs,
-        probs_low,
-        attended,
-        middle,
-        two_low,
-        up_act,
-        activ_low,
-    )
-    return (output, saved)
-
-
-def layer_backward(saved, mats, vecs, grad_out):
-    hidden, normed_low, qkv_low, attn_probs, probs_low, attended, middle, two_low, up_act, activ_low = saved
-    tok, width = hidden.shape
-    head_dim = width // H
-    w_qkv, w_proj, w_fc, w_out = split_mats(mats, width)
-    gain_one, shift_one, bias_q, bias_v, bias_proj, gain_two, shift_two, bias_fc, bias_out = (
-        split_vecs(vecs, width)
-    )
-    low = jnp.bfloat16
-    out_low = grad_out.astype(low)
-    grad_bout = jnp.sum(grad_out, 0)
-    grad_act = contract(out_low, w_out, 1, 1)
-    unused_up, gelu_pull = jax.vjp(gelu_tanh, up_act)
-    grad_up = gelu_pull(grad_act)[0]
-    up_low = grad_up.astype(low)
-    grad_bfc = jnp.sum(grad_up, 0)
-    grad_two = contract(up_low, w_fc, 1, 0)
-    unused_two, norm_pull = jax.vjp(layer_norm, middle, gain_two, shift_two)
-    grad_mid_norm, grad_g2, grad_s2 = norm_pull(grad_two)
-    grad_mid = grad_out + grad_mid_norm
-    mid_low = grad_mid.astype(low)
-    grad_bproj = jnp.sum(grad_mid, 0)
-    grad_att = contract(mid_low, w_proj, 1, 0).astype(low).reshape(tok, H, head_dim)
-    grad_probs = jnp.einsum(
-        "thd,uhd->htu", grad_att, qkv_low[:, 2], preferred_element_type=jnp.float32
-    )
-    grad_vals = jnp.einsum("htu,thd->uhd", probs_low, grad_att, preferred_element_type=jnp.float32)
-    grad_scores = attn_probs * (grad_probs - jnp.sum(attn_probs * grad_probs, -1, keepdims=True))
-    score_low = (grad_scores * head_dim ** (-0.5)).astype(low)
-    grad_q = jnp.einsum(
-        "htu,uhd->thd", score_low, qkv_low[:, 1], preferred_element_type=jnp.float32
-    )
-    grad_k = jnp.einsum(
-        "htu,thd->uhd", score_low, qkv_low[:, 0], preferred_element_type=jnp.float32
-    )
-    grad_qkv = jnp.stack([grad_q, grad_k, grad_vals], 1).reshape(tok, 3 * width)
-    qkv_grad_low = grad_qkv.astype(low)
-    grad_normed = contract(qkv_grad_low, w_qkv, 1, 0)
-    unused_one, first_pull = jax.vjp(layer_norm, hidden, gain_one, shift_one)
-    grad_in_norm, grad_g1, grad_s1 = first_pull(grad_normed)
-    grad_in = grad_mid + grad_in_norm
-    grad_mats = weight_grads(
-        qkv_grad_low, mid_low, up_low, activ_low, normed_low, attended, two_low, out_low
-    )
-    grad_vecs = jnp.concatenate(
-        [
-            grad_g1,
-            grad_s1,
-            jnp.sum(grad_q, 0).reshape(width),
-            jnp.sum(grad_vals, 0).reshape(width),
-            grad_bproj,
-            grad_g2,
-            grad_s2,
-            grad_bfc,
-            grad_bout,
-        ]
-    )
-    return (grad_in, grad_mats, grad_vecs)
 
 
 def renew(weight, moment, average, grad, factor):
@@ -1096,7 +1375,6 @@
     data_at = lax.axis_index("dp")
     tok = token_ids.shape[0]
     own_rows, width = embed_table.shape
-    layers = blocks.shape[0]
     capacity = max(2, 2 * tok // devices)
     low = jnp.bfloat16
     blocks, block_moment, block_average = (
@@ -1120,7 +1398,6 @@
     local_rows = lax.all_to_all(send_rows, ("dp", "vocab"), split_axis=0, concat_axis=0, tiled=True)
     asked = (local_rows[:, None] == jnp.arange(own_rows, dtype=jnp.int32)[None, :]).astype(low)
     fetched = jnp.dot(asked, table_low, preferred_element_type=jnp.float32).astype(low)
-    blocks, fetched = lax.optimization_barrier((blocks, fetched))
     returned_rows = lax.all_to_all(
         fetched.reshape(devices, capacity, width),
         ("dp", "vocab"),
@@ -1128,6 +1405,7 @@
         concat_axis=0,
         tiled=True,
     ).reshape(devices * capacity, width)
+    blocks, returned_rows = lax.optimization_barrier((blocks, returned_rows))
     table_slice = lax.all_gather(table_padded, "dp", axis=0, tiled=True)
     target_owners = targets // own_rows
     codes = (
@@ -1147,8 +1425,6 @@
         .reshape(-1)
         .astype(jnp.float32)
     )
-    vec_width = (vecs_all.shape[0] - 2 * width) // layers
-
     lens_group = lengths[0]
     seg_group, pos_group, weight_group = jax.vmap(
         partial(doc_info, tok_count=tok, total_docs=devices * lens_group.shape[1])
@@ -1159,20 +1435,17 @@
     places = jnp.arange(tok, dtype=jnp.int32)
     attn_mask = (seg_ids[:, None] == seg_ids[None, :]) & (places[None, :] <= places[:, None])
 
-    gotten = jnp.dot(slot_hot, returned_rows, preferred_element_type=jnp.float32)
     pos_hot = (pos_ids[:, None] == jnp.arange(pos_rows, dtype=jnp.int32)[None, :]).astype(low)
-    hidden = gotten + contract(pos_hot, pos_low_t, 1, 1)
-    kept = []
-    for layer in range(layers):
-        hidden, saved = layer_forward(
-            hidden,
-            mats_all[layer],
-            vecs_all[layer * vec_width : (layer + 1) * vec_width],
-            attn_mask,
-        )
-        kept.append(saved)
-    tail = vecs_all[layers * vec_width :]
-    final_low = layer_norm(hidden, tail[:width], tail[width:]).astype(low)
+    vec_rows = vecs_all.reshape(-1, 1, width)
+    *saved, hidden, final_low = forward_layers(
+        slot_hot,
+        returned_rows,
+        pos_hot,
+        pos_low_t,
+        attn_mask.astype(jnp.float32),
+        vec_rows,
+        mats_all,
+    )
     grad_final, table_part, token_losses = head(
         final_low, jnp.broadcast_to(codes[None, :], (8, tok)), weight_group, table_slice
     )
@@ -1180,18 +1453,9 @@
     table_grad = lax.psum_scatter(table_part, "dp", scatter_dimension=0, tiled=True)[
         :own_rows
     ].astype(jnp.float32)
-    unused_final, final_pull = jax.vjp(layer_norm, hidden, tail[:width], tail[width:])
-    grad_hidden, grad_gf, grad_sf = final_pull(grad_final)
-    mats_parts = [None] * layers
-    vec_parts = [None] * layers
-    for layer in reversed(range(layers)):
-        grad_hidden, mats_parts[layer], vec_parts[layer] = layer_backward(
-            kept[layer],
-            mats_all[layer],
-            vecs_all[layer * vec_width : (layer + 1) * vec_width],
-            grad_hidden,
-        )
-    grad_vec_all = jnp.concatenate(vec_parts + [grad_gf, grad_sf])
+    grad_hidden, grad_vecs, grad_acc, grad_sums = backward_layers(
+        grad_final, hidden, vec_rows, saved, mats_all
+    )
     grad_pos = lax.dot_general(
         grad_hidden,
         pos_hot.astype(jnp.float32),
@@ -1199,7 +1463,7 @@
         precision=lax.Precision.HIGHEST,
     )
     send_grads = contract(slot_hot, grad_hidden.astype(low), 0, 0).astype(low)
-    mats_parts[0], send_grads = lax.optimization_barrier((mats_parts[0], send_grads))
+    grad_acc, send_grads = lax.optimization_barrier((grad_acc, send_grads))
     back_grads = lax.all_to_all(
         send_grads.reshape(devices, capacity, width),
         ("dp", "vocab"),
@@ -1209,10 +1473,10 @@
     ).reshape(-1, width)
     small_grads = pack_small(
         jnp.concatenate(
-            [grad_pos.reshape(devices, -1), grad_vec_all.reshape(devices, -1)], 1
+            [grad_pos.reshape(devices, -1), grad_vecs.reshape(devices, -1)], 1
         )
     )
-    mats_shard, small_shard = reduce_weights(mats_parts[0], mats_parts[1], small_grads)
+    mats_shard, small_shard = reduce_weights(grad_acc, grad_sums, small_grads)
     small_shard = small_shard.reshape(-1)
     pos_shard = small_shard[: pos_rows * pos_cols].reshape(pos_cols, pos_rows)
     vec_shard = small_shard[pos_rows * pos_cols : pos_rows * pos_cols + vec_own]

time: 546 us -> 496 us (0.908)
  matrix products: 97.1 us -> 4.65 us
  Pallas kernels: 307 us -> 397 us
  local copies, waits for them, and re-layouts: 47.1 us -> 12.6 us
  other arithmetic: 35.1 us -> 21.6 us
  waiting for transfers between devices: 7.5 us -> 17.5 us
    pallas_call x3, Pallas kernels: 135 us -> 232 us  [the longest x1 102 us: backward_layers(): pl.pallas_call(backward_kernel, grid=(2 * STEPS + 1,), out_shape=(shape((...]
    dot_general x19 -> x2, matrix products: 60.1 us -> 2.72 us  [contract(): lax.dot_general(left, right, (((left_dim,), (right_dim,)), ((), ())), pre...]
    dot_general x11 -> x0, matrix products: 30.1 us -> none  [the longest x2 7.22 us: layer_backward(): jnp.einsum('htu,uhd->thd', score_low, qkv_low[:, 1], preferred_element_ty...]
    convert_element_type x8 -> x0, local copies, waits for them, and re-layouts: 15.5 us -> none  [the longest x2 4.3 us: layer_backward(): qkv_grad_low = grad_qkv.astype(low)]
    unnamed x258 -> x47, local copies, waits for them, and re-layouts: 11.7 us -> 2.6 us
    all_to_all x1, waiting for transfers between devices: 1.63 us -> 10.6 us  [per_device(): lax.all_to_all(fetched.reshape(devices, capacity, width), ('dp', 'vocab')...]
    slice x4 -> x0, local copies, waits for them, and re-layouts: 8.21 us -> none  [the longest x2 6.21 us: split_mats(): return [mats[a:b] for a, b in zip(cuts[:-1], cuts[1:])]]
    pallas_call x1, Pallas kernels: 79 us -> 72 us  [reduce_weights(): pl.pallas_call(reduce_kernel, out_shape=(jax.ShapeDtypeStruct((2, rows //...]
  transfers between devices with their start and end apart: 5 -> 5, of which waited for: 2 -> 2; matrix products, arithmetic and copies ran while one was open for 28% -> 4% of each run, Pallas kernels for 40% -> 61%
where the time goes in v3:
time: 496 us; the launch traced here: 495 us
  Pallas kernels  397 us (80%)
  starting transfers between devices  22.8 us (5%)
  other arithmetic  21.6 us (4%)
  between operations  18.9 us (4%)
  waiting for transfers between devices  17.5 us (4%)
  local copies, waits for them, and re-layouts  12.6 us (3%)
    pallas_call x1, Pallas kernels, backward_layers(): pl.pallas_call(backward_kernel, grid=(2 * STEPS + 1,), out_shape=(shape((...  102 us
    pallas_call x1, Pallas kernels, gather_weights(): pl.pallas_call(gather_kernel, out_shape=(whole, jax.ShapeDtypeStruct((RIN...  96.8 us
    pallas_call x1, Pallas kernels, head(): pl.pallas_call(head_kernel, out_shape=(jax.ShapeDtypeStruct((tok, width),...  78.9 us
    pallas_call x1, Pallas kernels, reduce_weights(): pl.pallas_call(reduce_kernel, out_shape=(jax.ShapeDtypeStruct((2, rows //...  72 us
    pallas_call x1, Pallas kernels, forward_layers(): pl.pallas_call(forward_kernel, grid=(2 * STEPS,), out_shape=(shape((2, to...  33.2 us
    pallas_call x1, Pallas kernels, sum_all(): pl.pallas_call(sum_kernel, out_shape=jax.ShapeDtypeStruct(value.shape, jn...  14.2 us
    all_to_all x1, starting transfers between devices, per_device(): lax.all_to_all(send_rows, ('dp', 'vocab'), split_axis=0, concat_axis=0, t...  11.1 us
    all_to_all x1, waiting for transfers between devices, per_device(): lax.all_to_all(fetched.reshape(devices, capacity, width), ('dp', 'vocab')...  10.6 us
  transfers between devices with their start and end apart: 5, of which 2 were waited for; matrix products, arithmetic and copies ran while one was open for 4% of the time, Pallas kernels for 61%

profile of v3, /device:TPU:0, one launch (start us, length us, event | category | flops | bytes accessed | tf_op | source)
XLA Modules:
  0.0 495.1 jit_solution(8614423015606730660)
XLA Ops:
  7.2 1.4 convert_element_type.78
  10.6 11.1 %all-to-all-start = ((s32[128,2,1]{1,2,0:T(1,128)}), s32[128,2,1]{1,2,0:T(1,128)S(1)}, u32[]{:S(2)}, u32[]{:S(2)}) async-start(s32[128,2,1]{1,2,0:T(1,128)} %bitcast.1), calls=%async_computation | async-start | bytes 131072 | tf_op jit(solution)/shard_map/all_to_all | solution.py:1398
  24.1 6.9 %all-to-all-done = s32[128,2,1]{1,2,0:T(1,128)S(1)} async-done(((s32[128,2,1]{1,2,0:T(1,128)}), s32[128,2,1]{1,2,0:T(1,128)S(1)}, u32[]{:S(2)}, u32[]{:S(2)}) %all-to-all-start) | async-done | bytes 1056 | tf_op jit(solution)/shard_map/all_to_all | solution.py:1398
  33.8 4.8 all-to-all-start.1
  40.2 10.6 %all-to-all-done.1 = bf16[128,2,768]{2,1,0:T(2,128)(2,1)S(1)} async-done(((bf16[128,2,768]{2,1,0:T(2,128)(2,1)}), bf16[128,2,768]{2,1,0:T(2,128)(2,1)S(1)}, u32[]{:S(2)}, u32[]{:S(2)}) %all-to-all-start.1) | async-done | bytes 393248 | tf_op jit(solution)/shard_map/all_to_all | solution.py:1401
  51.6 96.8 %gather_weights.1 = (bf16[2,4,4,4,144,768]{5,4,3,2,1,0:T(8,128)(2,1)}, bf16[4,4,4,2,16,128]{5,4,3,2,1,0:T(8,128)(2,1)}) custom-call(f32[2,72,768]{2,1,0:T(8,128)} %bitcast.79, bf16[16,128]{1,0:T(8,128)(2,1)} %fusion.18.small_ref), custom_call_target="tpu_custom_call" | custom-call | bytes 250000000 | tf_op jit(solution)/shard_map/gather_weights/pallas_call | solution.py:199
  148.5 1.2 copy.61
  151.6 33.2 %forward_layers.1 = (f32[2,128,768]{2,1,0:T(8,128)}, bf16[2,128,768]{2,1,0:T(8,128)(2,1)}, bf16[2,3,128,768]{3,2,1,0:T(8,128)(2,1)}, f32[2,12,128,128]{3,2,1,0:T...) custom-call(bf16[128,256]{1,0:T(8,128)(2,1)} %fusion.7.hot_ref, ...), custom_call_target="tpu_custom_call" | custom-call | flops 3623878656 | bytes 28311552 | tf_op jit(solution)/shard_map/forward_layers/pallas_call | solution.py:1008
  185.4 78.9 %head.1 = (f32[128,768]{1,0:T(8,128)}, bf16[6400,768]{1,0:T(8,128)(2,1)}, f32[8,128]{1,0:T(8,128)}) custom-call(bf16[128,768]{1,0:T(8,128)(2,1)} %get-tuple-element.48.f_ref, s32[8,128]{1,0:T(8,128)} %broadcast_in_dim.38.code_ref, f32[8,128]{1,0:T(8,128)} %divide_multiply_fusion.weight_ref, bf16[6400,768]{1,0:T(8,128)(2,1)} %all-gather.2.cloned.1.call-done.table_ref), custom_call_target="tpu_custom_call" | custom-call | flops 30198988800 | bytes 19660800 | tf_op jit(solution)/shard_map/head/pallas_call | solution.py:843
  264.4 101.8 %backward_layers.1 = (f32[128,768]{1,0:T(8,128)}, f32[26,1,768]{2,1,0:T(1,128)}, bf16[4,4,4,144,384]{4,3,2,1,0:T(8,128)(2,1)}, bf16[3,4,4,48,384]{4,3,2,1,0:T(8,128)(2,1)}) custom-call(f32[128,768]{1,0:T(8,128)} %get-tuple-element.51.grad_ref, f32[128,768]{1,0:T(8,128)} %get-tuple-element.52.hidden_ref, f32[26,1,768]{2,1,0:T(1,128)} %reshape.131.vec_ref, ...), custom_call_target="tpu_custom_call" | custom-call | flops 7247757312 | bytes 28311552 | tf_op jit(solution)/shard_map/backward_layers/pallas_call | solution.py:1272
  366.2 1.1 reduce.2
  367.5 1.5 fusion.8
  370.5 6.8 %all-to-all-start.2 = ((bf16[128,2,768]{2,1,0:T(2,128)(2,1)}), bf16[128,2,768]{2,1,0:T(2,128)(2,1)S(1)}, u32[]{:S(2)}, u32[]{:S(2)}) async-start(bf16[128,2,768]{2,1,0:T(2,128)(2,1)} %reshape.125), calls=%async_computation.3 | async-start | bytes 786432 | tf_op jit(solution)/shard_map/all_to_all | solution.py:1467
  377.5 1.2 copy.56
  379.3 72.0 %reduce_weights.1 = (f32[2,72,768]{2,1,0:T(8,128)}, f32[16,128]{1,0:T(8,128)}) custom-call(bf16[4,4,4,144,384]{4,3,2,1,0:T(8,128)(2,1)} %get-tuple-element.65.acc_ref, bf16[3,4,4,48,384]{4,3,2,1,0:T(8,128)(2,1)} %get-tuple-element.66.mid_ref, f32[4,4,4,2,16,128]{5,4,3,2,1,0:T(8,128)} %bitcast.78), custom_call_target="tpu_custom_call" | custom-call | bytes 180000000 | tf_op jit(solution)/shard_map/reduce_weights/pallas_call | solution.py:517
  451.2 1.4 multiply_reduce_fusion.3
  452.6 1.3 multiply_reduce_fusion.2
  453.9 1.7 multiply_reduce_fusion.1
  455.8 2.4 multiply_reduce_fusion
  462.2 14.2 %sum_all.1 = f32[8,128]{1,0:T(8,128)} custom-call(f32[8,128]{1,0:T(8,128)} %broadcast_in_dim.40.in_ref), custom_call_target="tpu_custom_call" | custom-call | tf_op jit(solution)/shard_map/sum_all/pallas_call | solution.py:590
  476.4 1.3 fusion.29
  479.1 1.3 fusion.27
  484.1 1.5 fusion.28
  485.7 1.3 add_multiply_fusion
  (101 shorter events, 20.5 us)
Async XLA Ops:
  7.2 177.6 %all-gather.2.cloned.1.call-start = ((), (), s32[]{:S(2)}) async-start(), calls=%async_computation.4 | async-start | bytes 10444800 | tf_op jit(solution)/shard_map/all_gather | solution.py:1409
  8.6 13.2 %copy-start.12 = (s32[1,8,3]{1,0,2:T(1,128)S(1)}, s32[1,8,3]{1,0,2:T(1,128)}, u32[]{:S(2)}) copy-start(s32[1,8,3]{1,0,2:T(1,128)} %param.17) | copy-start | bytes 292
  8.6 15.5 %copy-start.11 = (f32[80,6]{0,1:T(8,128)S(1)}, f32[80,6]{0,1:T(8,128)}, u32[]{:S(2)}) copy-start(f32[80,6]{0,1:T(8,128)} %param.24) | copy-start | bytes 5764
  10.6 20.4 %all-to-all-start = ((s32[128,2,1]{1,2,0:T(1,128)}), s32[128,2,1]{1,2,0:T(1,128)S(1)}, u32[]{:S(2)}, u32[]{:S(2)}) async-start(s32[128,2,1]{1,2,0:T(1,128)} %bitcast.1), calls=%async_computation | async-start | bytes 131072 | tf_op jit(solution)/shard_map/all_to_all | solution.py:1398
  32.5 6.2 %copy-start.21 = (s32[128]{0:T(128)S(1)}, s32[128]{0:T(128)}, u32[]{:S(2)}) copy-start(s32[128]{0:T(128)} %param.16) | copy-start | bytes 1540
  32.5 6.2 %copy-start.18 = (f32[156]{0:T(256)S(1)}, f32[156]{0:T(256)}, u32[]{:S(2)}) copy-start(f32[156]{0:T(256)} %param.27) | copy-start | bytes 1876
  33.8 16.9 %all-to-all-start.1 = ((bf16[128,2,768]{2,1,0:T(2,128)(2,1)}), bf16[128,2,768]{2,1,0:T(2,128)(2,1)S(1)}, u32[]{:S(2)}, u32[]{:S(2)}) async-start(bf16[128,2,768]{2,1,0:T(2,128)(2,1)} %reshape.119), calls=%async_computation.1 | async-start | bytes 786432 | tf_op jit(solution)/shard_map/all_to_all | solution.py:1401
  38.6 417.2 %reduce-scatter.2.cloned.1.call-start = ((), (), s32[]{:S(2)}) async-start(), calls=%async_computation.5 | async-start | bytes 10444800 | tf_op jit(solution)/shard_map/reduce_scatter | solution.py:1453
  366.2 3.0 copy-start.5
  370.5 85.1 %all-to-all-start.2 = ((bf16[128,2,768]{2,1,0:T(2,128)(2,1)}), bf16[128,2,768]{2,1,0:T(2,128)(2,1)S(1)}, u32[]{:S(2)}, u32[]{:S(2)}) async-start(bf16[128,2,768]{2,1,0:T(2,128)(2,1)} %reshape.125), calls=%async_computation.3 | async-start | bytes 786432 | tf_op jit(solution)/shard_map/all_to_all | solution.py:1467
  455.8 23.3 %copy-start.19 = (f32[156]{0:T(256)S(1)}, f32[156]{0:T(256)}, u32[]{:S(2)}) copy-start(f32[156]{0:T(256)} %param.28) | copy-start | bytes 1876
  455.8 24.7 %copy-start.2 = (f32[2,768,72]{1,2,0:T(8,128)S(1)}, f32[2,768,72]{1,2,0:T(8,128)}, u32[]{:S(2)}) copy-start(f32[2,768,72]{1,2,0:T(8,128)} %param.21) | copy-start | bytes 1327108
  455.8 24.7 %copy-start.3 = (f32[2,72,768]{2,1,0:T(8,128)S(1)}, f32[2,72,768]{2,1,0:T(8,128)}, u32[]{:S(2)}) copy-start(f32[2,72,768]{2,1,0:T(8,128)} %get-tuple-element.68) | copy-start | bytes 1327108
  455.8 24.7 %copy-start.9 = (f32[2,768,72]{1,2,0:T(8,128)S(1)}, f32[2,768,72]{1,2,0:T(8,128)}, u32[]{:S(2)}) copy-start(f32[2,768,72]{1,2,0:T(8,128)} %param.22) | copy-start | bytes 1327108
  478.3 3.2 copy-start.17
  478.3 3.7 copy-start.16
  480.4 2.3 copy-start.15
  480.5 2.2 copy-start.13
  480.5 2.8 copy-start.8
  480.5 3.6 copy-start.7
  481.5 4.2 copy-start.4
  481.5 2.6 copy-start.1
  482.7 3.0 copy-start.10
  484.1 1.6 copy-start.6
  (3 other events, 3.5 us)
Sparse Core Ops, SparseCore 0:
  10.7 104.9 all-gather.1
  264.5 93.8 reduce-scatter.1

commit v4 on v3

--- a/solution.py
+++ b/solution.py
@@ -10,6 +10,7 @@
 H = 12
 RING = 4
 ORDERS = ((2, 1, 0), (1, 0, 2), (0, 2, 1))
+PARTS = ((0, 16), (16, 96), (112, 32))
 
 norm_eps = 1e-05
 clip_bound = 0.01
@@ -77,7 +78,6 @@
 ):
     at, core = place()
     rows, half = mine_ref.shape[1], mine_ref.shape[2] // 2
-    part = 2 * rows // 3
     sibling = device_at(at, 1 - core)
     greet(neighbours(at, core))
     wires = Wires(send, recv)
@@ -111,13 +111,15 @@
         index[order[phase]] = c
         for axis in order[:phase]:
             index[axis] = pl.ds(0, RING)
-        first, count = p * part, part
+        first, count = PARTS[p]
+        where = cols
         if piece is not None:
             if phase == 0:
-                first, count = (first, 32) if piece == 0 else (first + 32, part - 32)
+                cut, size = (0, half - 128) if piece == 0 else (half - 128, 128)
+                where = pl.ds(pl.multiple_of(core * half + cut, 128), size)
             else:
                 index[order[0]] = pl.ds(2 * piece, 2)
-        return out_ref.at[layer, index[0], index[1], index[2], pl.ds(first, count), cols]
+        return out_ref.at[layer, index[0], index[1], index[2], pl.ds(first, count), where]
 
     def small_bundle(phase, c):
         order = ORDERS[0]
@@ -259,7 +261,7 @@
             free, unused = self.axes(p)
             spot = [c, c, c]
             spot[free[0]], spot[free[1]] = cut, whole
-            return spot + [pl.ds(p * part, part)]
+            return spot + [p]
         if step == 1:
             unused, first = self.axes(p)
             spot = [cut, cut]
@@ -312,12 +314,8 @@
         held = self.level[0, layer] if step == 0 else self.level[step]
         index = self.index(layer, p, step, c, piece)
         sizes = [item[1] for item in index if isinstance(item, tuple)]
-        total = 1
-        for size in sizes:
-            total *= size
-
-        def body(n, unused):
-            inner = [lax.div(n, sizes[1]), lax.rem(n, sizes[1])] if len(sizes) == 2 else [n] * len(sizes)
+
+        def one(inner):
             places = iter(inner)
             spot = tuple(
                 item[0] + next(places) if isinstance(item, tuple) else item for item in index
@@ -326,12 +324,19 @@
             for term in terms:
                 value = value + term[tuple(inner) + (slice(None), slice(None))].astype(jnp.float32)
             into(held, spot, inner, value)
+
+        def body(n, unused):
+            if len(sizes) == 2:
+                for k in range(sizes[1]):
+                    one([n, k])
+            else:
+                one([n])
             return unused
 
-        if total == 1:
-            body(0, 0)
+        if sizes:
+            lax.fori_loop(0, sizes[0], body, 0)
         else:
-            lax.fori_loop(0, total, body, 0)
+            one([])
 
     def start(self, layer, step):
         for p in range(3):
@@ -414,9 +419,13 @@
 
     mid_load = pltpu.make_async_copy(mid_ref, mid.at[1], local.at[0])
     mid_load.start()
-    acc_load = pltpu.make_async_copy(acc_ref, acc, local.at[1])
-    acc_load.start()
-    small_load = pltpu.make_async_copy(small_ref.at[:, :, :, core], small_acc, local.at[2])
+    acc_loads = []
+    for n in range(RING * RING):
+        spot = (n // RING, n % RING)
+        op = pltpu.make_async_copy(acc_ref.at[spot], acc.at[spot], local.at[2 + n])
+        op.start()
+        acc_loads.append(op)
+    small_load = pltpu.make_async_copy(small_ref.at[:, :, :, core], small_acc, local.at[1])
     small_load.start()
     greet(neighbours(at, core))
     wires = Wires(send_small, recv_small)
@@ -462,24 +471,25 @@
             op.wait_recv()
         small_add(step, at[order[2 - step]], slots[step][1] + slots[step][2])
 
+    for op in acc_loads:
+        op.wait()
+    sums.start(0, 0)
     mid_load.wait()
     sums.start(1, 1)
-    acc_load.wait()
-    sums.start(0, 0)
     small_load.wait()
     small_swap.wait_recv()
     small_acc[...] = small_acc[...] + small_sib[...]
     op = small_start(0)
+    sums.turn(0, 0)
     sums.turn(1, 1)
+    ops = small_turn(0, op)
     sums.finish(1, 1)
     sums.start(1, 2)
-    sums.turn(0, 0)
-    ops = small_turn(0, op)
-    sums.turn(1, 2)
-    sums.finish(1, 2)
     small_finish(0, ops)
     op = small_start(1)
+    sums.turn(1, 2)
     ops = small_turn(1, op)
+    sums.finish(1, 2)
     small_finish(1, ops)
     op = small_start(2)
     ops = small_turn(2, op)
@@ -507,8 +517,8 @@
 
 
 def reduce_weights(acc, mid, small):
-    rows, half = acc.shape[3:]
-    part = rows // 3
+    part, half = acc.shape[4:]
+    rows = 3 * part
     torus = (RING, RING, RING)
     small_shape = small.shape[1:]
     hbm = pl.BlockSpec(memory_space=pltpu.HBM)
@@ -523,7 +533,7 @@
         in_specs=[hbm, hbm, hbm],
         out_specs=(vmem, vmem),
         scratch_shapes=[
-            pltpu.VMEM(torus + (rows, half), low),
+            pltpu.VMEM(torus + (3, part, half), low),
             pltpu.VMEM((2, 3, RING, RING, part, half), low),
             pltpu.VMEM((2, 3, RING, part, half), low),
             pltpu.VMEM((1, 3, 2, 2, RING, part, half), low),
@@ -543,7 +553,7 @@
             pltpu.SemaphoreType.DMA((60,)),
             pltpu.SemaphoreType.DMA((11,)),
             pltpu.SemaphoreType.DMA((11,)),
-            pltpu.SemaphoreType.DMA((3,)),
+            pltpu.SemaphoreType.DMA((2 + RING * RING,)),
         ],
         compiler_params=pltpu.CompilerParams(
             collective_id=1, has_side_effects=True, vmem_limit_bytes=58 * 2**20
@@ -879,6 +889,7 @@
     )(final_low, codes, weights, table)
 
 
+TILE_ORDER = (8, 9, 10, 11, 4, 5, 6, 7, 3, 0, 1, 2)
 G1, S1, BQ, BV, BPROJ, G2, S2, BFC, BOUT = 0, 1, 2, 3, 4, 5, 6, 7, 11
 STEPS = 12
 GELU_A, GELU_B = 0.7978845608028654, 0.044715
@@ -894,6 +905,26 @@
 
 def over_rows(left, right):
     return lax.dot_general(left, right, (((0,), (0,)), ((), ())), preferred_element_type=jnp.float32)
+
+
+def tile_across(left, tile):
+    return jnp.concatenate([across_k(left, block[...]) for block in tile], 1)
+
+
+def tile_along(left, tile):
+    total = None
+    for n, block in enumerate(tile):
+        rows = block.shape[0]
+        term = along_k(left[:, n * rows : (n + 1) * rows], block[...])
+        total = term if total is None else total + term
+    return total
+
+
+def tile_specs(width, tile):
+    return [
+        pl.BlockSpec((width // 3, width), lambda i, n=n: (3 * tile(i) + n, 0))
+        for n in range(3)
+    ]
 
 
 def normed(value):
@@ -921,7 +952,9 @@
     pos_ref,
     mask_ref,
     vec_ref,
-    w_ref,
+    w_0,
+    w_1,
+    w_2,
     x_out,
     a_out,
     qkv_out,
@@ -941,6 +974,8 @@
     width = cur.shape[1]
     head_dim = width // H
 
+    tile = (w_0, w_1, w_2)
+
     def vec(row):
         return vec_ref[layer * STEPS + row]
 
@@ -956,7 +991,7 @@
     @pl.when(s < 3)
     def project():
         bias = jnp.where(s == 0, vec(BQ), jnp.where(s == 2, vec(BV), 0.0))
-        qkv_out[layer, s] = (across_k(a_out[layer], w_ref[...]) + bias).astype(low)
+        qkv_out[layer, s] = (tile_across(a_out[layer], tile) + bias).astype(low)
 
     @pl.when(s == 2)
     def attend():
@@ -978,21 +1013,21 @@
 
     @pl.when(s == 3)
     def second_norm():
-        mid = cur[...] + across_k(o_out[layer], w_ref[...]) + vec(BPROJ)
+        mid = cur[...] + tile_across(o_out[layer], tile) + vec(BPROJ)
         mid_out[layer] = mid
         m_out[layer] = (normed(mid)[0] * vec(G2) + vec(S2)).astype(low)
         cur[...] = mid + vec(BOUT)
 
     @pl.when((s >= 4) & (s < 8))
     def widen():
-        u = across_k(m_out[layer], w_ref[...]) + vec(BFC + s - 4)
+        u = tile_across(m_out[layer], tile) + vec(BFC + s - 4)
         u_out[layer, s - 4] = u
         g = 0.5 * u * (1.0 + jnp.tanh(GELU_A * (u + GELU_B * (u * u * u))))
         g_out[layer, s - 4] = g.astype(low)
 
     @pl.when(s >= 8)
     def narrow():
-        cur[...] += along_k(g_out[layer, s - 8], w_ref[...])
+        cur[...] += tile_along(g_out[layer, s - 8], tile)
 
     @pl.when(step == 2 * STEPS - 1)
     def last_norm():
@@ -1021,7 +1056,7 @@
             shape((tok, width), f32),
             shape((tok, width), low),
         ),
-        in_specs=[vmem] * 6 + [pl.BlockSpec((width, width), lambda i: (i, 0))],
+        in_specs=[vmem] * 6 + tile_specs(width, lambda i: i),
         out_specs=(vmem,) * 11,
         scratch_shapes=[pltpu.VMEM((tok, width), f32)],
         compiler_params=pltpu.CompilerParams(vmem_limit_bytes=58 * 2**20),
@@ -1029,7 +1064,7 @@
             flops=2 * tok * mats.size, bytes_accessed=2 * mats.size, transcendentals=0
         ),
         name="forward_layers",
-    )(hot, rows, pos_hot, pos, mask, vecs, mats)
+    )(hot, rows, pos_hot, pos, mask, vecs, mats, mats, mats)
 
 
 def backward_kernel(
@@ -1045,7 +1080,9 @@
     m_ref,
     u_ref,
     g_ref,
-    w_ref,
+    w_0,
+    w_1,
+    w_2,
     dx_out,
     vec_out,
     acc_out,
@@ -1082,6 +1119,7 @@
     sums.level = {(0, 1): acc_1, 1: level_1}
     sums.halves, sums.fulls = {0: half_0}, {0: full_0}
     last = 2 * STEPS
+    tile = (w_0, w_1, w_2)
 
     def vec(row):
         return vec_ref[layer * STEPS + row]
@@ -1111,32 +1149,21 @@
         vec_out[last] = dg
         vec_out[last + 1] = ds
 
-    def collect(acc, before):
-        slot, b = lax.rem(before, 2), lax.rem(before, STEPS)
-        tile = jnp.where(b < 4, 8 + b, jnp.where(b < 8, b, jnp.where(b == 8, 3, b - 9)))
+    def collect(before):
+        slot, b = before % 2, before % STEPS
+        acc = acc_1 if before < STEPS else acc_0
+        tile_at = TILE_ORDER[b]
         pair_copy(slot).wait_recv()
-        rows, chunk = acc.shape[3], 16
-
-        def body(n, unused):
-            for u in range(4):
-                first = (n * 4 + u) * chunk
-                place_at = tile * width + first
-                block = lax.div(place_at, rows)
-                where = pl.ds(pl.multiple_of(lax.rem(place_at, rows), chunk), chunk)
-                here = pl.ds(pl.multiple_of(first, chunk), chunk)
-                value = own_s[here, :].astype(f32) + recv_s[slot, here, :].astype(f32)
-                acc[
-                    lax.div(block, RING * RING),
-                    lax.rem(lax.div(block, RING), RING),
-                    lax.rem(block, RING),
-                    where,
-                ] = value.astype(low)
-            return unused
-
-        lax.fori_loop(0, width // (4 * chunk), body, 0)
-
-    pl.when((step >= 1) & (step <= STEPS))(lambda: collect(acc_1, step - 1))
-    pl.when(step > STEPS)(lambda: collect(acc_0, step - 1))
+        granule = acc.shape[4]
+        count = width // granule
+        for g in range(count):
+            block, p = divmod(tile_at * count + g, 3)
+            here = slice(g * granule, (g + 1) * granule)
+            value = own_s[here, :].astype(f32) + recv_s[slot, here, :].astype(f32)
+            acc[block // (RING * RING), block // RING % RING, block % RING, p] = value.astype(low)
+
+    for n in range(1, last + 1):
+        pl.when(step == n)(lambda n=n: collect(n - 1))
 
     pl.when(step == STEPS)(lambda: sums.start(1, 0))
     pl.when(step == STEPS + 4)(lambda: sums.turn(1, 0))
@@ -1149,7 +1176,7 @@
 
     @pl.when((s < 4) & (step < last))
     def through_gelu():
-        dg = across_k(wide[...], w_ref[...])
+        dg = tile_across(wide[...], tile)
         u = u_ref[layer, s]
         square = u * u
         t = jnp.tanh(GELU_A * (u + GELU_B * (square * u)))
@@ -1167,7 +1194,7 @@
     @pl.when((s >= 4) & (s < 8))
     def through_fc():
         left = du_s[s - 4]
-        dx_out[...] += along_k(left, w_ref[...])
+        dx_out[...] += tile_along(left, tile)
         left_s[...] = left
 
     @pl.when(s == 8)
@@ -1180,7 +1207,7 @@
         mid_low = cur[...].astype(low)
         left_s[...] = mid_low
         set_right(o_ref[layer])
-        wide[...] = along_k(mid_low, w_ref[...]).astype(low)
+        wide[...] = tile_along(mid_low, tile).astype(low)
         lanes = lax.broadcasted_iota(jnp.int32, (1, 2 * head_dim), 1)
         scale = head_dim ** (-0.5)
         for pair in range(H // 2):
@@ -1217,7 +1244,7 @@
     @pl.when(s >= 9)
     def through_qkv():
         left = dqkv_s[s - 9]
-        dx_out[...] += along_k(left, w_ref[...])
+        dx_out[...] += tile_along(left, tile)
         left_s[...] = left
 
     @pl.when(step < last)
@@ -1238,17 +1265,21 @@
 
     @pl.when(step == last)
     def leave():
-        copy_acc = pltpu.make_async_copy(acc_0, acc_out, local.at[0])
-        copy_acc.start()
+        copies = []
+        for n in range(RING * RING):
+            spot = (n // RING, n % RING)
+            op = pltpu.make_async_copy(acc_0.at[spot], acc_out.at[spot], local.at[n])
+            op.start()
+            copies.append(op)
         dx_out[...] = cur[...]
         sums.finish(1, 0)
-        copy_sums = pltpu.make_async_copy(level_1.at[0], sums_out, local.at[1])
-        copy_sums.start()
+        copies.append(pltpu.make_async_copy(level_1.at[0], sums_out, local.at[RING * RING]))
+        copies[-1].start()
         for slot in range(2):
             pair_copy(slot).wait_send()
         sums.drain(1, 0)
-        copy_acc.wait()
-        copy_sums.wait()
+        for op in copies:
+            op.wait()
 
 
 def backward_layers(grad, hidden, vecs, saved, mats):
@@ -1257,16 +1288,13 @@
     shape = jax.ShapeDtypeStruct
     vmem = pl.BlockSpec(memory_space=pltpu.VMEM)
     hbm = pl.BlockSpec(memory_space=pltpu.HBM)
-    torus, half, rows = (RING, RING, RING), width // 2, 144
-    part = rows // 3
+    torus, half, part = (RING, RING, RING), width // 2, 48
 
     def tile(i):
         i = jnp.minimum(i, 2 * STEPS - 1)
         layer, s = 1 - i // STEPS, i % STEPS
-        return (
-            layer * STEPS
-            + jnp.where(s < 4, 8 + s, jnp.where(s < 8, s, jnp.where(s == 8, 3, s - 9))),
-            0,
+        return layer * STEPS + jnp.where(
+            s < 4, 8 + s, jnp.where(s < 8, s, jnp.where(s == 8, 3, s - 9))
         )
 
     return pl.pallas_call(
@@ -1275,10 +1303,10 @@
         out_shape=(
             shape((tok, width), f32),
             shape((2 * STEPS + 2, 1, width), f32),
-            shape(torus + (rows, half), low),
+            shape(torus + (3, part, half), low),
             shape((3, RING, RING, part, half), low),
         ),
-        in_specs=[vmem] * 12 + [pl.BlockSpec((width, width), tile)],
+        in_specs=[vmem] * 12 + tile_specs(width, tile),
         out_specs=(vmem, vmem, hbm, hbm),
         scratch_shapes=[
             pltpu.VMEM((tok, width), f32),
@@ -1290,8 +1318,8 @@
             pltpu.VMEM((width, half), low),
             pltpu.VMEM((2, width, half), low),
             pltpu.VMEM((2, width, half), low),
-            pltpu.VMEM(torus + (rows, half), low),
-            pltpu.VMEM(torus + (rows, half), low),
+            pltpu.VMEM(torus + (3, part, half), low),
+            pltpu.VMEM(torus + (3, part, half), low),
             pltpu.VMEM((1, 3, RING, RING, part, half), low),
             pltpu.VMEM((1, 3, 2, 2, RING, part, half), low),
             pltpu.VMEM((1, 3, 2, RING, RING, part, half), low),
@@ -1299,7 +1327,7 @@
             pltpu.SemaphoreType.DMA((12,)),
             pltpu.SemaphoreType.DMA((2,)),
             pltpu.SemaphoreType.DMA((2,)),
-            pltpu.SemaphoreType.DMA((2,)),
+            pltpu.SemaphoreType.DMA((RING * RING + 1,)),
         ],
         compiler_params=pltpu.CompilerParams(
             collective_id=4, has_side_effects=True, vmem_limit_bytes=60 * 2**20
@@ -1308,7 +1336,7 @@
             flops=4 * tok * mats.size, bytes_accessed=2 * mats.size, transcendentals=0
         ),
         name="backward_layers",
-    )(grad, hidden, vecs, *saved, mats)
+    )(grad, hidden, vecs, *saved, mats, mats, mats)
 
 
 def doc_info(doc_lens, tok_count, total_docs):

time: 496 us -> 528 us (1.065)
  Pallas kernels: 397 us -> 429 us
    pallas_call x1, Pallas kernels: 96.8 us -> 142 us  [gather_weights(): pl.pallas_call(gather_kernel, out_shape=(whole, jax.ShapeDtypeStruct((RIN...]
    pallas_call x1, Pallas kernels: 102 us -> 92.4 us  [backward_layers(): pl.pallas_call(backward_kernel, grid=(2 * STEPS + 1,), out_shape=(shape((...]
  transfers between devices with their start and end apart: 5 -> 5, of which waited for: 2 -> 2; matrix products, arithmetic and copies ran while one was open for 4% -> 4% of each run, Pallas kernels for 61% -> 64%
where the time goes in v4:
time: 528 us; the launch traced here: 527 us
  Pallas kernels  429 us (81%)
  starting transfers between devices  22.7 us (4%)
  other arithmetic  21.6 us (4%)
  between operations  18.9 us (4%)
  waiting for transfers between devices  17.5 us (3%)
  local copies, waits for them, and re-layouts  12.6 us (2%)
    pallas_call x1, Pallas kernels, gather_weights(): pl.pallas_call(gather_kernel, out_shape=(whole, jax.ShapeDtypeStruct((RIN...  142 us
    pallas_call x1, Pallas kernels, backward_layers(): pl.pallas_call(backward_kernel, grid=(2 * STEPS + 1,), out_shape=(shape((...  92.4 us
    pallas_call x1, Pallas kernels, head(): pl.pallas_call(head_kernel, out_shape=(jax.ShapeDtypeStruct((tok, width),...  78.2 us
    pallas_call x1, Pallas kernels, reduce_weights(): pl.pallas_call(reduce_kernel, out_shape=(jax.ShapeDtypeStruct((2, rows //...  69.4 us
    pallas_call x1, Pallas kernels, forward_layers(): pl.pallas_call(forward_kernel, grid=(2 * STEPS,), out_shape=(shape((2, to...  33 us
    pallas_call x1, Pallas kernels, sum_all(): pl.pallas_call(sum_kernel, out_shape=jax.ShapeDtypeStruct(value.shape, jn...  14.2 us
    all_to_all x1, starting transfers between devices, per_device(): lax.all_to_all(send_rows, ('dp', 'vocab'), split_axis=0, concat_axis=0, t...  11.1 us
  transfers between devices with their start and end apart: 5, of which 2 were waited for; matrix products, arithmetic and copies ran while one was open for 4% of the time, Pallas kernels for 64%

profile of v4, /device:TPU:0, one launch (start us, length us, event | category | flops | bytes accessed | tf_op | source)
XLA Modules:
  0.0 527.2 jit_solution(8854025606334283765)
XLA Ops:
  7.2 1.4 convert_element_type.78
  10.6 11.1 %all-to-all-start = ((s32[128,2,1]{1,2,0:T(1,128)}), s32[128,2,1]{1,2,0:T(1,128)S(1)}, u32[]{:S(2)}, u32[]{:S(2)}) async-start(s32[128,2,1]{1,2,0:T(1,128)} %bitcast.1), calls=%async_computation | async-start | bytes 131072 | tf_op jit(solution)/shard_map/all_to_all | solution.py:1426
  24.1 6.9 %all-to-all-done = s32[128,2,1]{1,2,0:T(1,128)S(1)} async-done(((s32[128,2,1]{1,2,0:T(1,128)}), s32[128,2,1]{1,2,0:T(1,128)S(1)}, u32[]{:S(2)}, u32[]{:S(2)}) %all-to-all-start) | async-done | bytes 1056 | tf_op jit(solution)/shard_map/all_to_all | solution.py:1426
  33.8 4.8 all-to-all-start.1
  40.2 10.6 %all-to-all-done.1 = bf16[128,2,768]{2,1,0:T(2,128)(2,1)S(1)} async-done(((bf16[128,2,768]{2,1,0:T(2,128)(2,1)}), bf16[128,2,768]{2,1,0:T(2,128)(2,1)S(1)}, u32[]{:S(2)}, u32[]{:S(2)}) %all-to-all-start.1) | async-done | bytes 393248 | tf_op jit(solution)/shard_map/all_to_all | solution.py:1429
  51.6 141.9 %gather_weights.1 = (bf16[2,4,4,4,144,768]{5,4,3,2,1,0:T(8,128)(2,1)}, bf16[4,4,4,2,16,128]{5,4,3,2,1,0:T(8,128)(2,1)}) custom-call(f32[2,72,768]{2,1,0:T(8,128)} %bitcast.83, bf16[16,128]{1,0:T(8,128)(2,1)} %fusion.18.small_ref), custom_call_target="tpu_custom_call" | custom-call | bytes 250000000 | tf_op jit(solution)/shard_map/gather_weights/pallas_call | solution.py:201
  193.5 1.2 copy.61
  196.7 33.0 %forward_layers.1 = (f32[2,128,768]{2,1,0:T(8,128)}, bf16[2,128,768]{2,1,0:T(8,128)(2,1)}, bf16[2,3,128,768]{3,2,1,0:T(8,128)(2,1)}, f32[2,12,128,128]{3,2,1,0:T...) custom-call(bf16[128,256]{1,0:T(8,128)(2,1)} %fusion.7.hot_ref, ...), custom_call_target="tpu_custom_call" | custom-call | flops 3623878656 | bytes 28311552 | tf_op jit(solution)/shard_map/forward_layers/pallas_call | solution.py:1043
  230.3 78.2 %head.1 = (f32[128,768]{1,0:T(8,128)}, bf16[6400,768]{1,0:T(8,128)(2,1)}, f32[8,128]{1,0:T(8,128)}) custom-call(bf16[128,768]{1,0:T(8,128)(2,1)} %get-tuple-element.48.f_ref, s32[8,128]{1,0:T(8,128)} %broadcast_in_dim.38.code_ref, f32[8,128]{1,0:T(8,128)} %divide_multiply_fusion.weight_ref, bf16[6400,768]{1,0:T(8,128)(2,1)} %all-gather.2.cloned.1.call-done.table_ref), custom_call_target="tpu_custom_call" | custom-call | flops 30198988800 | bytes 19660800 | tf_op jit(solution)/shard_map/head/pallas_call | solution.py:853
  308.5 92.4 %backward_layers.1 = (f32[128,768]{1,0:T(8,128)}, f32[26,1,768]{2,1,0:T(1,128)}, bf16[4,4,4,3,48,384]{5,4,3,2,1,0:T(8,128)(2,1)}, bf16[3,4,4,48,384]{4,3,2,1,0:T(8,128)(2,1)}) custom-call(f32[128,768]{1,0:T(8,128)} %get-tuple-element.51.grad_ref, f32[128,768]{1,0:T(8,128)} %get-tuple-element.52.hidden_ref, f32[26,1,768]{2,1,0:T(1,128)} %reshape.131.vec_ref, ...), custom_call_target="tpu_custom_call" | custom-call | flops 7247757312 | bytes 28311552 | tf_op jit(solution)/shard_map/backward_layers/pallas_call | solution.py:1300
  401.0 1.1 reduce.2
  402.3 1.5 fusion.8
  405.2 6.7 %all-to-all-start.2 = ((bf16[128,2,768]{2,1,0:T(2,128)(2,1)}), bf16[128,2,768]{2,1,0:T(2,128)(2,1)S(1)}, u32[]{:S(2)}, u32[]{:S(2)}) async-start(bf16[128,2,768]{2,1,0:T(2,128)(2,1)} %reshape.125), calls=%async_computation.3 | async-start | bytes 786432 | tf_op jit(solution)/shard_map/all_to_all | solution.py:1495
  412.2 1.2 copy.56
  413.9 69.4 %reduce_weights.1 = (f32[2,72,768]{2,1,0:T(8,128)}, f32[16,128]{1,0:T(8,128)}) custom-call(bf16[4,4,4,3,48,384]{5,4,3,2,1,0:T(8,128)(2,1)} %get-tuple-element.65.acc_ref, bf16[3,4,4,48,384]{4,3,2,1,0:T(8,128)(2,1)} %get-tuple-element.66.mid_ref, f32[4,4,4,2,16,128]{5,4,3,2,1,0:T(8,128)} %bitcast.82), custom_call_target="tpu_custom_call" | custom-call | bytes 180000000 | tf_op jit(solution)/shard_map/reduce_weights/pallas_call | solution.py:527
  483.3 1.4 multiply_reduce_fusion.3
  484.7 1.3 multiply_reduce_fusion.2
  486.0 1.7 multiply_reduce_fusion.1
  487.9 2.4 multiply_reduce_fusion
  494.3 14.2 %sum_all.1 = f32[8,128]{1,0:T(8,128)} custom-call(f32[8,128]{1,0:T(8,128)} %broadcast_in_dim.40.in_ref), custom_call_target="tpu_custom_call" | custom-call | tf_op jit(solution)/shard_map/sum_all/pallas_call | solution.py:600
  508.5 1.3 fusion.29
  511.2 1.3 fusion.27
  516.2 1.5 fusion.28
  517.8 1.3 add_multiply_fusion
  (101 shorter events, 20.5 us)
Async XLA Ops:
  7.2 222.5 %all-gather.2.cloned.1.call-start = ((), (), s32[]{:S(2)}) async-start(), calls=%async_computation.4 | async-start | bytes 10444800 | tf_op jit(solution)/shard_map/all_gather | solution.py:1437
  8.6 13.2 %copy-start.12 = (s32[1,8,3]{1,0,2:T(1,128)S(1)}, s32[1,8,3]{1,0,2:T(1,128)}, u32[]{:S(2)}) copy-start(s32[1,8,3]{1,0,2:T(1,128)} %param.17) | copy-start | bytes 292
  8.6 15.5 %copy-start.11 = (f32[80,6]{0,1:T(8,128)S(1)}, f32[80,6]{0,1:T(8,128)}, u32[]{:S(2)}) copy-start(f32[80,6]{0,1:T(8,128)} %param.24) | copy-start | bytes 5764
  10.6 20.4 %all-to-all-start = ((s32[128,2,1]{1,2,0:T(1,128)}), s32[128,2,1]{1,2,0:T(1,128)S(1)}, u32[]{:S(2)}, u32[]{:S(2)}) async-start(s32[128,2,1]{1,2,0:T(1,128)} %bitcast.1), calls=%async_computation | async-start | bytes 131072 | tf_op jit(solution)/shard_map/all_to_all | solution.py:1426
  32.5 6.2 %copy-start.21 = (s32[128]{0:T(128)S(1)}, s32[128]{0:T(128)}, u32[]{:S(2)}) copy-start(s32[128]{0:T(128)} %param.16) | copy-start | bytes 1540
  32.5 6.2 %copy-start.18 = (f32[156]{0:T(256)S(1)}, f32[156]{0:T(256)}, u32[]{:S(2)}) copy-start(f32[156]{0:T(256)} %param.27) | copy-start | bytes 1876
  33.8 16.9 %all-to-all-start.1 = ((bf16[128,2,768]{2,1,0:T(2,128)(2,1)}), bf16[128,2,768]{2,1,0:T(2,128)(2,1)S(1)}, u32[]{:S(2)}, u32[]{:S(2)}) async-start(bf16[128,2,768]{2,1,0:T(2,128)(2,1)} %reshape.119), calls=%async_computation.1 | async-start | bytes 786432 | tf_op jit(solution)/shard_map/all_to_all | solution.py:1429
  38.6 449.3 %reduce-scatter.2.cloned.1.call-start = ((), (), s32[]{:S(2)}) async-start(), calls=%async_computation.5 | async-start | bytes 10444800 | tf_op jit(solution)/shard_map/reduce_scatter | solution.py:1481
  401.0 3.0 copy-start.5
  405.2 82.4 %all-to-all-start.2 = ((bf16[128,2,768]{2,1,0:T(2,128)(2,1)}), bf16[128,2,768]{2,1,0:T(2,128)(2,1)S(1)}, u32[]{:S(2)}, u32[]{:S(2)}) async-start(bf16[128,2,768]{2,1,0:T(2,128)(2,1)} %reshape.125), calls=%async_computation.3 | async-start | bytes 786432 | tf_op jit(solution)/shard_map/all_to_all | solution.py:1495
  487.8 23.4 %copy-start.19 = (f32[156]{0:T(256)S(1)}, f32[156]{0:T(256)}, u32[]{:S(2)}) copy-start(f32[156]{0:T(256)} %param.28) | copy-start | bytes 1876
  487.9 24.8 %copy-start.2 = (f32[2,768,72]{1,2,0:T(8,128)S(1)}, f32[2,768,72]{1,2,0:T(8,128)}, u32[]{:S(2)}) copy-start(f32[2,768,72]{1,2,0:T(8,128)} %param.21) | copy-start | bytes 1327108
  487.9 24.8 %copy-start.3 = (f32[2,72,768]{2,1,0:T(8,128)S(1)}, f32[2,72,768]{2,1,0:T(8,128)}, u32[]{:S(2)}) copy-start(f32[2,72,768]{2,1,0:T(8,128)} %get-tuple-element.68) | copy-start | bytes 1327108
  487.9 24.8 %copy-start.9 = (f32[2,768,72]{1,2,0:T(8,128)S(1)}, f32[2,768,72]{1,2,0:T(8,128)}, u32[]{:S(2)}) copy-start(f32[2,768,72]{1,2,0:T(8,128)} %param.22) | copy-start | bytes 1327108
  510.5 3.2 copy-start.17
  510.5 3.7 copy-start.16
  512.5 2.3 copy-start.15
  512.6 2.2 copy-start.13
  512.7 2.8 copy-start.8
  512.7 3.6 copy-start.7
  513.6 4.2 copy-start.4
  513.6 2.6 copy-start.1
  514.8 3.0 copy-start.10
  516.2 1.6 copy-start.6
  (3 other events, 3.5 us)
Sparse Core Ops, SparseCore 0:
  10.7 100.7 all-gather.1
  308.7 92.3 reduce-scatter.1

commit v5 on v4

--- a/solution.py
+++ b/solution.py
@@ -10,7 +10,6 @@
 H = 12
 RING = 4
 ORDERS = ((2, 1, 0), (1, 0, 2), (0, 2, 1))
-PARTS = ((0, 16), (16, 96), (112, 32))
 
 norm_eps = 1e-05
 clip_bound = 0.01
@@ -68,25 +67,78 @@
     pl.semaphore_wait(barrier, len(devices))
 
 
+def ring_peers(at, core):
+    near = [device_at(moved(at, axis, by), core) for axis in range(3) for by in range(1, RING)]
+    return near + [device_at(at, 1 - core)]
+
+
 def neighbours(at, core):
     near = [device_at(moved(at, axis, by), core) for axis in range(3) for by in (1, RING - 1)]
     return near + [device_at(at, 1 - core)]
 
 
 def gather_kernel(
-    mine_ref, small_ref, out_ref, small_out, peer, block, send, recv, local
+    mine_ref,
+    small_ref,
+    table_ref,
+    spread_ref,
+    earlier_ref,
+    slot_ref,
+    swap_ref,
+    out_ref,
+    small_out,
+    rows_out,
+    asked_out,
+    peer,
+    block,
+    asked_rows,
+    over_z,
+    over_y,
+    sorted_rows,
+    over_x,
+    send,
+    recv,
+    local,
 ):
     at, core = place()
+    z, y, x = at
     rows, half = mine_ref.shape[1], mine_ref.shape[2] // 2
+    part = 2 * rows // 3
+    low, f32 = jnp.bfloat16, jnp.float32
     sibling = device_at(at, 1 - core)
-    greet(neighbours(at, core))
+    greet(ring_peers(at, core))
     wires = Wires(send, recv)
     cols = pl.ds(pl.multiple_of(core * half, half), half)
     other = pl.ds(pl.multiple_of((1 - core) * half, half), half)
 
     swap = wires.copy(mine_ref.at[:, :, other], peer, sibling)
-    small_local = pltpu.make_async_copy(small_ref, small_out.at[at[0], at[1], at[2], core], local.at[0])
-    small_local.start()
+    small_out[z, y, x, core] = small_ref[...]
+
+    def right(axis):
+        return device_at(moved(at, axis, 1), core)
+
+    def left(axis):
+        return device_at(moved(at, axis, RING - 1), core)
+
+    def all_around(axis, src_of, dst):
+        out = []
+        for by in range(1, RING):
+            there = moved(at, axis, by)
+            out.append(wires.copy(src_of(there[axis]), dst, device_at(there, core)))
+        return out
+
+    def small_start(phase):
+        index = [z, y, x]
+        for axis in ORDERS[0][:phase]:
+            index[axis] = pl.ds(0, RING)
+        own = small_out.at[index[0], index[1], index[2], core]
+        return all_around(ORDERS[0][phase], lambda c: own, own)
+
+    def arrive(ops):
+        for op in ops:
+            op.wait_recv()
+
+    small_ops = small_start(0)
     swap.wait_recv()
     for layer in range(2):
         own = jnp.where(core == 0, mine_ref[layer, :, :half], mine_ref[layer, :, half:])
@@ -94,13 +146,11 @@
         both = jnp.concatenate(
             [jnp.where(core == 0, own, got), jnp.where(core == 0, got, own)], 0
         )
-        block[layer] = both.astype(jnp.bfloat16)
+        block[layer] = both.astype(low)
     block_local = []
     for layer in range(2):
         op = pltpu.make_async_copy(
-            block.at[layer],
-            out_ref.at[layer, at[0], at[1], at[2], :, cols],
-            local.at[1 + layer],
+            block.at[layer], out_ref.at[layer, z, y, x, :, cols], local.at[layer]
         )
         op.start()
         block_local.append(op)
@@ -111,37 +161,19 @@
         index[order[phase]] = c
         for axis in order[:phase]:
             index[axis] = pl.ds(0, RING)
-        first, count = PARTS[p]
-        where = cols
+        first, count = p * part, part
         if piece is not None:
             if phase == 0:
-                cut, size = (0, half - 128) if piece == 0 else (half - 128, 128)
-                where = pl.ds(pl.multiple_of(core * half + cut, 128), size)
+                first, count = (first, 32) if piece == 0 else (first + 32, part - 32)
             else:
                 index[order[0]] = pl.ds(2 * piece, 2)
-        return out_ref.at[layer, index[0], index[1], index[2], pl.ds(first, count), where]
-
-    def small_bundle(phase, c):
-        order = ORDERS[0]
-        index = list(at)
-        index[order[phase]] = c
-        for axis in order[:phase]:
-            index[axis] = pl.ds(0, RING)
-        return small_out.at[index[0], index[1], index[2], core]
-
-    def right(axis):
-        return device_at(moved(at, axis, 1), core)
-
-    def left(axis):
-        return device_at(moved(at, axis, RING - 1), core)
+        return out_ref.at[layer, index[0], index[1], index[2], pl.ds(first, count), cols]
 
     chains = [(layer, p) for layer in range(2) for p in range(3)]
     pending = []
-    small_local.wait()
-    for op in block_local:
-        op.wait()
-    for phase in range(3):
-        steps = {}
+    steps, forwards = {}, {}
+
+    def start(phase):
         for key in chains:
             layer, p = key
             axis = ORDERS[p][phase]
@@ -149,10 +181,8 @@
             if phase == 2:
                 pending.append(wires.copy(src, src, sibling))
             steps[key] = (wires.copy(src, src, right(axis)), wires.copy(src, src, left(axis)))
-        axis = ORDERS[0][phase]
-        src = small_bundle(phase, at[axis])
-        small_steps = (wires.copy(src, src, right(axis)), wires.copy(src, src, left(axis)))
-        forwards = {}
+
+    def forward(phase):
         for key in chains:
             layer, p = key
             axis = ORDERS[p][phase]
@@ -168,11 +198,8 @@
                 for c in (before, after):
                     src = bundle(layer, p, phase, c)
                     pending.append(wires.copy(src, src, sibling))
-        axis = ORDERS[0][phase]
-        for op in small_steps:
-            op.wait_recv()
-        src = small_bundle(phase, lax.rem(at[axis] + 3, RING))
-        small_forward = wires.copy(src, src, right(axis))
+
+    def finish(phase):
         for key in chains:
             layer, p = key
             axis = ORDERS[p][phase]
@@ -182,46 +209,120 @@
                 if phase == 2:
                     src = bundle(layer, p, phase, across, piece)
                     pending.append(wires.copy(src, src, sibling))
-        small_forward.wait_recv()
-    src = small_out.at[:, :, :, core]
-    pending.append(wires.copy(src, src, sibling))
-    for op in pending:
-        op.wait_recv()
+
+    arrive(block_local_wait(block_local))
+    start(0)
+    arrive(small_ops)
+    small_ops = small_start(1)
+    forward(0)
+    arrive(small_ops)
+    small_ops = small_start(2)
+    finish(0)
+    start(1)
+    arrive(small_ops)
+    own = small_out.at[:, :, :, core]
+    small_ops = [wires.copy(own, own, sibling)]
+    forward(1)
+    arrive(small_ops)
+
+    count = 2 * RING**3
+    smalls = small_out[...].reshape((count,) + small_ref.shape)
+    high, rest = (
+        jnp.dot(spread_ref[...], smalls[:, IDS_ROW + n, :], preferred_element_type=f32)
+        for n in range(2)
+    )
+    own_rows = TABLE_ROWS
+    me = ((z * RING + y) * RING + x) * 2 + core
+    local_id = high * 256.0 + rest - (me * own_rows).astype(f32)
+    mine = (local_id >= 0.0) & (local_id < float(own_rows))
+    rank = jnp.dot(
+        jnp.where(mine, 1.0, 0.0).astype(low), earlier_ref[...], preferred_element_type=f32
+    )
+    picked = jnp.where(mine & (rank == slot_ref[...]), local_id, 0.0)
+    row = jnp.sum(picked, 1, keepdims=True).astype(jnp.int32)
+    places = lax.broadcasted_iota(jnp.int32, asked_out.shape, 1)
+    asked = jnp.where(places == row, 1.0, 0.0).astype(low)
+    asked_out[...] = asked
+    found = jnp.dot(asked, table_ref[...], preferred_element_type=f32).astype(low)
+    asked_rows[...] = found.reshape(asked_rows.shape)
+    over_z[z] = asked_rows[z]
+    row_ops = all_around(0, lambda c: asked_rows.at[c], over_z.at[z])
+
+    finish(1)
+    start(2)
+    arrive(row_ops)
+    over_y[y] = over_z[:, y]
+    row_ops = all_around(1, lambda c: over_z.at[:, c], over_y.at[y])
+    forward(2)
+    arrive(row_ops)
+    sorted_rows[...] = (
+        jnp.dot(
+            swap_ref[...], over_y[...].reshape(2 * count, table_ref.shape[1]), preferred_element_type=f32
+        )
+        .astype(low)
+        .reshape(sorted_rows.shape)
+    )
+    over_x[x] = sorted_rows[x]
+    row_ops = all_around(2, lambda c: sorted_rows.at[c], over_x.at[x])
+    finish(2)
+    arrive(row_ops)
+    pending.append(wires.copy(over_x.at[:, 1 - core], rows_out.at[:, core], sibling))
+    rows_out[:, core] = over_x[:, core]
+    arrive(pending)
     wires.drain()
 
 
-GATHER_COPIES = 1 + 3 * (6 * 4 + 3) + 6 * 5 + 1
-
-
-def gather_weights(mine, small):
+def block_local_wait(ops):
+    for op in ops:
+        op.wait()
+    return []
+
+
+IDS_ROW = 8
+TABLE_ROWS = 393
+GATHER_COPIES = 1 + 3 * (6 * 4 + 3) + 6 * 5 + 1 + 9 + 1
+
+
+def gather_weights(mine, small, table, spread, earlier, slots, swap):
     layers, rows, width = mine.shape
-    whole = jax.ShapeDtypeStruct((layers, RING, RING, RING, 2 * rows, width), jnp.bfloat16)
+    table_rows = table.shape[0]
+    count = 2 * RING**3
+    low = jnp.bfloat16
     hbm = pl.BlockSpec(memory_space=pltpu.HBM)
     vmem = pl.BlockSpec(memory_space=pltpu.VMEM)
-    mats, small_all = pl.pallas_call(
+    mats, small_all, fetched, asked = pl.pallas_call(
         gather_kernel,
         out_shape=(
-            whole,
-            jax.ShapeDtypeStruct((RING, RING, RING, 2) + small.shape, jnp.bfloat16),
+            jax.ShapeDtypeStruct((layers, RING, RING, RING, 2 * rows, width), low),
+            jax.ShapeDtypeStruct((RING, RING, RING, 2) + small.shape, low),
+            jax.ShapeDtypeStruct((RING, 2, count // 4, width), low),
+            jax.ShapeDtypeStruct((2 * count, table_rows), low),
         ),
-        in_specs=[vmem, vmem],
-        out_specs=(hbm, hbm),
+        in_specs=[vmem] * 7,
+        out_specs=(hbm, vmem, vmem, vmem),
         scratch_shapes=[
             pltpu.VMEM((layers, rows, width // 2), jnp.float32),
-            pltpu.VMEM((layers, 2 * rows, width // 2), jnp.bfloat16),
+            pltpu.VMEM((layers, 2 * rows, width // 2), low),
+            pltpu.VMEM((RING, RING, 16, width), low),
+            pltpu.VMEM((RING, RING, 16, width), low),
+            pltpu.VMEM((RING, RING, 16, width), low),
+            pltpu.VMEM((RING, 2, count // 4, width), low),
+            pltpu.VMEM((RING, 2, count // 4, width), low),
             pltpu.SemaphoreType.DMA((GATHER_COPIES,)),
             pltpu.SemaphoreType.DMA((GATHER_COPIES,)),
-            pltpu.SemaphoreType.DMA((3,)),
+            pltpu.SemaphoreType.DMA((2,)),
         ],
         compiler_params=pltpu.CompilerParams(
             collective_id=0, has_side_effects=True, vmem_limit_bytes=58 * 2**20
         ),
         cost_estimate=pl.CostEstimate(flops=0, bytes_accessed=250 * 10**6, transcendentals=0),
         name="gather_weights",
-    )(mine, small)
+    )(mine, small, table, spread, earlier, slots, swap)
     return (
         mats.reshape(layers * RING**3 * 2 * rows, width),
-        small_all.reshape((2 * RING**3,) + small.shape),
+        small_all.reshape((count,) + small.shape),
+        fetched.reshape(2 * count, width),
+        asked,
     )
 
 
@@ -382,11 +483,14 @@
 
 def reduce_kernel(
     acc_ref,
-    mid_ref,
     small_ref,
+    rows_ref,
+    swap_ref,
     out_ref,
     small_out,
-    acc,
+    rows_out,
+    acc_0,
+    acc_1,
     mid,
     thin,
     half_0,
@@ -402,6 +506,10 @@
     small_thin,
     final,
     final_peer,
+    over_core,
+    over_x,
+    sorted_rows,
+    over_y,
     send,
     recv,
     send_small,
@@ -412,22 +520,24 @@
     own_rows, half = final_peer.shape[1], final_peer.shape[2]
     sibling = device_at(at, 1 - core)
     sums = Reduction(at, core, send, recv)
-    sums.level = {(0, 0): acc, 1: mid, 2: thin}
+    sums.level = {(0, 0): acc_0, (0, 1): acc_1, 1: mid, 2: thin}
     sums.halves = {0: half_0, 1: half_1, 2: half_2}
     sums.fulls = {0: full_0, 1: full_1, 2: full_2}
     sums.final = final
 
-    mid_load = pltpu.make_async_copy(mid_ref, mid.at[1], local.at[0])
-    mid_load.start()
-    acc_loads = []
-    for n in range(RING * RING):
-        spot = (n // RING, n % RING)
-        op = pltpu.make_async_copy(acc_ref.at[spot], acc.at[spot], local.at[2 + n])
-        op.start()
-        acc_loads.append(op)
-    small_load = pltpu.make_async_copy(small_ref.at[:, :, :, core], small_acc, local.at[1])
+    accs = (acc_0, acc_1)
+    loads = {}
+    for layer in (1, 0):
+        for n in range(RING * RING):
+            spot = (n // RING, n % RING)
+            op = pltpu.make_async_copy(
+                acc_ref.at[(layer,) + spot], accs[layer].at[spot], local.at[1 + 16 * layer + n]
+            )
+            op.start()
+            loads[layer, n] = op
+    small_load = pltpu.make_async_copy(small_ref.at[:, :, :, core], small_acc, local.at[0])
     small_load.start()
-    greet(neighbours(at, core))
+    greet(ring_peers(at, core))
     wires = Wires(send_small, recv_small)
     small_swap = wires.copy(small_ref.at[:, :, :, 1 - core], small_sib, sibling)
 
@@ -471,36 +581,71 @@
             op.wait_recv()
         small_add(step, at[order[2 - step]], slots[step][1] + slots[step][2])
 
-    for op in acc_loads:
-        op.wait()
-    sums.start(0, 0)
-    mid_load.wait()
-    sums.start(1, 1)
+    z, y, x = at
+
+    def all_around(axis, src_of, dst):
+        out = []
+        for by in range(1, RING):
+            there = moved(at, axis, by)
+            out.append(wires.copy(src_of(there[axis]), dst, device_at(there, core)))
+        return out
+
+    def arrive(ops):
+        for op in ops:
+            op.wait_recv()
+
+    for layer in (1, 0):
+        for n in range(RING * RING):
+            loads[layer, n].wait()
+        sums.start(layer, 0)
+    row_ops = [wires.copy(rows_ref.at[:, 1 - core], over_core.at[:, core], sibling)]
+    over_core[:, core] = rows_ref[:, core]
     small_load.wait()
     small_swap.wait_recv()
     small_acc[...] = small_acc[...] + small_sib[...]
     op = small_start(0)
+    arrive(row_ops)
+    over_x[x] = over_core[x]
+    row_ops = all_around(2, lambda c: over_core.at[c], over_x.at[x])
+    sums.turn(1, 0)
     sums.turn(0, 0)
+    ops = small_turn(0, op)
+    arrive(row_ops)
+    count, width = swap_ref.shape[0], rows_ref.shape[3]
+    sorted_rows[...] = (
+        jnp.dot(
+            swap_ref[...], over_x[...].reshape(count, width), preferred_element_type=jnp.float32
+        )
+        .astype(jnp.bfloat16)
+        .reshape(sorted_rows.shape)
+    )
+    over_y[y] = sorted_rows[y]
+    row_ops = all_around(1, lambda c: sorted_rows.at[c], over_y.at[y])
+    small_finish(0, ops)
+    op = small_start(1)
+    sums.finish(1, 0)
+    sums.start(1, 1)
+    arrive(row_ops)
+    rows_out[z] = over_y[:, z]
+    row_ops = all_around(0, lambda c: over_y.at[:, c], rows_out.at[z])
+    ops = small_turn(1, op)
+    sums.finish(0, 0)
+    sums.start(0, 1)
+    small_finish(1, ops)
+    op = small_start(2)
     sums.turn(1, 1)
-    ops = small_turn(0, op)
+    ops = small_turn(2, op)
+    sums.turn(0, 1)
     sums.finish(1, 1)
     sums.start(1, 2)
-    small_finish(0, ops)
-    op = small_start(1)
-    sums.turn(1, 2)
-    ops = small_turn(1, op)
-    sums.finish(1, 2)
-    small_finish(1, ops)
-    op = small_start(2)
-    ops = small_turn(2, op)
-    sums.finish(0, 0)
-    sums.start(0, 1)
-    small_finish(2, ops)
-    sums.turn(0, 1)
     sums.finish(0, 1)
     sums.start(0, 2)
+    small_finish(2, ops)
+    sums.turn(1, 2)
     sums.turn(0, 2)
+    sums.finish(1, 2)
     sums.finish(0, 2)
+    arrive(row_ops)
 
     theirs = pl.ds(pl.multiple_of((1 - core) * own_rows, own_rows), own_rows)
     swap = wires.copy(final.at[:, theirs], final_peer, sibling)
@@ -511,13 +656,14 @@
         got = final_peer[layer]
         out_ref[layer, :, :half] = jnp.where(core == 0, own, got)
         out_ref[layer, :, half:] = jnp.where(core == 0, got, own)
-    for layer, step in ((1, 1), (1, 2), (0, 0), (0, 1), (0, 2)):
-        sums.drain(layer, step)
+    for layer in range(2):
+        for step in range(3):
+            sums.drain(layer, step)
     wires.drain()
 
 
-def reduce_weights(acc, mid, small):
-    part, half = acc.shape[4:]
+def reduce_weights(acc, small, rows_back, swap):
+    part, half = acc.shape[5:]
     rows = 3 * part
     torus = (RING, RING, RING)
     small_shape = small.shape[1:]
@@ -529,17 +675,19 @@
         out_shape=(
             jax.ShapeDtypeStruct((2, rows // 2, 2 * half), jnp.float32),
             jax.ShapeDtypeStruct(small_shape, jnp.float32),
+            jax.ShapeDtypeStruct((RING, RING, 16, 2 * half), low),
         ),
-        in_specs=[hbm, hbm, hbm],
-        out_specs=(vmem, vmem),
+        in_specs=[hbm, hbm, vmem, vmem],
+        out_specs=(vmem, vmem, vmem),
         scratch_shapes=[
+            pltpu.VMEM(torus + (3, part, half), low),
             pltpu.VMEM(torus + (3, part, half), low),
             pltpu.VMEM((2, 3, RING, RING, part, half), low),
             pltpu.VMEM((2, 3, RING, part, half), low),
-            pltpu.VMEM((1, 3, 2, 2, RING, part, half), low),
+            pltpu.VMEM((2, 3, 2, 2, RING, part, half), low),
             pltpu.VMEM((2, 3, 2, 2, part, half), low),
             pltpu.VMEM((2, 3, 2, 32, half), low),
-            pltpu.VMEM((1, 3, 2, RING, RING, part, half), low),
+            pltpu.VMEM((2, 3, 2, RING, RING, part, half), low),
             pltpu.VMEM((2, 3, 2, RING, part, half), low),
             pltpu.VMEM((2, 3, 2, part, half), low),
             pltpu.VMEM(torus + small_shape, jnp.float32),
@@ -549,18 +697,22 @@
             pltpu.VMEM((3,) + small_shape, jnp.float32),
             pltpu.VMEM((2, rows, half), jnp.float32),
             pltpu.VMEM((2, rows // 2, half), jnp.float32),
-            pltpu.SemaphoreType.DMA((60,)),
-            pltpu.SemaphoreType.DMA((60,)),
-            pltpu.SemaphoreType.DMA((11,)),
-            pltpu.SemaphoreType.DMA((11,)),
-            pltpu.SemaphoreType.DMA((2 + RING * RING,)),
+            pltpu.VMEM((RING, 2, 32, 2 * half), low),
+            pltpu.VMEM((RING, 2, 32, 2 * half), low),
+            pltpu.VMEM((RING, RING, 16, 2 * half), low),
+            pltpu.VMEM((RING, RING, 16, 2 * half), low),
+            pltpu.SemaphoreType.DMA((72,)),
+            pltpu.SemaphoreType.DMA((72,)),
+            pltpu.SemaphoreType.DMA((21,)),
+            pltpu.SemaphoreType.DMA((21,)),
+            pltpu.SemaphoreType.DMA((33,)),
         ],
         compiler_params=pltpu.CompilerParams(
             collective_id=1, has_side_effects=True, vmem_limit_bytes=58 * 2**20
         ),
-        cost_estimate=pl.CostEstimate(flops=0, bytes_accessed=180 * 10**6, transcendentals=0),
+        cost_estimate=pl.CostEstimate(flops=0, bytes_accessed=280 * 10**6, transcendentals=0),
         name="reduce_weights",
-    )(acc, mid, small.reshape(torus + (2,) + small_shape))
+    )(acc, small.reshape(torus + (2,) + small_shape), rows_back, swap)
 
 
 def sum_kernel(in_ref, out_ref, slots, send, recv):
@@ -1080,13 +1232,14 @@
     m_ref,
     u_ref,
     g_ref,
+    hot_ref,
     w_0,
     w_1,
     w_2,
     dx_out,
     vec_out,
+    rows_out,
     acc_out,
-    sums_out,
     cur,
     wide,
     du_s,
@@ -1098,11 +1251,6 @@
     recv_s,
     acc_0,
     acc_1,
-    level_1,
-    half_0,
-    full_0,
-    send,
-    recv,
     send_pair,
     recv_pair,
     local,
@@ -1115,9 +1263,6 @@
     head_dim = width // H
     at, core = place()
     sibling = device_at(at, 1 - core)
-    sums = Reduction(at, core, send, recv)
-    sums.level = {(0, 1): acc_1, 1: level_1}
-    sums.halves, sums.fulls = {0: half_0}, {0: full_0}
     last = 2 * STEPS
     tile = (w_0, w_1, w_2)
 
@@ -1143,7 +1288,7 @@
 
     @pl.when(step == 0)
     def enter():
-        greet(neighbours(at, core))
+        greet([sibling])
         dx, dg, ds = norm_back(grad_ref[...], hidden_ref[...], vec_ref[last])
         cur[...] = dx
         vec_out[last] = dg
@@ -1165,8 +1310,20 @@
     for n in range(1, last + 1):
         pl.when(step == n)(lambda n=n: collect(n - 1))
 
-    pl.when(step == STEPS)(lambda: sums.start(1, 0))
-    pl.when(step == STEPS + 4)(lambda: sums.turn(1, 0))
+    def leave_copies(layer, acc):
+        return [
+            pltpu.make_async_copy(
+                acc.at[n // RING, n % RING],
+                acc_out.at[layer, n // RING, n % RING],
+                local.at[layer * RING * RING + n],
+            )
+            for n in range(RING * RING)
+        ]
+
+    @pl.when(step == STEPS)
+    def leave_second():
+        for op in leave_copies(1, acc_1):
+            op.start()
 
     @pl.when((s == 0) & (step < last))
     def begin():
@@ -1265,24 +1422,19 @@
 
     @pl.when(step == last)
     def leave():
-        copies = []
-        for n in range(RING * RING):
-            spot = (n // RING, n % RING)
-            op = pltpu.make_async_copy(acc_0.at[spot], acc_out.at[spot], local.at[n])
+        for op in leave_copies(0, acc_0):
             op.start()
-            copies.append(op)
         dx_out[...] = cur[...]
-        sums.finish(1, 0)
-        copies.append(pltpu.make_async_copy(level_1.at[0], sums_out, local.at[RING * RING]))
-        copies[-1].start()
+        rows = over_rows(hot_ref[...], cur[...].astype(low)).astype(low)
+        rows_out[...] = rows.reshape(rows_out.shape)
         for slot in range(2):
             pair_copy(slot).wait_send()
-        sums.drain(1, 0)
-        for op in copies:
-            op.wait()
-
-
-def backward_layers(grad, hidden, vecs, saved, mats):
+        for layer_at, acc in ((1, acc_1), (0, acc_0)):
+            for op in leave_copies(layer_at, acc):
+                op.wait()
+
+
+def backward_layers(grad, hidden, vecs, saved, hot, mats):
     tok, width = grad.shape
     low, f32 = jnp.bfloat16, jnp.float32
     shape = jax.ShapeDtypeStruct
@@ -1303,11 +1455,11 @@
         out_shape=(
             shape((tok, width), f32),
             shape((2 * STEPS + 2, 1, width), f32),
-            shape(torus + (3, part, half), low),
-            shape((3, RING, RING, part, half), low),
+            shape((RING, 2, 32, width), low),
+            shape((2,) + torus + (3, part, half), low),
         ),
-        in_specs=[vmem] * 12 + tile_specs(width, tile),
-        out_specs=(vmem, vmem, hbm, hbm),
+        in_specs=[vmem] * 13 + tile_specs(width, tile),
+        out_specs=(vmem, vmem, vmem, hbm),
         scratch_shapes=[
             pltpu.VMEM((tok, width), f32),
             pltpu.VMEM((tok, width), low),
@@ -1320,14 +1472,9 @@
             pltpu.VMEM((2, width, half), low),
             pltpu.VMEM(torus + (3, part, half), low),
             pltpu.VMEM(torus + (3, part, half), low),
-            pltpu.VMEM((1, 3, RING, RING, part, half), low),
-            pltpu.VMEM((1, 3, 2, 2, RING, part, half), low),
-            pltpu.VMEM((1, 3, 2, RING, RING, part, half), low),
-            pltpu.SemaphoreType.DMA((12,)),
-            pltpu.SemaphoreType.DMA((12,)),
             pltpu.SemaphoreType.DMA((2,)),
             pltpu.SemaphoreType.DMA((2,)),
-            pltpu.SemaphoreType.DMA((RING * RING + 1,)),
+            pltpu.SemaphoreType.DMA((2 * RING * RING,)),
         ],
         compiler_params=pltpu.CompilerParams(
             collective_id=4, has_side_effects=True, vmem_limit_bytes=60 * 2**20
@@ -1336,7 +1483,7 @@
             flops=4 * tok * mats.size, bytes_accessed=2 * mats.size, transcendentals=0
         ),
         name="backward_layers",
-    )(grad, hidden, vecs, *saved, mats, mats, mats)
+    )(grad, hidden, vecs, *saved, hot, mats, mats, mats)
 
 
 def doc_info(doc_lens, tok_count, total_docs):
@@ -1415,25 +1562,6 @@
     table_padded = jnp.pad(table_low, ((0, pad_rows), (0, 0)))
     slot_rows = own_rows + pad_rows
 
-    owners = token_ids // own_rows
-    tokens = jnp.arange(tok, dtype=jnp.int32)
-    earlier = jnp.sum((owners[:, None] == owners[None, :]) & (tokens[None, :] < tokens[:, None]), 1)
-    slot_hot = (owners * capacity + earlier)[:, None] == jnp.arange(
-        devices * capacity, dtype=jnp.int32
-    )[None, :]
-    send_rows = jnp.sum(jnp.where(slot_hot, (token_ids % own_rows)[:, None], 0), 0)
-    slot_hot = slot_hot.astype(low)
-    local_rows = lax.all_to_all(send_rows, ("dp", "vocab"), split_axis=0, concat_axis=0, tiled=True)
-    asked = (local_rows[:, None] == jnp.arange(own_rows, dtype=jnp.int32)[None, :]).astype(low)
-    fetched = jnp.dot(asked, table_low, preferred_element_type=jnp.float32).astype(low)
-    returned_rows = lax.all_to_all(
-        fetched.reshape(devices, capacity, width),
-        ("dp", "vocab"),
-        split_axis=0,
-        concat_axis=0,
-        tiled=True,
-    ).reshape(devices * capacity, width)
-    blocks, returned_rows = lax.optimization_barrier((blocks, returned_rows))
     table_slice = lax.all_gather(table_padded, "dp", axis=0, tiled=True)
     target_owners = targets // own_rows
     codes = (
@@ -1442,10 +1570,33 @@
         + targets % own_rows
     )
 
-    small = pack_small(
-        jnp.concatenate([jnp.transpose(pos_table).reshape(-1), vectors]).astype(low)
-    )
-    mats_all, small_all = gather_weights(blocks, small)
+    owners = token_ids // own_rows
+    tokens = jnp.arange(tok, dtype=jnp.int32)
+    rank = jnp.sum((owners[:, None] == owners[None, :]) & (tokens[None, :] < tokens[:, None]), 1)
+    slot_count = devices * capacity
+    slots = jnp.arange(slot_count, dtype=jnp.int32)
+    arrival = (
+        (owners % 8) * 32 + (owners // 8 % RING) * 8 + (owners // 32) * capacity + rank
+    )
+    slot_hot = (arrival[:, None] == slots[None, :]).astype(low)
+    spread = (slots[:, None] // capacity == jnp.arange(devices)[None, :]).astype(low)
+    earlier = (tokens[:, None] < tokens[None, :]).astype(low)
+    slot_number = jnp.broadcast_to((slots % capacity).astype(jnp.float32)[:, None], (slot_count, tok))
+    by_owner = (
+        (slots % 64 // 16) * 2 + slots // 64 * 8 + slots % 16 // 2 * 32 + slots % capacity
+    )
+    swap = (by_owner[:, None] == slots[None, :]).astype(low)
+    values = jnp.concatenate([jnp.transpose(pos_table).reshape(-1), vectors]).astype(low)
+    small = jnp.concatenate(
+        [
+            jnp.pad(values, (0, IDS_ROW * LANES - values.shape[0])).reshape(IDS_ROW, LANES),
+            jnp.stack([token_ids // 256, token_ids % 256]).astype(low),
+            jnp.zeros((SMALL_ROWS - IDS_ROW - 2, LANES), low),
+        ]
+    )
+    mats_all, small_all, returned_rows, asked = gather_weights(
+        blocks, small, table_padded, spread, earlier, slot_number, jnp.transpose(swap)
+    )
     small_all = small_all.reshape(devices, -1)
     pos_low_t = small_all[:, : pos_rows * pos_cols].reshape(width, pos_rows)
     vecs_all = (
@@ -1481,8 +1632,8 @@
     table_grad = lax.psum_scatter(table_part, "dp", scatter_dimension=0, tiled=True)[
         :own_rows
     ].astype(jnp.float32)
-    grad_hidden, grad_vecs, grad_acc, grad_sums = backward_layers(
-        grad_final, hidden, vec_rows, saved, mats_all
+    grad_hidden, grad_vecs, rows_back, grad_acc = backward_layers(
+        grad_final, hidden, vec_rows, saved, slot_hot, mats_all
     )
     grad_pos = lax.dot_general(
         grad_hidden,
@@ -1490,25 +1641,16 @@
         (((0,), (0,)), ((), ())),
         precision=lax.Precision.HIGHEST,
     )
-    send_grads = contract(slot_hot, grad_hidden.astype(low), 0, 0).astype(low)
-    grad_acc, send_grads = lax.optimization_barrier((grad_acc, send_grads))
-    back_grads = lax.all_to_all(
-        send_grads.reshape(devices, capacity, width),
-        ("dp", "vocab"),
-        split_axis=0,
-        concat_axis=0,
-        tiled=True,
-    ).reshape(-1, width)
     small_grads = pack_small(
         jnp.concatenate(
             [grad_pos.reshape(devices, -1), grad_vecs.reshape(devices, -1)], 1
         )
     )
-    mats_shard, small_shard = reduce_weights(grad_acc, grad_sums, small_grads)
+    mats_shard, small_shard, back_grads = reduce_weights(grad_acc, small_grads, rows_back, swap)
     small_shard = small_shard.reshape(-1)
     pos_shard = small_shard[: pos_rows * pos_cols].reshape(pos_cols, pos_rows)
     vec_shard = small_shard[pos_rows * pos_cols : pos_rows * pos_cols + vec_own]
-    table_grad = table_grad + contract(asked, back_grads, 0, 0)
+    table_grad = table_grad + contract(asked, back_grads.reshape(slot_count, width), 0, 0)[:own_rows]
     local_squares = (
         jnp.sum(table_grad * table_grad)
         + jnp.sum(mats_shard * mats_shard)

time: 528 us -> 478 us (0.905)
  starting transfers between devices: 22.7 us -> 0.08 us
  waiting for transfers between devices: 17.5 us -> 0.05 us
  Pallas kernels: 429 us -> 423 us
    all_to_all x3 -> x0, starting transfers between devices: 22.7 us -> none  [the longest x1 11.1 us: per_device(): lax.all_to_all(send_rows, ('dp', 'vocab'), split_axis=0, concat_axis=0, t...]
    all_to_all x3 -> x0, waiting for transfers between devices: 17.5 us -> none  [the longest x1 10.6 us: per_device(): lax.all_to_all(fetched.reshape(devices, capacity, width), ('dp', 'vocab')...]
    pallas_call x1, Pallas kernels: 142 us -> 128 us  [gather_weights(): pl.pallas_call(gather_kernel, out_shape=(jax.ShapeDtypeStruct((layers, RI...]
    pallas_call x1, Pallas kernels: 69.4 us -> 81.4 us  [reduce_weights(): pl.pallas_call(reduce_kernel, out_shape=(jax.ShapeDtypeStruct((2, rows //...]
    pallas_call x1, Pallas kernels: 92.4 us -> 86.8 us  [backward_layers(): pl.pallas_call(backward_kernel, grid=(2 * STEPS + 1,), out_shape=(shape((...]
  transfers between devices with their start and end apart: 5 -> 2, of which waited for: 2 -> 0; matrix products, arithmetic and copies ran while one was open for 4% -> 4% of each run, Pallas kernels for 64% -> 69%
where the time goes in v5:
time: 478 us; the launch traced here: 477 us
  Pallas kernels  423 us (88%)
  other arithmetic  22.8 us (5%)
  between operations  18.8 us (4%)
  local copies, waits for them, and re-layouts  9.15 us (2%)
    pallas_call x1, Pallas kernels, gather_weights(): pl.pallas_call(gather_kernel, out_shape=(jax.ShapeDtypeStruct((layers, RI...  128 us
    pallas_call x1, Pallas kernels, backward_layers(): pl.pallas_call(backward_kernel, grid=(2 * STEPS + 1,), out_shape=(shape((...  86.8 us
    pallas_call x1, Pallas kernels, reduce_weights(): pl.pallas_call(reduce_kernel, out_shape=(jax.ShapeDtypeStruct((2, rows //...  81.4 us
    pallas_call x1, Pallas kernels, head(): pl.pallas_call(head_kernel, out_shape=(jax.ShapeDtypeStruct((tok, width),...  78.2 us
    pallas_call x1, Pallas kernels, forward_layers(): pl.pallas_call(forward_kernel, grid=(2 * STEPS,), out_shape=(shape((2, to...  32.9 us
    pallas_call x1, Pallas kernels, sum_all(): pl.pallas_call(sum_kernel, out_shape=jax.ShapeDtypeStruct(value.shape, jn...  15.4 us
  transfers between devices with their start and end apart: 2, of which 0 were waited for; matrix products, arithmetic and copies ran while one was open for 4% of the time, Pallas kernels for 69%

profile of v5, /device:TPU:0, one launch (start us, length us, event | category | flops | bytes accessed | tf_op | source)
XLA Modules:
  0.0 477.4 jit_solution(3545117633648727790)
XLA Ops:
  7.2 1.4 convert_element_type.87
  8.6 0.9 pad.17.table_ref
  13.5 127.8 %gather_weights.1 = (bf16[2,4,4,4,144,768]{5,4,3,2,1,0:T(8,128)(2,1)}, bf16[4,4,4,2,16,128]{5,4,3,2,1,0:T(8,128)(2,1)}, bf16[4,2,32,768]{3,2,1,0:T(8,128)(2,1)}, bf16[256,400]{1,0:T(8,128)(2,1)}) custom-call(f32[2,72,768]{2,1,0:T(8,128)} %bitcast.88, bf16[16,128]{1,0:T(8,128)(2,1)} %maximum_maximum_fusion.small_ref, bf16[400,768]{1,0:T(8,128)(2,1)} %pad.17.table_ref, ...), custom_call_target="tpu_custom_call" | custom-call | bytes 250000000 | tf_op jit(solution)/shard_map/gather_weights/pallas_call | solution.py:293
  141.3 1.2 copy.53
  142.6 0.8 reshape.227.vec_ref
  143.5 1.0 reshape.220.pos_ref
  147.6 32.9 %forward_layers.1 = (f32[2,128,768]{2,1,0:T(8,128)}, bf16[2,128,768]{2,1,0:T(8,128)(2,1)}, bf16[2,3,128,768]{3,2,1,0:T(8,128)(2,1)}, f32[2,12,128,128]{3,2,1,0:T...) custom-call(bf16[128,256]{1,0:T(8,128)(2,1)} %fusion.7.hot_ref, ...), custom_call_target="tpu_custom_call" | custom-call | flops 3623878656 | bytes 28311552 | tf_op jit(solution)/shard_map/forward_layers/pallas_call | solution.py:1195
  181.2 78.2 %head.1 = (f32[128,768]{1,0:T(8,128)}, bf16[6400,768]{1,0:T(8,128)(2,1)}, f32[8,128]{1,0:T(8,128)}) custom-call(bf16[128,768]{1,0:T(8,128)(2,1)} %get-tuple-element.46.f_ref, s32[8,128]{1,0:T(8,128)} %broadcast_in_dim.30.code_ref, f32[8,128]{1,0:T(8,128)} %divide_multiply_fusion.weight_ref, bf16[6400,768]{1,0:T(8,128)(2,1)} %all-gather.2.cloned.1.call-done.table_ref), custom_call_target="tpu_custom_call" | custom-call | flops 30198988800 | bytes 19660800 | tf_op jit(solution)/shard_map/head/pallas_call | solution.py:1005
  259.4 86.8 %backward_layers.1 = (f32[128,768]{1,0:T(8,128)}, f32[26,1,768]{2,1,0:T(1,128)}, bf16[4,2,32,768]{3,2,1,0:T(8,128)(2,1)}, bf16[2,4,4,4,3,48,384]{6,5,4,3,2,1,0:T(8,128)(2,1)}) custom-call(f32[128,768]{1,0:T(8,128)} %get-tuple-element.50.grad_ref, f32[128,768]{1,0:T(8,128)} %get-tuple-element.51.hidden_ref, f32[26,1,768]{2,1,0:T(1,128)} %reshape.227.vec_ref, ...), custom_call_target="tpu_custom_call" | custom-call | flops 7247757312 | bytes 28311552 | tf_op jit(solution)/shard_map/backward_layers/pallas_call | solution.py:1452
  346.2 1.1 reduce.1
  347.5 1.5 fusion.9
  349.4 1.2 copy.48
  351.1 81.4 %reduce_weights.1 = (f32[2,72,768]{2,1,0:T(8,128)}, f32[16,128]{1,0:T(8,128)}, bf16[4,4,16,768]{3,2,1,0:T(8,128)(2,1)}) custom-call(bf16[2,4,4,4,3,48,384]{6,5,4,3,2,1,0:T(8,128)(2,1)} %get-tuple-element.61.acc_ref, f32[4,4,4,2,16,128]{5,4,3,2,1,0:T(8,128)} %bitcast.87, bf16[4,2,32,768]{3,2,1,0:T(8,128)(2,1)} %get-tuple-element.64.rows_ref, ...), custom_call_target="tpu_custom_call" | custom-call | bytes 280000000 | tf_op jit(solution)/shard_map/reduce_weights/pallas_call | solution.py:673
  432.6 1.4 multiply_reduce_fusion.3
  433.9 1.3 multiply_reduce_fusion.2
  435.2 1.7 multiply_reduce_fusion.1
  437.0 2.4 multiply_reduce_fusion
  443.3 15.4 %sum_all.1 = f32[8,128]{1,0:T(8,128)} custom-call(f32[8,128]{1,0:T(8,128)} %broadcast_in_dim.32.in_ref), custom_call_target="tpu_custom_call" | custom-call | tf_op jit(solution)/shard_map/sum_all/pallas_call | solution.py:752
  458.8 1.3 fusion.48
  461.5 1.3 fusion.46
  462.9 0.9 convert_bitcast_fusion
  465.7 0.8 fusion.2
  466.5 1.5 fusion.47
  468.0 1.3 add_multiply_fusion
  (93 shorter events, 13.1 us)
Async XLA Ops:
  7.2 173.4 %all-gather.2.cloned.1.call-start = ((), (), s32[]{:S(2)}) async-start(), calls=%async_computation.1 | async-start | bytes 10444800 | tf_op jit(solution)/shard_map/all_gather | solution.py:1565
  8.6 1.0 copy-start.18
  8.6 1.0 copy-start.12
  8.6 1.1 copy-start.11
  8.6 2.0 copy-start.21
  9.5 427.4 %reduce-scatter.2.cloned.1.call-start = ((), (), s32[]{:S(2)}) async-start(), calls=%async_computation.2 | async-start | bytes 10444800 | tf_op jit(solution)/shard_map/reduce_scatter | solution.py:1632
  141.3 3.5 copy-start.20
  349.4 1.2 copy-start.14
  351.1 85.8 %copy-start.9 = (bf16[256,400]{1,0:T(8,128)(2,1)S(1)}, bf16[256,400]{1,0:T(8,128)(2,1)}, u32[]{:S(2)}) copy-start(bf16[256,400]{1,0:T(8,128)(2,1)} %get-tuple-element.49) | copy-start | bytes 614404
  436.9 24.5 %copy-start.19 = (f32[156]{0:T(256)S(1)}, f32[156]{0:T(256)}, u32[]{:S(2)}) copy-start(f32[156]{0:T(256)} %param.28) | copy-start | bytes 1876
  436.9 25.9 %copy-start.2 = (f32[2,768,72]{1,2,0:T(8,128)S(1)}, f32[2,768,72]{1,2,0:T(8,128)}, u32[]{:S(2)}) copy-start(f32[2,768,72]{1,2,0:T(8,128)} %param.21) | copy-start | bytes 1327108
  436.9 25.9 %copy-start.3 = (f32[2,72,768]{2,1,0:T(8,128)S(1)}, f32[2,72,768]{2,1,0:T(8,128)}, u32[]{:S(2)}) copy-start(f32[2,72,768]{2,1,0:T(8,128)} %get-tuple-element.66) | copy-start | bytes 1327108
  437.0 25.9 %copy-start.8 = (f32[2,768,72]{1,2,0:T(8,128)S(1)}, f32[2,768,72]{1,2,0:T(8,128)}, u32[]{:S(2)}) copy-start(f32[2,768,72]{1,2,0:T(8,128)} %param.22) | copy-start | bytes 1327108
  460.7 3.2 copy-start.17
  460.7 3.7 copy-start.16
  462.8 2.3 copy-start.15
  462.9 2.2 copy-start.13
  462.9 2.8 copy-start.7
  462.9 3.6 copy-start.6
  463.9 4.2 copy-start.4
  463.9 2.6 copy-start.1
  465.1 3.0 copy-start.10
  466.5 1.6 copy-start.5
  468.0 1.4 copy-start
Sparse Core Ops, SparseCore 0:
  10.7 127.2 all-gather.1
  259.5 89.4 reduce-scatter.1

commit v6 on v5

--- a/solution.py
+++ b/solution.py
@@ -715,16 +715,31 @@
     )(acc, small.reshape(torus + (2,) + small_shape), rows_back, swap)
 
 
-def sum_kernel(in_ref, out_ref, slots, send, recv):
+def sum_kernel(
+    part_ref, asked_ref, back_ref, mats_ref, small_ref, loss_ref, out_ref, table_ref, slots, send, recv
+):
     at, core = place()
     sibling = device_at(at, 1 - core)
-    partners = [sibling] + [
-        device_at(moved(at, axis, by), core) for axis in range(3) for by in range(1, RING)
-    ]
-    greet(partners)
+    greet(ring_peers(at, core))
     wires = Wires(send, recv)
-    slots[0, core] = in_ref[...]
-    swap = wires.copy(in_ref, slots.at[0, core], sibling)
+    table = part_ref[...].astype(jnp.float32) + lax.dot_general(
+        asked_ref[...],
+        back_ref[...],
+        (((0,), (0,)), ((), ())),
+        preferred_element_type=jnp.float32,
+    )
+    table_ref[...] = table
+
+    def total(value):
+        while value.ndim > 2:
+            value = jnp.sum(value, 0)
+        return jnp.sum(jnp.sum(value, 0, keepdims=True), 1, keepdims=True)
+
+    mats, small = mats_ref[...], small_ref[...]
+    squares = total(table * table) + total(mats * mats) + total(small * small)
+    rows = lax.broadcasted_iota(jnp.int32, out_ref.shape, 0)
+    slots[0, core] = jnp.where(rows == 0, total(loss_ref[...]), squares)
+    swap = wires.copy(slots.at[0, core], slots.at[0, core], sibling)
     swap.wait_recv()
     value = slots[0, 0] + slots[0, 1]
     for axis in range(3):
@@ -747,21 +762,57 @@
     wires.drain()
 
 
-def sum_all(value):
+def sum_all(part, asked, back, mats, small, losses):
     vmem = pl.BlockSpec(memory_space=pltpu.VMEM)
+    value = (8, 128)
     return pl.pallas_call(
         sum_kernel,
-        out_shape=jax.ShapeDtypeStruct(value.shape, jnp.float32),
-        in_specs=[vmem],
-        out_specs=vmem,
+        out_shape=(
+            jax.ShapeDtypeStruct(value, jnp.float32),
+            jax.ShapeDtypeStruct(part.shape, jnp.float32),
+        ),
+        in_specs=[vmem] * 6,
+        out_specs=(vmem, vmem),
         scratch_shapes=[
-            pltpu.VMEM((4, RING) + value.shape, jnp.float32),
+            pltpu.VMEM((4, RING) + value, jnp.float32),
             pltpu.SemaphoreType.DMA((10,)),
             pltpu.SemaphoreType.DMA((10,)),
         ],
-        compiler_params=pltpu.CompilerParams(collective_id=2, has_side_effects=True),
+        compiler_params=pltpu.CompilerParams(
+            collective_id=2, has_side_effects=True, vmem_limit_bytes=32 * 2**20
+        ),
+        cost_estimate=pl.CostEstimate(flops=0, bytes_accessed=40 * 10**6, transcendentals=0),
         name="sum_all",
-    )(value)
+    )(part, asked, back, mats, small, losses)
+
+
+def update_kernel(sums_ref, *refs):
+    norm = jnp.sqrt(sums_ref[1:2, 0:1])
+    factor = clip_bound / jnp.maximum(norm, clip_bound)
+    for n in range(2):
+        weight, moment, average, grad = refs[4 * n : 4 * n + 4]
+        outs = refs[8 + 4 * n : 12 + 4 * n]
+        rows = weight.shape[0]
+        results = renew(weight[...], moment[...], average[...], grad[:rows, :], factor)
+        for out, value in zip(outs, results):
+            out[...] = value
+
+
+def update(sums, table, mats):
+    vmem = pl.BlockSpec(memory_space=pltpu.VMEM)
+    shapes = []
+    for item in (table[0], mats[0]):
+        shapes += [jax.ShapeDtypeStruct(item.shape, jnp.float32)] * 3
+        shapes += [jax.ShapeDtypeStruct(item.shape, jnp.bfloat16)]
+    outs = pl.pallas_call(
+        update_kernel,
+        out_shape=tuple(shapes),
+        in_specs=[vmem] * 9,
+        out_specs=(vmem,) * 8,
+        compiler_params=pltpu.CompilerParams(vmem_limit_bytes=40 * 2**20),
+        name="update",
+    )(sums, *table, *mats)
+    return outs[:4], outs[4:]
 
 
 TILE = 800
@@ -1059,24 +1110,11 @@
     return lax.dot_general(left, right, (((0,), (0,)), ((), ())), preferred_element_type=jnp.float32)
 
 
-def tile_across(left, tile):
-    return jnp.concatenate([across_k(left, block[...]) for block in tile], 1)
-
-
-def tile_along(left, tile):
-    total = None
-    for n, block in enumerate(tile):
-        rows = block.shape[0]
-        term = along_k(left[:, n * rows : (n + 1) * rows], block[...])
-        total = term if total is None else total + term
-    return total
-
-
-def tile_specs(width, tile):
-    return [
-        pl.BlockSpec((width // 3, width), lambda i, n=n: (3 * tile(i) + n, 0))
-        for n in range(3)
-    ]
+def tile_copy(mats_ref, weights, ready, tile, step):
+    rows = weights.shape[1]
+    return pltpu.make_async_copy(
+        mats_ref.at[pl.ds(tile * rows, rows)], weights.at[step], ready.at[step]
+    )
 
 
 def normed(value):
@@ -1104,9 +1142,7 @@
     pos_ref,
     mask_ref,
     vec_ref,
-    w_0,
-    w_1,
-    w_2,
+    mats_ref,
     x_out,
     a_out,
     qkv_out,
@@ -1119,6 +1155,8 @@
     hidden_out,
     final_out,
     cur,
+    weights,
+    ready,
 ):
     step = pl.program_id(0)
     layer, s = lax.div(step, STEPS), lax.rem(step, STEPS)
@@ -1126,10 +1164,14 @@
     width = cur.shape[1]
     head_dim = width // H
 
-    tile = (w_0, w_1, w_2)
 
     def vec(row):
         return vec_ref[layer * STEPS + row]
+
+    @pl.when(step == 0)
+    def fetch():
+        for n in range(2 * STEPS):
+            tile_copy(mats_ref, weights, ready, n, n).start()
 
     @pl.when(step == 0)
     def embed():
@@ -1140,10 +1182,12 @@
         x_out[layer] = cur[...]
         a_out[layer] = (normed(cur[...])[0] * vec(G1) + vec(S1)).astype(low)
 
+    tile_copy(mats_ref, weights, ready, 0, step).wait()
+
     @pl.when(s < 3)
     def project():
         bias = jnp.where(s == 0, vec(BQ), jnp.where(s == 2, vec(BV), 0.0))
-        qkv_out[layer, s] = (tile_across(a_out[layer], tile) + bias).astype(low)
+        qkv_out[layer, s] = (across_k(a_out[layer], weights[step]) + bias).astype(low)
 
     @pl.when(s == 2)
     def attend():
@@ -1165,21 +1209,21 @@
 
     @pl.when(s == 3)
     def second_norm():
-        mid = cur[...] + tile_across(o_out[layer], tile) + vec(BPROJ)
+        mid = cur[...] + across_k(o_out[layer], weights[step]) + vec(BPROJ)
         mid_out[layer] = mid
         m_out[layer] = (normed(mid)[0] * vec(G2) + vec(S2)).astype(low)
         cur[...] = mid + vec(BOUT)
 
     @pl.when((s >= 4) & (s < 8))
     def widen():
-        u = tile_across(m_out[layer], tile) + vec(BFC + s - 4)
+        u = across_k(m_out[layer], weights[step]) + vec(BFC + s - 4)
         u_out[layer, s - 4] = u
         g = 0.5 * u * (1.0 + jnp.tanh(GELU_A * (u + GELU_B * (u * u * u))))
         g_out[layer, s - 4] = g.astype(low)
 
     @pl.when(s >= 8)
     def narrow():
-        cur[...] += tile_along(g_out[layer, s - 8], tile)
+        cur[...] += along_k(g_out[layer, s - 8], weights[step])
 
     @pl.when(step == 2 * STEPS - 1)
     def last_norm():
@@ -1208,15 +1252,19 @@
             shape((tok, width), f32),
             shape((tok, width), low),
         ),
-        in_specs=[vmem] * 6 + tile_specs(width, lambda i: i),
+        in_specs=[vmem] * 6 + [pl.BlockSpec(memory_space=pltpu.HBM)],
         out_specs=(vmem,) * 11,
-        scratch_shapes=[pltpu.VMEM((tok, width), f32)],
+        scratch_shapes=[
+            pltpu.VMEM((tok, width), f32),
+            pltpu.VMEM((2 * STEPS, width, width), low),
+            pltpu.SemaphoreType.DMA((2 * STEPS,)),
+        ],
         compiler_params=pltpu.CompilerParams(vmem_limit_bytes=58 * 2**20),
         cost_estimate=pl.CostEstimate(
             flops=2 * tok * mats.size, bytes_accessed=2 * mats.size, transcendentals=0
         ),
         name="forward_layers",
-    )(hot, rows, pos_hot, pos, mask, vecs, mats, mats, mats)
+    )(hot, rows, pos_hot, pos, mask, vecs, mats)
 
 
 def backward_kernel(
@@ -1233,9 +1281,7 @@
     u_ref,
     g_ref,
     hot_ref,
-    w_0,
-    w_1,
-    w_2,
+    mats_ref,
     dx_out,
     vec_out,
     rows_out,
@@ -1244,16 +1290,15 @@
     wide,
     du_s,
     dqkv_s,
-    left_s,
-    right_s,
-    own_s,
-    send_s,
-    recv_s,
-    acc_0,
-    acc_1,
-    send_pair,
-    recv_pair,
-    local,
+    lefts,
+    rights,
+    right_send,
+    weights,
+    ready,
+    send_left,
+    recv_left,
+    send_right,
+    recv_right,
 ):
     step = pl.program_id(0)
     layer, s = 1 - lax.div(step, STEPS), lax.rem(step, STEPS)
@@ -1264,7 +1309,7 @@
     at, core = place()
     sibling = device_at(at, 1 - core)
     last = 2 * STEPS
-    tile = (w_0, w_1, w_2)
+    slot = lax.rem(step, 4)
 
     def vec(row):
         return vec_ref[layer * STEPS + row]
@@ -1272,68 +1317,63 @@
     def put(row, value):
         vec_out[layer * STEPS + row] = value
 
-    def pair_copy(slot):
+    def to_sibling(src, dst, send, recv):
         return pltpu.make_async_remote_copy(
-            src_ref=send_s.at[slot],
-            dst_ref=recv_s.at[slot],
-            send_sem=send_pair.at[slot],
-            recv_sem=recv_pair.at[slot],
+            src_ref=src,
+            dst_ref=dst,
+            send_sem=send,
+            recv_sem=recv,
             device_id=sibling,
             device_id_type=pl.DeviceIdType.MESH,
         )
 
-    def set_right(value):
-        right_s[:, :half] = jnp.where(core == 0, value[:, :half], value[:, half:])
-        right_s[:, half:] = jnp.where(core == 0, value[:, half:], value[:, :half])
+    def left_copy(n):
+        return to_sibling(
+            lefts.at[n, pl.ds(0, tok)],
+            lefts.at[n, pl.ds(tok, tok)],
+            send_left.at[n],
+            recv_left.at[n],
+        )
+
+    def right_copy(n):
+        return to_sibling(
+            right_send.at[n], rights.at[n, pl.ds(tok, tok)], send_right.at[n], recv_right.at[n]
+        )
+
+    def set_left(value):
+        lefts[slot, :tok, :] = value
+
+    def set_right(n, value):
+        pl.when(step >= STEPS)(lambda: right_copy(n).wait_send())
+        rights[n, :tok, :] = jnp.where(core == 0, value[:, :half], value[:, half:])
+        right_send[n] = jnp.where(core == 0, value[:, half:], value[:, :half])
 
     @pl.when(step == 0)
     def enter():
+        for n in range(last):
+            tile = STEPS * (1 - n // STEPS) + TILE_ORDER[n % STEPS]
+            tile_copy(mats_ref, weights, ready, tile, n).start()
         greet([sibling])
         dx, dg, ds = norm_back(grad_ref[...], hidden_ref[...], vec_ref[last])
         cur[...] = dx
         vec_out[last] = dg
         vec_out[last + 1] = ds
 
-    def collect(before):
-        slot, b = before % 2, before % STEPS
-        acc = acc_1 if before < STEPS else acc_0
-        tile_at = TILE_ORDER[b]
-        pair_copy(slot).wait_recv()
-        granule = acc.shape[4]
-        count = width // granule
-        for g in range(count):
-            block, p = divmod(tile_at * count + g, 3)
-            here = slice(g * granule, (g + 1) * granule)
-            value = own_s[here, :].astype(f32) + recv_s[slot, here, :].astype(f32)
-            acc[block // (RING * RING), block // RING % RING, block % RING, p] = value.astype(low)
-
-    for n in range(1, last + 1):
-        pl.when(step == n)(lambda n=n: collect(n - 1))
-
-    def leave_copies(layer, acc):
-        return [
-            pltpu.make_async_copy(
-                acc.at[n // RING, n % RING],
-                acc_out.at[layer, n // RING, n % RING],
-                local.at[layer * RING * RING + n],
-            )
-            for n in range(RING * RING)
-        ]
-
-    @pl.when(step == STEPS)
-    def leave_second():
-        for op in leave_copies(1, acc_1):
-            op.start()
+    @pl.when(step < last)
+    def arrived():
+        tile_copy(mats_ref, weights, ready, 0, step).wait()
+
+    pl.when((step >= 4) & (step < last))(lambda: left_copy(slot).wait_send())
 
     @pl.when((s == 0) & (step < last))
     def begin():
         put(BOUT, jnp.sum(cur[...], 0, keepdims=True))
-        set_right(cur[...].astype(low))
+        set_right(0, cur[...].astype(low))
         wide[...] = cur[...].astype(low)
 
     @pl.when((s < 4) & (step < last))
     def through_gelu():
-        dg = tile_across(wide[...], tile)
+        dg = across_k(wide[...], weights[step])
         u = u_ref[layer, s]
         square = u * u
         t = jnp.tanh(GELU_A * (u + GELU_B * (square * u)))
@@ -1341,18 +1381,18 @@
         du = dg * slope
         put(BFC + s, jnp.sum(du, 0, keepdims=True))
         du_s[s] = du.astype(low)
-        left_s[...] = g_ref[layer, s]
+        set_left(g_ref[layer, s])
 
     @pl.when(s == 4)
     def begin_fc():
-        set_right(m_ref[layer])
+        set_right(1, m_ref[layer])
         dx_out[...] = jnp.zeros_like(dx_out)
 
     @pl.when((s >= 4) & (s < 8))
     def through_fc():
         left = du_s[s - 4]
-        dx_out[...] += tile_along(left, tile)
-        left_s[...] = left
+        dx_out[...] += along_k(left, weights[step])
+        set_left(left)
 
     @pl.when(s == 8)
     def through_attention():
@@ -1362,9 +1402,9 @@
         cur[...] = cur[...] + dx
         put(BPROJ, jnp.sum(cur[...], 0, keepdims=True))
         mid_low = cur[...].astype(low)
-        left_s[...] = mid_low
-        set_right(o_ref[layer])
-        wide[...] = tile_along(mid_low, tile).astype(low)
+        set_left(mid_low)
+        set_right(2, o_ref[layer])
+        wide[...] = along_k(mid_low, weights[step]).astype(low)
         lanes = lax.broadcasted_iota(jnp.int32, (1, 2 * head_dim), 1)
         scale = head_dim ** (-0.5)
         for pair in range(H // 2):
@@ -1395,23 +1435,34 @@
 
     @pl.when(s == 9)
     def begin_qkv():
-        set_right(a_ref[layer])
+        set_right(3, a_ref[layer])
         dx_out[...] = jnp.zeros_like(dx_out)
 
     @pl.when(s >= 9)
     def through_qkv():
         left = dqkv_s[s - 9]
-        dx_out[...] += tile_along(left, tile)
-        left_s[...] = left
+        dx_out[...] += along_k(left, weights[step])
+        set_left(left)
+
+    def kind_of(at_s):
+        return jnp.where(at_s < 4, 0, jnp.where(at_s < 8, 1, jnp.where(at_s == 8, 2, 3)))
+
+    def fresh(at_s):
+        return (at_s == 0) | (at_s == 4) | (at_s == 8) | (at_s == 9)
+
+    @pl.when(step >= 2)
+    def gradient():
+        slot_then, s_then = lax.rem(step - 2, 4), lax.rem(step - 2, STEPS)
+        kind = kind_of(s_then)
+        left_copy(slot_then).wait_recv()
+        pl.when(fresh(s_then))(lambda: right_copy(kind).wait_recv())
+        grad = over_rows(lefts[slot_then], rights[kind])
+        acc_out[0] = grad.astype(low).reshape(acc_out.shape[1:])
 
     @pl.when(step < last)
-    def gradient():
-        slot = lax.rem(step, 2)
-        grad = over_rows(left_s[...], right_s[...])
-        pl.when(step >= 2)(lambda: pair_copy(slot).wait_send())
-        own_s[...] = grad[:, :half].astype(low)
-        send_s[slot] = grad[:, half:].astype(low)
-        pair_copy(slot).start()
+    def share():
+        left_copy(slot).start()
+        pl.when(fresh(s))(lambda: right_copy(kind_of(s)).start())
 
     @pl.when(s == STEPS - 1)
     def end_layer():
@@ -1420,18 +1471,14 @@
         put(S1, ds)
         cur[...] = cur[...] + dx
 
-    @pl.when(step == last)
+    @pl.when(step == last + 1)
     def leave():
-        for op in leave_copies(0, acc_0):
-            op.start()
         dx_out[...] = cur[...]
         rows = over_rows(hot_ref[...], cur[...].astype(low)).astype(low)
         rows_out[...] = rows.reshape(rows_out.shape)
-        for slot in range(2):
-            pair_copy(slot).wait_send()
-        for layer_at, acc in ((1, acc_1), (0, acc_0)):
-            for op in leave_copies(layer_at, acc):
-                op.wait()
+        for n in range(4):
+            left_copy(n).wait_send()
+            right_copy(n).wait_send()
 
 
 def backward_layers(grad, hidden, vecs, saved, hot, mats):
@@ -1440,41 +1487,44 @@
     shape = jax.ShapeDtypeStruct
     vmem = pl.BlockSpec(memory_space=pltpu.VMEM)
     hbm = pl.BlockSpec(memory_space=pltpu.HBM)
-    torus, half, part = (RING, RING, RING), width // 2, 48
+    half, part = width // 2, 48
+    granules = width // part
 
     def tile(i):
-        i = jnp.minimum(i, 2 * STEPS - 1)
+        i = jnp.clip(i - 2, 0, 2 * STEPS - 1)
         layer, s = 1 - i // STEPS, i % STEPS
-        return layer * STEPS + jnp.where(
-            s < 4, 8 + s, jnp.where(s < 8, s, jnp.where(s == 8, 3, s - 9))
+        return (
+            layer,
+            jnp.where(s < 4, 8 + s, jnp.where(s < 8, s, jnp.where(s == 8, 3, s - 9))),
+            0,
+            0,
         )
 
     return pl.pallas_call(
         backward_kernel,
-        grid=(2 * STEPS + 1,),
+        grid=(2 * STEPS + 2,),
         out_shape=(
             shape((tok, width), f32),
             shape((2 * STEPS + 2, 1, width), f32),
             shape((RING, 2, 32, width), low),
-            shape((2,) + torus + (3, part, half), low),
+            shape((2, STEPS * granules, part, half), low),
         ),
-        in_specs=[vmem] * 13 + tile_specs(width, tile),
-        out_specs=(vmem, vmem, vmem, hbm),
+        in_specs=[vmem] * 13 + [hbm],
+        out_specs=(vmem, vmem, vmem, pl.BlockSpec((1, granules, part, half), tile)),
         scratch_shapes=[
             pltpu.VMEM((tok, width), f32),
             pltpu.VMEM((tok, width), low),
             pltpu.VMEM((4, tok, width), low),
             pltpu.VMEM((3, tok, width), low),
-            pltpu.VMEM((tok, width), low),
-            pltpu.VMEM((tok, width), low),
-            pltpu.VMEM((width, half), low),
-            pltpu.VMEM((2, width, half), low),
-            pltpu.VMEM((2, width, half), low),
-            pltpu.VMEM(torus + (3, part, half), low),
-            pltpu.VMEM(torus + (3, part, half), low),
-            pltpu.SemaphoreType.DMA((2,)),
-            pltpu.SemaphoreType.DMA((2,)),
-            pltpu.SemaphoreType.DMA((2 * RING * RING,)),
+            pltpu.VMEM((4, 2 * tok, width), low),
+            pltpu.VMEM((4, 2 * tok, half), low),
+            pltpu.VMEM((4, tok, half), low),
+            pltpu.VMEM((2 * STEPS, width, width), low),
+            pltpu.SemaphoreType.DMA((2 * STEPS,)),
+            pltpu.SemaphoreType.DMA((4,)),
+            pltpu.SemaphoreType.DMA((4,)),
+            pltpu.SemaphoreType.DMA((4,)),
+            pltpu.SemaphoreType.DMA((4,)),
         ],
         compiler_params=pltpu.CompilerParams(
             collective_id=4, has_side_effects=True, vmem_limit_bytes=60 * 2**20
@@ -1483,7 +1533,7 @@
             flops=4 * tok * mats.size, bytes_accessed=2 * mats.size, transcendentals=0
         ),
         name="backward_layers",
-    )(grad, hidden, vecs, *saved, hot, mats, mats, mats)
+    )(grad, hidden, vecs, *saved, hot, mats)
 
 
 def doc_info(doc_lens, tok_count, total_docs):
@@ -1628,10 +1678,7 @@
     grad_final, table_part, token_losses = head(
         final_low, jnp.broadcast_to(codes[None, :], (8, tok)), weight_group, table_slice
     )
-    loss_part = jnp.sum(token_losses)
-    table_grad = lax.psum_scatter(table_part, "dp", scatter_dimension=0, tiled=True)[
-        :own_rows
-    ].astype(jnp.float32)
+    table_part = lax.psum_scatter(table_part, "dp", scatter_dimension=0, tiled=True)
     grad_hidden, grad_vecs, rows_back, grad_acc = backward_layers(
         grad_final, hidden, vec_rows, saved, slot_hot, mats_all
     )
@@ -1646,26 +1693,31 @@
             [grad_pos.reshape(devices, -1), grad_vecs.reshape(devices, -1)], 1
         )
     )
-    mats_shard, small_shard, back_grads = reduce_weights(grad_acc, small_grads, rows_back, swap)
+    mats_shard, small_shard, back_grads = reduce_weights(grad_acc.reshape(2, RING, RING, RING, 3, 48, width // 2), small_grads, rows_back, swap)
+    both_sums, table_grad = sum_all(
+        table_part,
+        asked,
+        back_grads.reshape(slot_count, width),
+        mats_shard,
+        small_shard,
+        token_losses,
+    )
     small_shard = small_shard.reshape(-1)
     pos_shard = small_shard[: pos_rows * pos_cols].reshape(pos_cols, pos_rows)
     vec_shard = small_shard[pos_rows * pos_cols : pos_rows * pos_cols + vec_own]
-    table_grad = table_grad + contract(asked, back_grads.reshape(slot_count, width), 0, 0)[:own_rows]
-    local_squares = (
-        jnp.sum(table_grad * table_grad)
-        + jnp.sum(mats_shard * mats_shard)
-        + jnp.sum(pos_shard * pos_shard)
-        + jnp.sum(vec_shard * vec_shard)
-    )
-    both_sums = sum_all(
-        jnp.broadcast_to(jnp.pad(jnp.stack([loss_part, local_squares]), (0, 6))[:, None], (8, LANES))
-    )
     loss_sum, squares = both_sums[0, 0], both_sums[1, 0]
     grad_norm = jnp.sqrt(squares)
     factor = clip_bound / jnp.maximum(grad_norm, clip_bound)
-    embed_out = renew(embed_table, embed_moment, embed_average, table_grad, factor)
-    block_out = renew(blocks, block_moment, block_average, mats_shard, factor)
-    block_out = tuple(jnp.transpose(item, (0, 2, 1)) for item in block_out)
+    own_shape = blocks.shape
+    flat = lambda item: item.reshape(-1, width)
+    embed_out, block_out = update(
+        both_sums,
+        (embed_table, embed_moment, embed_average, table_grad),
+        (flat(blocks), flat(block_moment), flat(block_average), flat(mats_shard)),
+    )
+    block_out = tuple(
+        jnp.transpose(item.reshape(own_shape), (0, 2, 1)) for item in block_out
+    )
     pos_out = renew(
         jnp.transpose(pos_table),
         jnp.transpose(pos_moment),
@@ -1675,7 +1727,7 @@
     )
     pos_out = tuple(jnp.transpose(item) for item in pos_out)
     vector_out = renew(vectors, vector_moment, vector_average, vec_shard, factor)
-    return (loss_sum, grad_norm) + embed_out + block_out + pos_out + vector_out
+    return (loss_sum, grad_norm) + tuple(embed_out) + block_out + pos_out + vector_out
 
 
 def solution(mesh):

time: 478 us -> 437 us (0.914)
  Pallas kernels: 423 us -> 387 us
  other arithmetic: 22.8 us -> 12.5 us
  local copies, waits for them, and re-layouts: 9.15 us -> 18 us
    pallas_call x2 -> x3, Pallas kernels: 102 us -> 54.3 us  [the longest x1 37 us: backward_layers(): pl.pallas_call(backward_kernel, grid=(2 * STEPS + 2,), out_shape=(shape((...]
    pallas_call x1, Pallas kernels: 81.4 us -> 101 us  [reduce_weights(): pl.pallas_call(reduce_kernel, out_shape=(jax.ShapeDtypeStruct((2, rows //...]
    unnamed x47 -> x55, local copies, waits for them, and re-layouts: 2.59 us -> 12.9 us
    pallas_call x1, Pallas kernels: 32.9 us -> 26 us  [forward_layers(): pl.pallas_call(forward_kernel, grid=(2 * STEPS,), out_shape=(shape((2, to...]
    reduce_sum x4 -> x0, other arithmetic: 4.97 us -> none  [the longest x1 1.73 us: per_device(): jnp.sum(mats_shard * mats_shard)]
  transfers between devices with their start and end apart: 2 -> 2, of which waited for: 0 -> 0; matrix products, arithmetic and copies ran while one was open for 4% -> 3% of each run, Pallas kernels for 69% -> 67%
where the time goes in v6:
time: 437 us; the launch traced here: 436 us
  Pallas kernels  387 us (89%)
  local copies, waits for them, and re-layouts  18 us (4%)
  between operations  16.2 us (4%)
  other arithmetic  12.5 us (3%)
    pallas_call x1, Pallas kernels, gather_weights(): pl.pallas_call(gather_kernel, out_shape=(jax.ShapeDtypeStruct((layers, RI...  128 us
    pallas_call x1, Pallas kernels, reduce_weights(): pl.pallas_call(reduce_kernel, out_shape=(jax.ShapeDtypeStruct((2, rows //...  101 us
    pallas_call x1, Pallas kernels, head(): pl.pallas_call(head_kernel, out_shape=(jax.ShapeDtypeStruct((tok, width),...  78.1 us
    pallas_call x1, Pallas kernels, backward_layers(): pl.pallas_call(backward_kernel, grid=(2 * STEPS + 2,), out_shape=(shape((...  37 us
    pallas_call x1, Pallas kernels, forward_layers(): pl.pallas_call(forward_kernel, grid=(2 * STEPS,), out_shape=(shape((2, to...  26 us
    pallas_call x1, Pallas kernels, sum_all(): pl.pallas_call(sum_kernel, out_shape=(jax.ShapeDtypeStruct(value, jnp.flo...  14 us
    unnamed x55, local copies, waits for them, and re-layouts  12.9 us
  transfers between devices with their start and end apart: 2, of which 0 were waited for; matrix products, arithmetic and copies ran while one was open for 3% of the time, Pallas kernels for 67%

profile of v6, /device:TPU:0, one launch (start us, length us, event | category | flops | bytes accessed | tf_op | source)
XLA Modules:
  0.0 435.8 jit_solution(10819512512637127558)
XLA Ops:
  7.2 1.4 convert_element_type.76
  8.6 0.9 pad.13.table_ref
  13.5 128.0 %gather_weights.1 = (bf16[2,4,4,4,144,768]{5,4,3,2,1,0:T(8,128)(2,1)}, bf16[4,4,4,2,16,128]{5,4,3,2,1,0:T(8,128)(2,1)}, bf16[4,2,32,768]{3,2,1,0:T(8,128)(2,1)}, bf16[256,400]{1,0:T(8,128)(2,1)}) custom-call(f32[2,72,768]{2,1,0:T(8,128)} %bitcast.78, bf16[16,128]{1,0:T(8,128)(2,1)} %maximum_maximum_fusion.small_ref, bf16[400,768]{1,0:T(8,128)(2,1)} %pad.13.table_ref, ...), custom_call_target="tpu_custom_call" | custom-call | bytes 250000000 | tf_op jit(solution)/shard_map/gather_weights/pallas_call | solution.py:293
  141.5 1.2 copy.53
  142.7 1.0 reshape.246.pos_ref
  147.8 26.0 %forward_layers.1 = (f32[2,128,768]{2,1,0:T(8,128)}, bf16[2,128,768]{2,1,0:T(8,128)(2,1)}, bf16[2,3,128,768]{3,2,1,0:T(8,128)(2,1)}, f32[2,12,128,128]{3,2,1,0:T...) custom-call(bf16[128,256]{1,0:T(8,128)(2,1)} %fusion.3.hot_ref, ...), custom_call_target="tpu_custom_call" | custom-call | flops 3623878656 | bytes 28311552 | tf_op jit(solution)/shard_map/forward_layers/pallas_call | solution.py:1239
  174.4 78.1 %head.1 = (f32[128,768]{1,0:T(8,128)}, bf16[6400,768]{1,0:T(8,128)(2,1)}, f32[8,128]{1,0:T(8,128)}) custom-call(bf16[128,768]{1,0:T(8,128)(2,1)} %get-tuple-element.56.f_ref, s32[8,128]{1,0:T(8,128)} %broadcast_in_dim.24.code_ref, f32[8,128]{1,0:T(8,128)} %divide_multiply_fusion.weight_ref, bf16[6400,768]{1,0:T(8,128)(2,1)} %all-gather.2.cloned.1.call-done.table_ref), custom_call_target="tpu_custom_call" | custom-call | flops 30198988800 | bytes 19660800 | tf_op jit(solution)/shard_map/head/pallas_call | solution.py:1056
  252.5 37.0 %backward_layers.1 = (f32[128,768]{1,0:T(8,128)}, f32[26,1,768]{2,1,0:T(1,128)}, bf16[4,2,32,768]{3,2,1,0:T(8,128)(2,1)}, bf16[2,192,48,384]{3,2,1,0:T(8,128)(2,1)}) custom-call(f32[128,768]{1,0:T(8,128)} %get-tuple-element.59.grad_ref, f32[128,768]{1,0:T(8,128)} %get-tuple-element.60.hidden_ref, f32[26,1,768]{2,1,0:T(1,128)} %reshape.262.vec_ref, ...), custom_call_target="tpu_custom_call" | custom-call | flops 7247757312 | bytes 28311552 | tf_op jit(solution)/shard_map/backward_layers/pallas_call | solution.py:1503
  289.5 1.1 reduce
  290.8 1.5 fusion.5
  292.7 1.2 copy.48
  293.9 101.0 %reduce_weights.1 = (f32[2,72,768]{2,1,0:T(8,128)}, f32[16,128]{1,0:T(8,128)}, bf16[4,4,16,768]{3,2,1,0:T(8,128)(2,1)}) custom-call(bf16[2,4,4,4,3,48,384]{6,5,4,3,2,1,0:T(8,128)(2,1)} %bitcast.88, f32[4,4,4,2,16,128]{5,4,3,2,1,0:T(8,128)} %bitcast.89, bf16[4,2,32,768]{3,2,1,0:T(8,128)(2,1)} %get-tuple-element.73.rows_ref, ...), custom_call_target="tpu_custom_call" | custom-call | bytes 280000000 | tf_op jit(solution)/shard_map/reduce_weights/pallas_call | solution.py:673
  395.0 1.1 copy-done.2
  396.1 1.1 copy-done.8
  397.2 1.0 copy-done.11
  398.2 0.9 copy-done.12
  399.8 14.0 %sum_all.1 = (f32[8,128]{1,0:T(8,128)S(1)}, f32[400,768]{1,0:T(8,128)S(1)}) custom-call(bf16[400,768]{1,0:T(8,128)(2,1)S(1)} %copy-done.8, bf16[256,400]{1,0:T(8,128)(2,1)S(1)} %copy-done.12, bf16[256,768]{1,0:T(8,128)(2,1)S(1)} %bitcast.83, f32[2,72,768]{2,1,0:T(8,128)S(1)} %copy-done.2, f32[16,128]{1,0:T(8,128)S(1)} %copy-done.13, f32[8,128]{1,0:T(8,128)S(1)} %copy-done.14), custom_call_target="tpu_custom_call" | custom-call | bytes 40000000 | tf_op jit(solution)/shard_map/sum_all/pallas_call | solution.py:768
  413.8 1.0 copy-done.6
  416.9 1.3 fusion.41
  420.0 1.0 copy-done.3
  421.0 1.3 copy-done.5
  422.3 1.3 copy-done.7
  423.6 1.0 copy-done.10
  424.6 3.2 update.1
  (91 shorter events, 13.0 us)
Async XLA Ops:
  7.2 166.6 %all-gather.2.cloned.1.call-start = ((), (), s32[]{:S(2)}) async-start(), calls=%async_computation.1 | async-start | bytes 10444800 | tf_op jit(solution)/shard_map/all_gather | solution.py:1615
  8.6 1.0 copy-start.16
  8.6 1.1 copy-start.17
  8.6 1.9 copy-start.25
  9.5 385.4 %reduce-scatter.2.cloned.1.call-start = ((), (), s32[]{:S(2)}) async-start(), calls=%async_computation.2 | async-start | bytes 10444800 | tf_op jit(solution)/shard_map/reduce_scatter | solution.py:1681
  141.5 3.5 copy-start.24
  293.8 101.1 %copy-start.14 = (f32[8,128]{1,0:T(8,128)S(1)}, f32[8,128]{1,0:T(8,128)}, u32[]{:S(2)}) copy-start(f32[8,128]{1,0:T(8,128)} %get-tuple-element.77.loss_ref) | copy-start | bytes 12292
  293.8 123.0 %copy-start.23 = (f32[156]{0:T(256)S(1)}, f32[156]{0:T(256)}, u32[]{:S(2)}) copy-start(f32[156]{0:T(256)} %param.28) | copy-start | bytes 1876
  293.8 124.4 %copy-start.20 = (f32[80,6]{0,1:T(8,128)S(1)}, f32[80,6]{0,1:T(8,128)}, u32[]{:S(2)}) copy-start(f32[80,6]{0,1:T(8,128)} %param.25) | copy-start | bytes 5764
  293.8 125.0 %copy-start.18 = (f32[80,6]{0,1:T(8,128)S(1)}, f32[80,6]{0,1:T(8,128)}, u32[]{:S(2)}) copy-start(f32[80,6]{0,1:T(8,128)} %param.26) | copy-start | bytes 5764
  293.8 125.6 %copy-start.21 = (f32[156]{0:T(256)S(1)}, f32[156]{0:T(256)}, u32[]{:S(2)}) copy-start(f32[156]{0:T(256)} %param.29) | copy-start | bytes 1876
  293.9 126.1 %copy-start.4 = (f32[393,768]{1,0:T(8,128)S(1)}, f32[393,768]{1,0:T(8,128)}, u32[]{:S(2)}) copy-start(f32[393,768]{1,0:T(8,128)} %refs_1_.1) | copy-start | bytes 3621892
  293.9 126.1 %copy-start.9 = (f32[2,768,72]{1,2,0:T(8,128)S(1)}, f32[2,768,72]{1,2,0:T(8,128)}, u32[]{:S(2)}) copy-start(f32[2,768,72]{1,2,0:T(8,128)} %param.22) | copy-start | bytes 1327108
  394.9 25.1 %copy-start = (f32[393,768]{1,0:T(8,128)S(1)}, f32[393,768]{1,0:T(8,128)}, u32[]{:S(2)}) copy-start(f32[393,768]{1,0:T(8,128)} %refs_0_.1) | copy-start | bytes 3621892
  394.9 25.1 %copy-start.1 = (f32[2,768,72]{1,2,0:T(8,128)S(1)}, f32[2,768,72]{1,2,0:T(8,128)}, u32[]{:S(2)}) copy-start(f32[2,768,72]{1,2,0:T(8,128)} %param.21) | copy-start | bytes 1327108
  395.0 1.1 copy-start.2
  396.1 1.1 copy-start.8
  413.8 1.0 copy-start.6
  418.2 9.6 %copy-start.19 = (f32[156]{0:T(256)}, f32[156]{0:T(256)S(1)}, u32[]{:S(2)}) copy-start(f32[156]{0:T(256)S(1)} %get-tuple-element.91) | copy-start | bytes 1876
  418.8 9.0 %copy-start.15 = (f32[6,80]{1,0:T(8,128)}, f32[6,80]{1,0:T(8,128)S(1)}, u32[]{:S(2)}) copy-start(f32[6,80]{1,0:T(8,128)S(1)} %get-tuple-element.94) | copy-start | bytes 5764
  420.0 1.0 copy-start.3
  421.0 1.3 copy-start.5
  422.3 1.3 copy-start.7
  423.6 1.0 copy-start.10
  (4 other events, 3.6 us)
Sparse Core Ops, SparseCore 0:
  10.7 127.3 all-gather.1
  252.6 106.0 reduce-scatter.1

commit v7 on v6

--- a/solution.py
+++ b/solution.py
@@ -2,6 +2,8 @@
 
 import jax
 import jax.numpy as jnp
+import ml_dtypes
+import numpy as np
 from jax import lax
 from jax.experimental import pallas as pl
 from jax.experimental.pallas import tpu as pltpu
@@ -326,6 +328,9 @@
     )
 
 
+SUM_PARTS = ((0, 2), (2, 5), (7, 2))
+
+
 class Reduction:
     def __init__(self, at, core, send, recv):
         self.at, self.core, self.send, self.recv = at, core, send, recv
@@ -356,32 +361,39 @@
         return c, lax.rem(c + 1, RING), lax.rem(c + 2, RING), lax.rem(c + 3, RING), right, left
 
     def index(self, layer, p, step, c, piece=None):
-        part = 48
         cut, whole = (0, RING) if piece is None else (2 * piece, 2), (0, RING)
         if step == 0:
             free, unused = self.axes(p)
             spot = [c, c, c]
             spot[free[0]], spot[free[1]] = cut, whole
-            return spot + [p]
+            return spot + [pl.ds(*SUM_PARTS[p])]
         if step == 1:
             unused, first = self.axes(p)
             spot = [cut, cut]
             spot[first] = c
-            return [layer % self.level[1].shape[0], p] + spot
+            return [layer] + spot
         if piece is None:
-            return [layer, p, c]
-        return [layer, p, c, pl.ds(0, 32) if piece == 0 else pl.ds(32, part - 32)]
+            return [layer, c]
+        return [layer, c, pl.ds(*self.cut(p, piece))]
+
+    def cut(self, p, piece):
+        count = SUM_PARTS[p][1]
+        first = (count + 1) // 2
+        return (0, first) if piece == 0 else (first, count - first)
 
     def view(self, layer, p, step, c, piece=None):
         index = self.index(layer, p, step, c, piece)
-        held = self.level[0, layer] if step == 0 else self.level[step]
+        held = self.held(layer, p, step)
         return held.at[tuple(pl.ds(*item) if isinstance(item, tuple) else item for item in index)]
 
+    def held(self, layer, p, step):
+        return self.level[0, layer] if step == 0 else self.level[step][p]
+
     def slot(self, layer, p, step, side, whole):
-        store = (self.fulls if whole else self.halves)[step]
+        store = (self.fulls if whole else self.halves)[step][p]
         if step == 2 and not whole:
-            return store.at[layer, p, side, pl.ds(0, 32 if side == 0 else 16)]
-        return store.at[layer % store.shape[0], p, side]
+            return store.at[layer, side, pl.ds(0, self.cut(p, side)[1])]
+        return store.at[layer, side]
 
     def half_copies(self, layer, p, step):
         unused, after, across, before, right, left = self.ring(p, step)
@@ -412,7 +424,7 @@
         return out
 
     def add(self, layer, p, step, c, piece, terms, into):
-        held = self.level[0, layer] if step == 0 else self.level[step]
+        held = self.held(layer, p, step)
         index = self.index(layer, p, step, c, piece)
         sizes = [item[1] for item in index if isinstance(item, tuple)]
 
@@ -423,7 +435,7 @@
             )
             value = held[spot].astype(jnp.float32)
             for term in terms:
-                value = value + term[tuple(inner) + (slice(None), slice(None))].astype(jnp.float32)
+                value = value + term[tuple(inner) + (slice(None),) * 3].astype(jnp.float32)
             into(held, spot, inner, value)
 
         def body(n, unused):
@@ -467,11 +479,12 @@
 
             def up(held, spot, inner, value, p=p):
                 if step == 2:
-                    self.final[layer, p * 48 : (p + 1) * 48] = value
+                    first, count = SUM_PARTS[p]
+                    rows = value.reshape(count * value.shape[1], value.shape[2])
+                    self.final[layer, 16 * first : 16 * (first + count)] = rows
                 else:
-                    target = self.level[step + 1]
-                    spot = (layer % target.shape[0], p) + tuple(inner)
-                    target[spot] = value.astype(target.dtype)
+                    target = self.level[step + 1][p]
+                    target[(layer,) + tuple(inner)] = value.astype(target.dtype)
 
             self.add(layer, p, step, c, None, terms, up)
 
@@ -491,14 +504,7 @@
     rows_out,
     acc_0,
     acc_1,
-    mid,
-    thin,
-    half_0,
-    half_1,
-    half_2,
-    full_0,
-    full_1,
-    full_2,
+    by_part,
     small_acc,
     small_sib,
     small_wide,
@@ -520,9 +526,9 @@
     own_rows, half = final_peer.shape[1], final_peer.shape[2]
     sibling = device_at(at, 1 - core)
     sums = Reduction(at, core, send, recv)
-    sums.level = {(0, 0): acc_0, (0, 1): acc_1, 1: mid, 2: thin}
-    sums.halves = {0: half_0, 1: half_1, 2: half_2}
-    sums.fulls = {0: full_0, 1: full_1, 2: full_2}
+    sums.level = {(0, 0): acc_0, (0, 1): acc_1, 1: by_part[0], 2: by_part[1]}
+    sums.halves = dict(enumerate(by_part[2:5]))
+    sums.fulls = dict(enumerate(by_part[5:8]))
     sums.final = final
 
     accs = (acc_0, acc_1)
@@ -663,8 +669,8 @@
 
 
 def reduce_weights(acc, small, rows_back, swap):
-    part, half = acc.shape[5:]
-    rows = 3 * part
+    granules, part, half = acc.shape[4:]
+    rows = granules * part
     torus = (RING, RING, RING)
     small_shape = small.shape[1:]
     hbm = pl.BlockSpec(memory_space=pltpu.HBM)
@@ -680,16 +686,21 @@
         in_specs=[hbm, hbm, vmem, vmem],
         out_specs=(vmem, vmem, vmem),
         scratch_shapes=[
-            pltpu.VMEM(torus + (3, part, half), low),
-            pltpu.VMEM(torus + (3, part, half), low),
-            pltpu.VMEM((2, 3, RING, RING, part, half), low),
-            pltpu.VMEM((2, 3, RING, part, half), low),
-            pltpu.VMEM((2, 3, 2, 2, RING, part, half), low),
-            pltpu.VMEM((2, 3, 2, 2, part, half), low),
-            pltpu.VMEM((2, 3, 2, 32, half), low),
-            pltpu.VMEM((2, 3, 2, RING, RING, part, half), low),
-            pltpu.VMEM((2, 3, 2, RING, part, half), low),
-            pltpu.VMEM((2, 3, 2, part, half), low),
+            pltpu.VMEM(torus + (granules, part, half), low),
+            pltpu.VMEM(torus + (granules, part, half), low),
+            [
+                [pltpu.VMEM(lead + (count(p), part, half), low) for p in range(3)]
+                for lead, count in (
+                    ((2, RING, RING), lambda p: SUM_PARTS[p][1]),
+                    ((2, RING), lambda p: SUM_PARTS[p][1]),
+                    ((2, 2, 2, RING), lambda p: SUM_PARTS[p][1]),
+                    ((2, 2, 2), lambda p: SUM_PARTS[p][1]),
+                    ((2, 2), lambda p: (SUM_PARTS[p][1] + 1) // 2),
+                    ((2, 2, RING, RING), lambda p: SUM_PARTS[p][1]),
+                    ((2, 2, RING), lambda p: SUM_PARTS[p][1]),
+                    ((2, 2), lambda p: SUM_PARTS[p][1]),
+                )
+            ],
             pltpu.VMEM(torus + small_shape, jnp.float32),
             pltpu.VMEM(torus + small_shape, jnp.float32),
             pltpu.VMEM((3, RING, RING) + small_shape, jnp.float32),
@@ -708,7 +719,7 @@
             pltpu.SemaphoreType.DMA((33,)),
         ],
         compiler_params=pltpu.CompilerParams(
-            collective_id=1, has_side_effects=True, vmem_limit_bytes=58 * 2**20
+            collective_id=1, has_side_effects=True, vmem_limit_bytes=44 * 2**20
         ),
         cost_estimate=pl.CostEstimate(flops=0, bytes_accessed=280 * 10**6, transcendentals=0),
         name="reduce_weights",
@@ -716,11 +727,18 @@
 
 
 def sum_kernel(
-    part_ref, asked_ref, back_ref, mats_ref, small_ref, loss_ref, out_ref, table_ref, slots, send, recv
+    part_ref, asked_ref, back_ref, mats_ref, small_ref, loss_ref, out_ref, table_ref, group, slots, send, recv
 ):
     at, core = place()
-    sibling = device_at(at, 1 - core)
-    greet(ring_peers(at, core))
+    members = group.shape[0]
+    peers = [
+        (lax.axis_index("dp"), lax.rem(lax.axis_index("vocab") + by, members))
+        for by in range(1, members)
+    ]
+    greet(
+        peers
+        + [device_at(moved(at, axis, by), core) for axis in range(2) for by in range(1, RING)]
+    )
     wires = Wires(send, recv)
     table = part_ref[...].astype(jnp.float32) + lax.dot_general(
         asked_ref[...],
@@ -738,26 +756,30 @@
     mats, small = mats_ref[...], small_ref[...]
     squares = total(table * table) + total(mats * mats) + total(small * small)
     rows = lax.broadcasted_iota(jnp.int32, out_ref.shape, 0)
-    slots[0, core] = jnp.where(rows == 0, total(loss_ref[...]), squares)
-    swap = wires.copy(slots.at[0, core], slots.at[0, core], sibling)
-    swap.wait_recv()
-    value = slots[0, 0] + slots[0, 1]
-    for axis in range(3):
-        slots[1 + axis, at[axis]] = value
+    vocab = lax.axis_index("vocab")
+    group[vocab] = jnp.where(rows == 0, total(loss_ref[...]), squares)
+    ops = [wires.copy(group.at[vocab], group.at[vocab], peer) for peer in peers]
+    for op in ops:
+        op.wait_recv()
+    value = group[0]
+    for m in range(1, members):
+        value = value + group[m]
+    for axis in range(2):
+        slots[axis, at[axis]] = value
         ops = []
         for by in range(1, RING):
             ops.append(
                 wires.copy(
-                    slots.at[1 + axis, at[axis]],
-                    slots.at[1 + axis, at[axis]],
+                    slots.at[axis, at[axis]],
+                    slots.at[axis, at[axis]],
                     device_at(moved(at, axis, by), core),
                 )
             )
         for op in ops:
             op.wait_recv()
-        value = slots[1 + axis, 0]
+        value = slots[axis, 0]
         for c in range(1, RING):
-            value = value + slots[1 + axis, c]
+            value = value + slots[axis, c]
     out_ref[...] = value
     wires.drain()
 
@@ -774,12 +796,13 @@
         in_specs=[vmem] * 6,
         out_specs=(vmem, vmem),
         scratch_shapes=[
-            pltpu.VMEM((4, RING) + value, jnp.float32),
-            pltpu.SemaphoreType.DMA((10,)),
-            pltpu.SemaphoreType.DMA((10,)),
+            pltpu.VMEM((8,) + value, jnp.float32),
+            pltpu.VMEM((2, RING) + value, jnp.float32),
+            pltpu.SemaphoreType.DMA((13,)),
+            pltpu.SemaphoreType.DMA((13,)),
         ],
         compiler_params=pltpu.CompilerParams(
-            collective_id=2, has_side_effects=True, vmem_limit_bytes=32 * 2**20
+            collective_id=2, has_side_effects=True, vmem_limit_bytes=24 * 2**20
         ),
         cost_estimate=pl.CostEstimate(flops=0, bytes_accessed=40 * 10**6, transcendentals=0),
         name="sum_all",
@@ -809,7 +832,7 @@
         out_shape=tuple(shapes),
         in_specs=[vmem] * 9,
         out_specs=(vmem,) * 8,
-        compiler_params=pltpu.CompilerParams(vmem_limit_bytes=40 * 2**20),
+        compiler_params=pltpu.CompilerParams(vmem_limit_bytes=32 * 2**20),
         name="update",
     )(sums, *table, *mats)
     return outs[:4], outs[4:]
@@ -1487,7 +1510,7 @@
     shape = jax.ShapeDtypeStruct
     vmem = pl.BlockSpec(memory_space=pltpu.VMEM)
     hbm = pl.BlockSpec(memory_space=pltpu.HBM)
-    half, part = width // 2, 48
+    half, part = width // 2, 16
     granules = width // part
 
     def tile(i):
@@ -1607,9 +1630,8 @@
     )
     pos_rows, pos_cols = pos_table.shape
     vec_own = vectors.shape[0]
-    table_low = embed_table.astype(low)
     pad_rows = -own_rows % 16
-    table_padded = jnp.pad(table_low, ((0, pad_rows), (0, 0)))
+    table_padded = jnp.pad(embed_table, ((0, pad_rows), (0, 0))).astype(low)
     slot_rows = own_rows + pad_rows
 
     table_slice = lax.all_gather(table_padded, "dp", axis=0, tiled=True)
@@ -1629,13 +1651,13 @@
         (owners % 8) * 32 + (owners // 8 % RING) * 8 + (owners // 32) * capacity + rank
     )
     slot_hot = (arrival[:, None] == slots[None, :]).astype(low)
-    spread = (slots[:, None] // capacity == jnp.arange(devices)[None, :]).astype(low)
-    earlier = (tokens[:, None] < tokens[None, :]).astype(low)
-    slot_number = jnp.broadcast_to((slots % capacity).astype(jnp.float32)[:, None], (slot_count, tok))
-    by_owner = (
-        (slots % 64 // 16) * 2 + slots // 64 * 8 + slots % 16 // 2 * 32 + slots % capacity
-    )
-    swap = (by_owner[:, None] == slots[None, :]).astype(low)
+    hot = lambda condition: condition.astype(ml_dtypes.bfloat16)
+    line, step = np.arange(slot_count), np.arange(tok)
+    spread = hot(line[:, None] // capacity == np.arange(devices)[None, :])
+    earlier = hot(step[:, None] < step[None, :])
+    slot_number = np.broadcast_to((line % capacity).astype(np.float32)[:, None], (slot_count, tok)).copy()
+    by_owner = line % 64 // 16 * 2 + line // 64 * 8 + line % 16 // 2 * 32 + line % capacity
+    swap = hot(by_owner[:, None] == line[None, :])
     values = jnp.concatenate([jnp.transpose(pos_table).reshape(-1), vectors]).astype(low)
     small = jnp.concatenate(
         [
@@ -1645,7 +1667,7 @@
         ]
     )
     mats_all, small_all, returned_rows, asked = gather_weights(
-        blocks, small, table_padded, spread, earlier, slot_number, jnp.transpose(swap)
+        blocks, small, table_padded, spread, earlier, slot_number, swap.T.copy()
     )
     small_all = small_all.reshape(devices, -1)
     pos_low_t = small_all[:, : pos_rows * pos_cols].reshape(width, pos_rows)
@@ -1693,7 +1715,7 @@
             [grad_pos.reshape(devices, -1), grad_vecs.reshape(devices, -1)], 1
         )
     )
-    mats_shard, small_shard, back_grads = reduce_weights(grad_acc.reshape(2, RING, RING, RING, 3, 48, width // 2), small_grads, rows_back, swap)
+    mats_shard, small_shard, back_grads = reduce_weights(grad_acc.reshape(2, RING, RING, RING, 9, 16, width // 2), small_grads, rows_back, swap)
     both_sums, table_grad = sum_all(
         table_part,
         asked,

time: 437 us -> 430 us (0.984)
  transfers between devices with their start and end apart: 2 -> 2, of which waited for: 0 -> 0; matrix products, arithmetic and copies ran while one was open for 3% -> 2% of each run, Pallas kernels for 67% -> 68%
where the time goes in v7:
time: 430 us; the launch traced here: 429 us
  Pallas kernels  386 us (90%)
  local copies, waits for them, and re-layouts  16.2 us (4%)
  between operations  16.2 us (4%)
  other arithmetic  9.02 us (2%)
    pallas_call x1, Pallas kernels, gather_weights(): pl.pallas_call(gather_kernel, out_shape=(jax.ShapeDtypeStruct((layers, RI...  127 us
    pallas_call x1, Pallas kernels, reduce_weights(): pl.pallas_call(reduce_kernel, out_shape=(jax.ShapeDtypeStruct((2, rows //...  102 us
    pallas_call x1, Pallas kernels, head(): pl.pallas_call(head_kernel, out_shape=(jax.ShapeDtypeStruct((tok, width),...  78 us
    pallas_call x1, Pallas kernels, backward_layers(): pl.pallas_call(backward_kernel, grid=(2 * STEPS + 2,), out_shape=(shape((...  37 us
    pallas_call x1, Pallas kernels, forward_layers(): pl.pallas_call(forward_kernel, grid=(2 * STEPS,), out_shape=(shape((2, to...  26 us
    pallas_call x1, Pallas kernels, sum_all(): pl.pallas_call(sum_kernel, out_shape=(jax.ShapeDtypeStruct(value, jnp.flo...  13.3 us
    unnamed x55, local copies, waits for them, and re-layouts  11.8 us
  transfers between devices with their start and end apart: 2, of which 0 were waited for; matrix products, arithmetic and copies ran while one was open for 2% of the time, Pallas kernels for 68%

profile of v7, /device:TPU:0, one launch (start us, length us, event | category | flops | bytes accessed | tf_op | source)
XLA Modules:
  0.0 429.3 jit_solution(5589857561502567267)
XLA Ops:
  7.2 1.4 convert.24
  8.6 0.9 pad.14.table_ref
  10.6 126.9 %gather_weights.1 = (bf16[2,4,4,4,144,768]{5,4,3,2,1,0:T(8,128)(2,1)}, bf16[4,4,4,2,16,128]{5,4,3,2,1,0:T(8,128)(2,1)}, bf16[4,2,32,768]{3,2,1,0:T(8,128)(2,1)}, bf16[256,400]{1,0:T(8,128)(2,1)}) custom-call(f32[2,72,768]{2,1,0:T(8,128)} %bitcast.79, bf16[16,128]{1,0:T(8,128)(2,1)} %maximum_maximum_fusion.small_ref, bf16[400,768]{1,0:T(8,128)(2,1)} %pad.14.table_ref, ...), custom_call_target="tpu_custom_call" | custom-call | bytes 250000000 | tf_op jit(solution)/shard_map/gather_weights/pallas_call | solution.py:295
  137.6 1.2 copy.58
  138.8 1.0 reshape.137.pos_ref
  139.9 0.8 reshape.153.vec_ref
  143.9 26.0 %forward_layers.1 = (f32[2,128,768]{2,1,0:T(8,128)}, bf16[2,128,768]{2,1,0:T(8,128)(2,1)}, bf16[2,3,128,768]{3,2,1,0:T(8,128)(2,1)}, f32[2,12,128,128]{3,2,1,0:T...) custom-call(bf16[128,256]{1,0:T(8,128)(2,1)} %fusion.1.hot_ref, ...), custom_call_target="tpu_custom_call" | custom-call | flops 3623878656 | bytes 28311552 | tf_op jit(solution)/shard_map/forward_layers/pallas_call | solution.py:1262
  170.5 78.0 %head.1 = (f32[128,768]{1,0:T(8,128)}, bf16[6400,768]{1,0:T(8,128)(2,1)}, f32[8,128]{1,0:T(8,128)}) custom-call(bf16[128,768]{1,0:T(8,128)(2,1)} %get-tuple-element.56.f_ref, s32[8,128]{1,0:T(8,128)} %broadcast_in_dim.25.code_ref, f32[8,128]{1,0:T(8,128)} %divide_multiply_fusion.weight_ref, bf16[6400,768]{1,0:T(8,128)(2,1)} %all-gather.2.cloned.1.call-done.table_ref), custom_call_target="tpu_custom_call" | custom-call | flops 30198988800 | bytes 19660800 | tf_op jit(solution)/shard_map/head/pallas_call | solution.py:1079
  248.6 37.0 %backward_layers.1 = (f32[128,768]{1,0:T(8,128)}, f32[26,1,768]{2,1,0:T(1,128)}, bf16[4,2,32,768]{3,2,1,0:T(8,128)(2,1)}, bf16[2,576,16,384]{3,2,1,0:T(8,128)(2,1)}) custom-call(f32[128,768]{1,0:T(8,128)} %get-tuple-element.59.grad_ref, f32[128,768]{1,0:T(8,128)} %get-tuple-element.60.hidden_ref, f32[26,1,768]{2,1,0:T(1,128)} %reshape.153.vec_ref, ...), custom_call_target="tpu_custom_call" | custom-call | flops 7247757312 | bytes 28311552 | tf_op jit(solution)/shard_map/backward_layers/pallas_call | solution.py:1526
  285.6 1.1 reduce
  286.9 1.5 fusion.2
  288.9 0.8 copy-done.11
  289.8 101.7 %reduce_weights.1 = (f32[2,72,768]{2,1,0:T(8,128)S(1)}, f32[16,128]{1,0:T(8,128)S(1)}, bf16[4,4,16,768]{3,2,1,0:T(8,128)(2,1)S(1)}) custom-call(bf16[2,4,4,4,9,16,384]{6,5,4,3,2,1,0:T(8,128)(2,1)} %bitcast.89, f32[4,4,4,2,16,128]{5,4,3,2,1,0:T(8,128)S(1)} %bitcast.78, bf16[4,2,32,768]{3,2,1,0:T(8,128)(2,1)S(1)} %copy-done.11, bf16[256,256]{1,0:T(8,128)(2,1)S(1)} %copy-done.13), custom_call_target="tpu_custom_call" | custom-call | bytes 280000000 | tf_op jit(solution)/shard_map/reduce_weights/pallas_call | solution.py:679
  391.5 0.7 copy-done.9
  392.3 1.2 copy-done.6
  393.5 1.0 copy-done.10
  394.5 0.9 copy-done.12
  395.4 13.3 %sum_all.1 = (f32[8,128]{1,0:T(8,128)S(1)}, f32[400,768]{1,0:T(8,128)S(1)}) custom-call(bf16[400,768]{1,0:T(8,128)(2,1)S(1)} %copy-done.6, bf16[256,400]{1,0:T(8,128)(2,1)S(1)} %copy-done.12, bf16[256,768]{1,0:T(8,128)(2,1)S(1)} %bitcast.84, f32[2,72,768]{2,1,0:T(8,128)S(1)} %get-tuple-element.75.mats_ref, f32[16,128]{1,0:T(8,128)S(1)} %get-tuple-element.76.small_ref, ...), custom_call_target="tpu_custom_call" | custom-call | bytes 40000000 | tf_op jit(solution)/shard_map/sum_all/pallas_call | solution.py:790
  408.7 1.0 copy-done.4
  413.5 1.3 copy-done.3
  414.8 1.3 copy-done.5
  416.1 1.0 copy-done.7
  417.1 1.0 copy-done.8
  418.1 3.2 update.1
  (84 shorter events, 8.7 us)
Async XLA Ops:
  7.2 162.7 %all-gather.2.cloned.1.call-start = ((), (), s32[]{:S(2)}) async-start(), calls=%async_computation.1 | async-start | bytes 10444800 | tf_op jit(solution)/shard_map/all_gather | solution.py:1637
  8.6 1.0 copy-start.16
  8.6 1.1 copy-start.17
  8.6 1.3 copy-start.25
  9.5 382.7 %reduce-scatter.2.cloned.1.call-start = ((), (), s32[]{:S(2)}) async-start(), calls=%async_computation.2 | async-start | bytes 10444800 | tf_op jit(solution)/shard_map/reduce_scatter | solution.py:1703
  137.6 3.5 copy-start.24
  288.7 1.0 copy-start.11
  288.7 1.0 copy-start.13
  289.8 102.5 %copy-start.14 = (f32[8,128]{1,0:T(8,128)S(1)}, f32[8,128]{1,0:T(8,128)}, u32[]{:S(2)}) copy-start(f32[8,128]{1,0:T(8,128)} %get-tuple-element.77.loss_ref) | copy-start | bytes 12292
  289.8 121.3 %copy-start.23 = (f32[156]{0:T(256)S(1)}, f32[156]{0:T(256)}, u32[]{:S(2)}) copy-start(f32[156]{0:T(256)} %param.33) | copy-start | bytes 1876
  289.8 121.9 %copy-start.20 = (f32[80,6]{0,1:T(8,128)S(1)}, f32[80,6]{0,1:T(8,128)}, u32[]{:S(2)}) copy-start(f32[80,6]{0,1:T(8,128)} %param.30) | copy-start | bytes 5764
  289.8 122.5 %copy-start.18 = (f32[80,6]{0,1:T(8,128)S(1)}, f32[80,6]{0,1:T(8,128)}, u32[]{:S(2)}) copy-start(f32[80,6]{0,1:T(8,128)} %param.31) | copy-start | bytes 5764
  289.8 123.1 %copy-start.21 = (f32[156]{0:T(256)S(1)}, f32[156]{0:T(256)}, u32[]{:S(2)}) copy-start(f32[156]{0:T(256)} %param.34) | copy-start | bytes 1876
  289.8 123.7 %copy-start.2 = (f32[393,768]{1,0:T(8,128)S(1)}, f32[393,768]{1,0:T(8,128)}, u32[]{:S(2)}) copy-start(f32[393,768]{1,0:T(8,128)} %refs_1_.1) | copy-start | bytes 3621892
  392.3 21.2 %copy-start = (f32[393,768]{1,0:T(8,128)S(1)}, f32[393,768]{1,0:T(8,128)}, u32[]{:S(2)}) copy-start(f32[393,768]{1,0:T(8,128)} %refs_0_.1) | copy-start | bytes 3621892
  392.3 21.2 %copy-start.1 = (f32[2,768,72]{1,2,0:T(8,128)S(1)}, f32[2,768,72]{1,2,0:T(8,128)}, u32[]{:S(2)}) copy-start(f32[2,768,72]{1,2,0:T(8,128)} %param.26) | copy-start | bytes 1327108
  392.3 1.2 copy-start.6
  408.7 1.0 copy-start.4
  411.7 9.6 %copy-start.19 = (f32[156]{0:T(256)}, f32[156]{0:T(256)S(1)}, u32[]{:S(2)}) copy-start(f32[156]{0:T(256)S(1)} %get-tuple-element.91) | copy-start | bytes 1876
  412.3 9.0 %copy-start.15 = (f32[6,80]{1,0:T(8,128)}, f32[6,80]{1,0:T(8,128)S(1)}, u32[]{:S(2)}) copy-start(f32[6,80]{1,0:T(8,128)S(1)} %get-tuple-element.94) | copy-start | bytes 5764
  413.5 1.3 copy-start.3
  414.8 1.3 copy-start.5
  416.1 1.0 copy-start.7
  417.1 1.0 copy-start.8
  (4 other events, 3.7 us)
Sparse Core Ops, SparseCore 0:
  10.7 124.4 all-gather.1
  248.7 101.8 reduce-scatter.1

commit v8 on v6

--- a/solution.py
+++ b/solution.py
@@ -2,6 +2,8 @@
 
 import jax
 import jax.numpy as jnp
+import ml_dtypes
+import numpy as np
 from jax import lax
 from jax.experimental import pallas as pl
 from jax.experimental.pallas import tpu as pltpu
@@ -779,7 +781,7 @@
             pltpu.SemaphoreType.DMA((10,)),
         ],
         compiler_params=pltpu.CompilerParams(
-            collective_id=2, has_side_effects=True, vmem_limit_bytes=32 * 2**20
+            collective_id=2, has_side_effects=True, vmem_limit_bytes=24 * 2**20
         ),
         cost_estimate=pl.CostEstimate(flops=0, bytes_accessed=40 * 10**6, transcendentals=0),
         name="sum_all",
@@ -799,17 +801,21 @@
 
 
 def update(sums, table, mats):
-    vmem = pl.BlockSpec(memory_space=pltpu.VMEM)
     shapes = []
     for item in (table[0], mats[0]):
         shapes += [jax.ShapeDtypeStruct(item.shape, jnp.float32)] * 3
         shapes += [jax.ShapeDtypeStruct(item.shape, jnp.bfloat16)]
+    width = table[0].shape[1]
+    block = pl.BlockSpec((144, width), lambda i: (i, 0))
+    third = pl.BlockSpec((mats[0].shape[0] // 3, width), lambda i: (i, 0))
+    whole = pl.BlockSpec(sums.shape, lambda i: (0, 0))
     outs = pl.pallas_call(
         update_kernel,
+        grid=(3,),
         out_shape=tuple(shapes),
-        in_specs=[vmem] * 9,
-        out_specs=(vmem,) * 8,
-        compiler_params=pltpu.CompilerParams(vmem_limit_bytes=40 * 2**20),
+        in_specs=[whole] + [block] * 4 + [third] * 4,
+        out_specs=(block,) * 4 + (third,) * 4,
+        compiler_params=pltpu.CompilerParams(vmem_limit_bytes=32 * 2**20),
         name="update",
     )(sums, *table, *mats)
     return outs[:4], outs[4:]
@@ -1607,9 +1613,8 @@
     )
     pos_rows, pos_cols = pos_table.shape
     vec_own = vectors.shape[0]
-    table_low = embed_table.astype(low)
     pad_rows = -own_rows % 16
-    table_padded = jnp.pad(table_low, ((0, pad_rows), (0, 0)))
+    table_padded = jnp.pad(embed_table, ((0, pad_rows), (0, 0))).astype(low)
     slot_rows = own_rows + pad_rows
 
     table_slice = lax.all_gather(table_padded, "dp", axis=0, tiled=True)
@@ -1629,13 +1634,13 @@
         (owners % 8) * 32 + (owners // 8 % RING) * 8 + (owners // 32) * capacity + rank
     )
     slot_hot = (arrival[:, None] == slots[None, :]).astype(low)
-    spread = (slots[:, None] // capacity == jnp.arange(devices)[None, :]).astype(low)
-    earlier = (tokens[:, None] < tokens[None, :]).astype(low)
-    slot_number = jnp.broadcast_to((slots % capacity).astype(jnp.float32)[:, None], (slot_count, tok))
-    by_owner = (
-        (slots % 64 // 16) * 2 + slots // 64 * 8 + slots % 16 // 2 * 32 + slots % capacity
-    )
-    swap = (by_owner[:, None] == slots[None, :]).astype(low)
+    hot = lambda condition: condition.astype(ml_dtypes.bfloat16)
+    line, step = np.arange(slot_count), np.arange(tok)
+    spread = hot(line[:, None] // capacity == np.arange(devices)[None, :])
+    earlier = hot(step[:, None] < step[None, :])
+    slot_number = np.broadcast_to((line % capacity).astype(np.float32)[:, None], (slot_count, tok)).copy()
+    by_owner = line % 64 // 16 * 2 + line // 64 * 8 + line % 16 // 2 * 32 + line % capacity
+    swap = hot(by_owner[:, None] == line[None, :])
     values = jnp.concatenate([jnp.transpose(pos_table).reshape(-1), vectors]).astype(low)
     small = jnp.concatenate(
         [
@@ -1645,7 +1650,7 @@
         ]
     )
     mats_all, small_all, returned_rows, asked = gather_weights(
-        blocks, small, table_padded, spread, earlier, slot_number, jnp.transpose(swap)
+        blocks, small, table_padded, spread, earlier, slot_number, swap.T.copy()
     )
     small_all = small_all.reshape(devices, -1)
     pos_low_t = small_all[:, : pos_rows * pos_cols].reshape(width, pos_rows)

time: 437 us -> 430 us (0.984)
  no operation moved by 1% of the time
where the time goes in v8:
time: 430 us; the launch traced here: 429 us
  Pallas kernels  384 us (89%)
  local copies, waits for them, and re-layouts  17.3 us (4%)
  between operations  16.2 us (4%)
  other arithmetic  10.4 us (2%)
    pallas_call x1, Pallas kernels, gather_weights(): pl.pallas_call(gather_kernel, out_shape=(jax.ShapeDtypeStruct((layers, RI...  127 us
    pallas_call x1, Pallas kernels, reduce_weights(): pl.pallas_call(reduce_kernel, out_shape=(jax.ShapeDtypeStruct((2, rows //...  98.7 us
    pallas_call x1, Pallas kernels, head(): pl.pallas_call(head_kernel, out_shape=(jax.ShapeDtypeStruct((tok, width),...  78 us
    pallas_call x1, Pallas kernels, backward_layers(): pl.pallas_call(backward_kernel, grid=(2 * STEPS + 2,), out_shape=(shape((...  37 us
    pallas_call x1, Pallas kernels, forward_layers(): pl.pallas_call(forward_kernel, grid=(2 * STEPS,), out_shape=(shape((2, to...  26 us
    pallas_call x1, Pallas kernels, sum_all(): pl.pallas_call(sum_kernel, out_shape=(jax.ShapeDtypeStruct(value, jnp.flo...  13.7 us
    unnamed x55, local copies, waits for them, and re-layouts  12.9 us
  transfers between devices with their start and end apart: 2, of which 0 were waited for; matrix products, arithmetic and copies ran while one was open for 3% of the time, Pallas kernels for 67%

profile of v8, /device:TPU:0, one launch (start us, length us, event | category | flops | bytes accessed | tf_op | source)
XLA Modules:
  0.0 429.3 jit_solution(11297928192599883105)
XLA Ops:
  7.2 1.4 convert.24
  8.6 0.9 pad.14.table_ref
  10.6 126.9 %gather_weights.1 = (bf16[2,4,4,4,144,768]{5,4,3,2,1,0:T(8,128)(2,1)}, bf16[4,4,4,2,16,128]{5,4,3,2,1,0:T(8,128)(2,1)}, bf16[4,2,32,768]{3,2,1,0:T(8,128)(2,1)}, bf16[256,400]{1,0:T(8,128)(2,1)}) custom-call(f32[2,72,768]{2,1,0:T(8,128)} %bitcast.78, bf16[16,128]{1,0:T(8,128)(2,1)} %maximum_maximum_fusion.small_ref, bf16[400,768]{1,0:T(8,128)(2,1)} %pad.14.table_ref, ...), custom_call_target="tpu_custom_call" | custom-call | bytes 250000000 | tf_op jit(solution)/shard_map/gather_weights/pallas_call | solution.py:295
  137.6 1.2 copy.58
  138.8 1.0 reshape.137.pos_ref
  143.9 26.0 %forward_layers.1 = (f32[2,128,768]{2,1,0:T(8,128)}, bf16[2,128,768]{2,1,0:T(8,128)(2,1)}, bf16[2,3,128,768]{3,2,1,0:T(8,128)(2,1)}, f32[2,12,128,128]{3,2,1,0:T...) custom-call(bf16[128,256]{1,0:T(8,128)(2,1)} %fusion.1.hot_ref, ...), custom_call_target="tpu_custom_call" | custom-call | flops 3623878656 | bytes 28311552 | tf_op jit(solution)/shard_map/forward_layers/pallas_call | solution.py:1245
  170.5 78.0 %head.1 = (f32[128,768]{1,0:T(8,128)}, bf16[6400,768]{1,0:T(8,128)(2,1)}, f32[8,128]{1,0:T(8,128)}) custom-call(bf16[128,768]{1,0:T(8,128)(2,1)} %get-tuple-element.56.f_ref, s32[8,128]{1,0:T(8,128)} %broadcast_in_dim.25.code_ref, f32[8,128]{1,0:T(8,128)} %divide_multiply_fusion.weight_ref, bf16[6400,768]{1,0:T(8,128)(2,1)} %all-gather.2.cloned.1.call-done.table_ref), custom_call_target="tpu_custom_call" | custom-call | flops 30198988800 | bytes 19660800 | tf_op jit(solution)/shard_map/head/pallas_call | solution.py:1062
  248.6 37.0 %backward_layers.1 = (f32[128,768]{1,0:T(8,128)}, f32[26,1,768]{2,1,0:T(1,128)}, bf16[4,2,32,768]{3,2,1,0:T(8,128)(2,1)}, bf16[2,192,48,384]{3,2,1,0:T(8,128)(2,1)}) custom-call(f32[128,768]{1,0:T(8,128)} %get-tuple-element.59.grad_ref, f32[128,768]{1,0:T(8,128)} %get-tuple-element.60.hidden_ref, f32[26,1,768]{2,1,0:T(1,128)} %reshape.153.vec_ref, ...), custom_call_target="tpu_custom_call" | custom-call | flops 7247757312 | bytes 28311552 | tf_op jit(solution)/shard_map/backward_layers/pallas_call | solution.py:1509
  285.6 1.1 reduce
  286.9 1.5 fusion.2
  288.7 1.2 copy.53
  289.9 98.7 %reduce_weights.1 = (f32[2,72,768]{2,1,0:T(8,128)}, f32[16,128]{1,0:T(8,128)}, bf16[4,4,16,768]{3,2,1,0:T(8,128)(2,1)}) custom-call(bf16[2,4,4,4,3,48,384]{6,5,4,3,2,1,0:T(8,128)(2,1)} %bitcast.88, f32[4,4,4,2,16,128]{5,4,3,2,1,0:T(8,128)} %bitcast.89, bf16[4,2,32,768]{3,2,1,0:T(8,128)(2,1)} %get-tuple-element.73.rows_ref, ...), custom_call_target="tpu_custom_call" | custom-call | bytes 280000000 | tf_op jit(solution)/shard_map/reduce_weights/pallas_call | solution.py:675
  388.8 1.1 copy-done.2
  389.9 1.1 copy-done.8
  391.0 1.0 copy-done.11
  391.9 0.9 copy-done.12
  393.6 13.7 %sum_all.1 = (f32[8,128]{1,0:T(8,128)S(1)}, f32[400,768]{1,0:T(8,128)S(1)}) custom-call(bf16[400,768]{1,0:T(8,128)(2,1)S(1)} %copy-done.8, bf16[256,400]{1,0:T(8,128)(2,1)S(1)} %copy-done.12, bf16[256,768]{1,0:T(8,128)(2,1)S(1)} %bitcast.83, f32[2,72,768]{2,1,0:T(8,128)S(1)} %copy-done.2, f32[16,128]{1,0:T(8,128)S(1)} %copy-done.13, f32[8,128]{1,0:T(8,128)S(1)} %copy-done.14), custom_call_target="tpu_custom_call" | custom-call | bytes 40000000 | tf_op jit(solution)/shard_map/sum_all/pallas_call | solution.py:770
  407.3 1.0 copy-done.6
  410.3 1.3 fusion.27
  413.4 1.0 copy-done.3
  414.4 1.3 copy-done.5
  415.7 1.3 copy-done.7
  417.0 1.0 copy-done.10
  418.0 3.3 update.1
  (84 shorter events, 10.1 us)
Async XLA Ops:
  7.2 162.7 %all-gather.2.cloned.1.call-start = ((), (), s32[]{:S(2)}) async-start(), calls=%async_computation.1 | async-start | bytes 10444800 | tf_op jit(solution)/shard_map/all_gather | solution.py:1620
  8.6 1.0 copy-start.16
  8.6 1.1 copy-start.17
  8.6 1.3 copy-start.25
  9.5 379.2 %reduce-scatter.2.cloned.1.call-start = ((), (), s32[]{:S(2)}) async-start(), calls=%async_computation.2 | async-start | bytes 10444800 | tf_op jit(solution)/shard_map/reduce_scatter | solution.py:1686
  137.6 3.5 copy-start.24
  289.9 98.8 %copy-start.14 = (f32[8,128]{1,0:T(8,128)S(1)}, f32[8,128]{1,0:T(8,128)}, u32[]{:S(2)}) copy-start(f32[8,128]{1,0:T(8,128)} %get-tuple-element.77.loss_ref) | copy-start | bytes 12292
  289.9 120.4 %copy-start.23 = (f32[156]{0:T(256)S(1)}, f32[156]{0:T(256)}, u32[]{:S(2)}) copy-start(f32[156]{0:T(256)} %param.33) | copy-start | bytes 1876
  289.9 121.7 %copy-start.20 = (f32[80,6]{0,1:T(8,128)S(1)}, f32[80,6]{0,1:T(8,128)}, u32[]{:S(2)}) copy-start(f32[80,6]{0,1:T(8,128)} %param.30) | copy-start | bytes 5764
  289.9 122.4 %copy-start.18 = (f32[80,6]{0,1:T(8,128)S(1)}, f32[80,6]{0,1:T(8,128)}, u32[]{:S(2)}) copy-start(f32[80,6]{0,1:T(8,128)} %param.31) | copy-start | bytes 5764
  289.9 122.9 %copy-start.21 = (f32[156]{0:T(256)S(1)}, f32[156]{0:T(256)}, u32[]{:S(2)}) copy-start(f32[156]{0:T(256)} %param.34) | copy-start | bytes 1876
  289.9 123.5 %copy-start.4 = (f32[393,768]{1,0:T(8,128)S(1)}, f32[393,768]{1,0:T(8,128)}, u32[]{:S(2)}) copy-start(f32[393,768]{1,0:T(8,128)} %refs_1_.1) | copy-start | bytes 3621892
  289.9 123.5 %copy-start.9 = (f32[2,768,72]{1,2,0:T(8,128)S(1)}, f32[2,768,72]{1,2,0:T(8,128)}, u32[]{:S(2)}) copy-start(f32[2,768,72]{1,2,0:T(8,128)} %param.27) | copy-start | bytes 1327108
  388.7 24.7 %copy-start = (f32[393,768]{1,0:T(8,128)S(1)}, f32[393,768]{1,0:T(8,128)}, u32[]{:S(2)}) copy-start(f32[393,768]{1,0:T(8,128)} %refs_0_.1) | copy-start | bytes 3621892
  388.7 24.7 %copy-start.1 = (f32[2,768,72]{1,2,0:T(8,128)S(1)}, f32[2,768,72]{1,2,0:T(8,128)}, u32[]{:S(2)}) copy-start(f32[2,768,72]{1,2,0:T(8,128)} %param.26) | copy-start | bytes 1327108
  388.7 1.1 copy-start.2
  389.9 1.1 copy-start.8
  407.3 1.0 copy-start.6
  411.6 9.6 %copy-start.19 = (f32[156]{0:T(256)}, f32[156]{0:T(256)S(1)}, u32[]{:S(2)}) copy-start(f32[156]{0:T(256)S(1)} %get-tuple-element.91) | copy-start | bytes 1876
  412.2 9.0 %copy-start.15 = (f32[6,80]{1,0:T(8,128)}, f32[6,80]{1,0:T(8,128)S(1)}, u32[]{:S(2)}) copy-start(f32[6,80]{1,0:T(8,128)S(1)} %get-tuple-element.94) | copy-start | bytes 5764
  413.4 1.0 copy-start.3
  414.4 1.3 copy-start.5
  415.7 1.3 copy-start.7
  417.0 1.0 copy-start.10
  (4 other events, 3.6 us)
Sparse Core Ops, SparseCore 0:
  10.7 124.4 all-gather.1
  248.7 102.8 reduce-scatter.1
